TPU v7x, 256 devices: a whole 4x4x8 slice. The times are simulated.
256 devices in a mesh: cuts: 2 (over y_hi), blk: 128 (over z, y_lo, x, core).
Axes of the slice: x: 4, y: 4 (y_hi: 2, y_lo: 2; y = y_hi * 2 + y_lo), z: 8, core: 2. Of those that a mesh axis runs over, the one named last changes fastest.
Arguments:
- image_embed: float32 [32768, 1152], P(('cuts', 'blk')), may hold values from -0.1875 to 0.1875
- text_embed: float32 [32768, 1152], P(('cuts', 'blk')), may hold values from -0.1875 to 0.1875
- log_scale: float32 [1], replicated, may hold values from 0.5 to 2.3
- bias: float32 [1], replicated, may hold values from -4 to -1
Outputs:
- image_grad: float32 [32768, 1152], P(('cuts', 'blk'))
- text_grad: float32 [32768, 1152], P(('cuts', 'blk'))
All inputs are finite; a program needn't handle non-finite values.
Results may differ from a plain program's by a relative error of at most 0.0003.
Values sent between devices are 32-bit elements; how exact they have to be, the bound alone decides.
No kernel may reach another device: no remote copies, remote signals or barrier semaphores. Data moves between devices by JAX's collectives and lax.ppermute only.
A program may use at most 128 MiB of HBM per device.

v0:
```python
import jax
import jax.numpy as jnp
from jax import lax
from jax.sharding import PartitionSpec as P

STEPS = 8


def shifted(block, axis, distance):
    devices = range(lax.axis_size(axis))
    route = [((i - distance) % len(devices), i) for i in devices]
    return lax.ppermute(block, axis, route)


def normalize(rows_in):
    inverse = lax.rsqrt(jnp.sum(rows_in * rows_in, axis=-1, keepdims=True) + 1e-06)
    return (rows_in * inverse, inverse)


def pair_grad(logits, positive):
    signs = jnp.where(positive, jnp.float32(1.0), jnp.float32(-1.0))
    return -signs * jax.nn.sigmoid(-signs * logits)


def local(image_embed, text_embed, log_scale, bias):
    hp = lax.Precision.HIGHEST
    x_rows, x_inv = normalize(image_embed)
    y_rows, y_inv = normalize(text_embed)
    scale = jnp.exp(log_scale[0])
    shift_bias = bias[0]
    local_rows = x_rows.shape[0]
    group = lax.axis_index("cuts")
    visiting = lax.all_gather(y_rows, "cuts", axis=0, tiled=True)
    row_ids = lax.broadcasted_iota(jnp.int32, (local_rows, visiting.shape[0]), 0)
    col_ids = lax.broadcasted_iota(jnp.int32, (local_rows, visiting.shape[0]), 1)
    own_pairs = col_ids == group * local_rows + row_ids
    no_pairs = jnp.zeros_like(own_pairs)
    image_part = jnp.zeros_like(x_rows)
    text_sums = jnp.zeros_like(visiting)
    for step in range(STEPS):
        if step > 0:
            visiting = shifted(visiting, "blk", 1)
        logits = scale * jnp.dot(x_rows, visiting.T, precision=hp) + shift_bias
        grads = pair_grad(logits, own_pairs if step == 0 else no_pairs)
        to_image = jnp.dot(grads, visiting, precision=hp)
        to_text = scale * jnp.dot(grads.T, x_rows, precision=hp)
        to_image, to_text = (to_image, to_text)
        image_part = image_part + to_image
        if step > 0:
            to_text = shifted(to_text, "blk", -step)
        text_sums = text_sums + to_text
    text_part = lax.psum_scatter(text_sums, "cuts", scatter_dimension=0, tiled=True)
    image_part = scale * image_part
    image_grad = x_inv * (
        image_part - x_rows * jnp.sum(x_rows * image_part, axis=-1, keepdims=True)
    )
    text_grad = y_inv * (text_part - y_rows * jnp.sum(y_rows * text_part, axis=-1, keepdims=True))
    return (image_grad, text_grad)


def solution(mesh):
    return jax.shard_map(
        local,
        mesh=mesh,
        in_specs=(P(("cuts", "blk"), None), P(("cuts", "blk"), None), P(), P()),
        out_specs=(P(("cuts", "blk"), None), P(("cuts", "blk"), None)),
        check_vma=False,
    )
```

profile of v0, /device:TPU:1, one launch (start us, length us, event | category | flops | bytes accessed | tf_op | source)
XLA Modules:
  0.0 384.7 jit_solution(7082408015735950572)
XLA Ops:
  7.2 0.0 all-gather.2.cloned.1.call-start
  7.2 1.2 multiply_reduce_fusion.2
  8.5 2.0 broadcast_multiply_fusion
  10.5 0.0 all-gather.2.cloned.1.call-update
  10.5 0.0 reduce-scatter.2.cloned.1.call-start
  10.5 33.3 %all-gather.2.cloned.1.call-done = f32[256,1152]{1,0:T(8,128)} async-done(((f32[128,1152]{1,0:T(8,128)}), f32[256,1152]{1,0:T(8,128)}) %all-gather.2.cloned.1.call-update) | async-done | bytes 1179664 | tf_op jit(solution)/shard_map/all_gather | solution.py:33
  43.8 1.7 collective-permute-start
  45.6 13.5 %collective-permute-done = f32[256,1152]{1,0:T(8,128)S(1)} collective-permute-done((f32[256,1152]{1,0:T(8,128)}, f32[256,1152]{1,0:T(8,128)S(1)}, u32[]{:S(2)}, u32[]{:S(2)}) %collective-permute-start) | collective-permute-done | bytes 1179680 | tf_op jit(solution)/shard_map/ppermute | solution.py:12
  59.0 2.4 collective-permute-start.1
  61.4 13.1 %collective-permute-done.1 = f32[256,1152]{1,0:T(8,128)S(1)} collective-permute-done((f32[256,1152]{1,0:T(8,128)S(1)}, f32[256,1152]{1,0:T(8,128)S(1)}, u32[]{:S(2)}, u32[]{:S(2)}) %collective-permute-start.1) | collective-permute-done | bytes 1179680 | tf_op jit(solution)/shard_map/ppermute | solution.py:12
  74.6 2.5 collective-permute-start.2
  77.1 13.1 %collective-permute-done.2 = f32[256,1152]{1,0:T(8,128)S(1)} collective-permute-done((f32[256,1152]{1,0:T(8,128)S(1)}, f32[256,1152]{1,0:T(8,128)S(1)}, u32[]{:S(2)}, u32[]{:S(2)}) %collective-permute-start.2) | collective-permute-done | bytes 1179680 | tf_op jit(solution)/shard_map/ppermute | solution.py:12
  90.2 2.5 collective-permute-start.3
  92.7 13.9 %collective-permute-done.3 = f32[256,1152]{1,0:T(8,128)S(1)} collective-permute-done((f32[256,1152]{1,0:T(8,128)S(1)}, f32[256,1152]{1,0:T(8,128)S(1)}, u32[]{:S(2)}, u32[]{:S(2)}) %collective-permute-start.3) | collective-permute-done | bytes 1179680 | tf_op jit(solution)/shard_map/ppermute | solution.py:12
  106.6 1.7 collective-permute-start.4
  109.7 0.1 multiply_reduce_fusion.3
  109.8 1.3 fusion.42
  111.1 0.6 copy-done.18
  111.7 1.2 convolution_multiply_fusion.6
  112.9 15.9 %collective-permute-start.7 = (f32[256,1152]{1,0:T(8,128)S(1)}, f32[256,1152]{1,0:T(8,128)S(1)}, u32[]{:S(2)}, u32[]{:S(2)}) collective-permute-start(f32[256,1152]{1,0:T(8,128)S(1)} %convolution_multiply_fusion.6), channel_id=1, source_target_pairs={{1,0},{2,1},{3,2},{4,3},{5,4},{6,5},{7,6},{8,7},{9,8},{10,9},{11,1... | collective-permute-start | bytes 3538952 | tf_op jit(solution)/shard_map/ppermute | solution.py:12
  128.8 1.3 fusion.37
  130.1 0.6 copy-done.19
  130.7 1.2 convolution_multiply_fusion.5
  131.9 21.0 %collective-permute-start.8 = (f32[256,1152]{1,0:T(8,128)S(1)}, f32[256,1152]{1,0:T(8,128)S(1)}, u32[]{:S(2)}, u32[]{:S(2)}) collective-permute-start(f32[256,1152]{1,0:T(8,128)S(1)} %convolution_multiply_fusion.5), channel_id=1, source_target_pairs={{2,0},{3,1},{4,2},{5,3},{6,4},{7,5},{8,6},{9,7},{10,8},{11,9},{12,... | collective-permute-start | bytes 3538952 | tf_op jit(solution)/shard_map/ppermute | solution.py:12
  152.9 1.3 fusion.32
  154.2 2.2 convolution_multiply_fusion.4
  156.4 1.3 fusion.27
  157.7 1.0 collective-permute-start.6
  158.6 2.3 convolution_multiply_fusion.3
  160.9 1.3 fusion.22
  162.2 2.2 convolution_multiply_fusion.2
  164.4 1.3 fusion.17
  165.7 2.2 convolution_multiply_fusion.1
  167.9 6.3 %collective-permute-done.6 = f32[256,1152]{1,0:T(8,128)S(1)} collective-permute-done((f32[256,1152]{1,0:T(8,128)S(1)}, f32[256,1152]{1,0:T(8,128)S(1)}, u32[]{:S(2)}, u32[]{:S(2)}) %collective-permute-start.6) | collective-permute-done | bytes 1179680 | tf_op jit(solution)/shard_map/ppermute | solution.py:12
  174.2 37.5 %collective-permute-start.11 = (f32[256,1152]{1,0:T(8,128)}, f32[256,1152]{1,0:T(8,128)}, u32[]{:S(2)}, u32[]{:S(2)}) collective-permute-start(f32[256,1152]{1,0:T(8,128)} %convolution_multiply_fusion.2), channel_id=1, source_target_pairs={{5,0},{6,1},{7,2},{8,3},{9,4},{10,5},{11,6},{12,7},{13,8},{14,9},{... | collective-permute-start | bytes 3538952 | tf_op jit(solution)/shard_map/ppermute | solution.py:12
  211.8 1.3 fusion.12
  213.0 2.2 convolution_multiply_fusion
  215.3 0.1 collective-permute-start.12
  215.4 0.9 copy-done.14
  216.3 1.0 copy-done.16
  217.3 2.7 fusion.49
  220.1 0.8 fusion.50
  220.9 20.4 %collective-permute-done.10 = f32[256,1152]{1,0:T(8,128)} collective-permute-done((f32[256,1152]{1,0:T(8,128)}, f32[256,1152]{1,0:T(8,128)}, u32[]{:S(2)}, u32[]{:S(2)}) %collective-permute-start.10) | collective-permute-done | bytes 1179680 | tf_op jit(solution)/shard_map/ppermute | solution.py:12
  241.3 25.3 %collective-permute-done.11 = f32[256,1152]{1,0:T(8,128)} collective-permute-done((f32[256,1152]{1,0:T(8,128)}, f32[256,1152]{1,0:T(8,128)}, u32[]{:S(2)}, u32[]{:S(2)}) %collective-permute-start.11) | collective-permute-done | bytes 1179680 | tf_op jit(solution)/shard_map/ppermute | solution.py:12
  266.6 25.3 %collective-permute-done.12 = f32[256,1152]{1,0:T(8,128)} collective-permute-done((f32[256,1152]{1,0:T(8,128)}, f32[256,1152]{1,0:T(8,128)}, u32[]{:S(2)}, u32[]{:S(2)}) %collective-permute-start.12) | collective-permute-done | bytes 1179680 | tf_op jit(solution)/shard_map/ppermute | solution.py:12
  291.8 21.1 %collective-permute-done.13 = f32[256,1152]{1,0:T(8,128)} collective-permute-done((f32[256,1152]{1,0:T(8,128)}, f32[256,1152]{1,0:T(8,128)}, u32[]{:S(2)}, u32[]{:S(2)}) %collective-permute-start.13) | collective-permute-done | bytes 1179680 | tf_op jit(solution)/shard_map/ppermute | solution.py:12
  312.9 5.4 %fusion.6 = f32[256,1152]{1,0:T(8,128)} fusion(f32[256,1152]{1,0:T(8,128)} %collective-permute-done.13, f32[256,1152]{1,0:T(8,128)} %collective-permute-done.12, f32[256,1152]{1,0:T(8,128)} %collective-permute-done.11, f32[256,1152]{1,0:T(8,128)} %collective-permute-done.10, f32[256,1152]{1,0:T(8,128)} %collective-permute-done.9, ...), kind=kOutput, calls=%fused_computation.14 | convolution fusion | flops 455491584 | bytes 10158596 | tf_op jit(solution)/shard_map/dot_general | solution.py:46
  318.3 0.0 reduce-scatter.2.cloned.1.call-update
  318.3 1.7 convolution_add_fusion.6
  320.1 0.8 convolution_add_fusion.5
  320.9 0.4 copy-done.3
  321.3 0.8 convolution_add_fusion.4
  322.1 0.5 copy-done.5
  322.6 0.8 convolution_add_fusion.3
  323.4 0.5 copy-done.7
  323.9 0.8 convolution_add_fusion.2
  324.7 0.5 copy-done.10
  325.2 0.8 convolution_add_fusion.1
  326.0 0.5 copy-done.12
  326.4 0.9 multiply_reduce_fusion.1
  327.4 1.0 subtract_multiply_fusion.1
  328.4 47.1 %reduce-scatter.2.cloned.1.call-done = f32[128,1152]{1,0:T(8,128)} async-done(((f32[256,1152]{1,0:T(8,128)}), f32[128,1152]{1,0:T(8,128)}) %reduce-scatter.2.cloned.1.call-update) | async-done | bytes 589840 | tf_op jit(solution)/shard_map/reduce_scatter | solution.py:52
  375.5 1.3 multiply_reduce_fusion
  376.9 1.0 subtract_multiply_fusion
  (65 shorter events, 0.2 us)
Async XLA Ops:
  7.2 102.5 %copy-start = (f32[128,1152]{1,0:T(8,128)S(1)}, f32[128,1152]{1,0:T(8,128)}, u32[]{:S(2)}) copy-start(f32[128,1152]{1,0:T(8,128)} %param.4) | copy-start | bytes 1769476
  7.2 36.7 %all-gather.2.cloned.1.call-start = ((), (), s32[]{:S(2)}) async-start(), calls=%async_computation.1 | async-start | bytes 1769472 | tf_op jit(solution)/shard_map/all_gather | solution.py:33
  10.5 365.0 %reduce-scatter.2.cloned.1.call-start = ((), (), s32[]{:S(2)}) async-start(), calls=%async_computation.2 | async-start | bytes 1769472 | tf_op jit(solution)/shard_map/reduce_scatter | solution.py:52
  43.8 15.2 %collective-permute-start = (f32[256,1152]{1,0:T(8,128)}, f32[256,1152]{1,0:T(8,128)S(1)}, u32[]{:S(2)}, u32[]{:S(2)}) collective-permute-start(f32[256,1152]{1,0:T(8,128)} %all-gather.2.cloned.1.call-done), channel_id=1, source_target_pairs={{127,0},{0,1},{1,2},{2,3},{3,4},{4,5},{5,6},{6,7},{7,8},{8,9},{9,1... | collective-permute-start | bytes 3538952 | tf_op jit(solution)/shard_map/ppermute | solution.py:12
  59.0 15.5 %collective-permute-start.1 = (f32[256,1152]{1,0:T(8,128)S(1)}, f32[256,1152]{1,0:T(8,128)S(1)}, u32[]{:S(2)}, u32[]{:S(2)}) collective-permute-start(f32[256,1152]{1,0:T(8,128)S(1)} %collective-permute-done), channel_id=1, source_target_pairs={{127,0},{0,1},{1,2},{2,3},{3,4},{4,5},{5,6},{6,7},{7,8},{8,9},{9,1... | collective-permute-start | bytes 3538952 | tf_op jit(solution)/shard_map/ppermute | solution.py:12
  74.6 15.6 %collective-permute-start.2 = (f32[256,1152]{1,0:T(8,128)S(1)}, f32[256,1152]{1,0:T(8,128)S(1)}, u32[]{:S(2)}, u32[]{:S(2)}) collective-permute-start(f32[256,1152]{1,0:T(8,128)S(1)} %collective-permute-done.1), channel_id=1, source_target_pairs={{127,0},{0,1},{1,2},{2,3},{3,4},{4,5},{5,6},{6,7},{7,8},{8,9},{9,1... | collective-permute-start | bytes 3538952 | tf_op jit(solution)/shard_map/ppermute | solution.py:12
  90.2 62.7 %copy-start.2 = (f32[256,1152]{1,0:T(8,128)}, f32[256,1152]{1,0:T(8,128)S(1)}, u32[]{:S(2)}) copy-start(f32[256,1152]{1,0:T(8,128)S(1)} %collective-permute-done.2) | copy-start | bytes 3538948
  90.2 16.4 %collective-permute-start.3 = (f32[256,1152]{1,0:T(8,128)S(1)}, f32[256,1152]{1,0:T(8,128)S(1)}, u32[]{:S(2)}, u32[]{:S(2)}) collective-permute-start(f32[256,1152]{1,0:T(8,128)S(1)} %collective-permute-done.2), channel_id=1, source_target_pairs={{127,0},{0,1},{1,2},{2,3},{3,4},{4,5},{5,6},{6,7},{7,8},{8,9},{9,1... | collective-permute-start | bytes 3538952 | tf_op jit(solution)/shard_map/ppermute | solution.py:12
  106.6 49.8 %copy-start.4 = (f32[256,1152]{1,0:T(8,128)}, f32[256,1152]{1,0:T(8,128)S(1)}, u32[]{:S(2)}) copy-start(f32[256,1152]{1,0:T(8,128)S(1)} %collective-permute-done.3) | copy-start | bytes 3538948
  106.6 22.2 %collective-permute-start.4 = (f32[256,1152]{1,0:T(8,128)S(1)}, f32[256,1152]{1,0:T(8,128)S(1)}, u32[]{:S(2)}, u32[]{:S(2)}) collective-permute-start(f32[256,1152]{1,0:T(8,128)S(1)} %collective-permute-done.3), channel_id=1, source_target_pairs={{127,0},{0,1},{1,2},{2,3},{3,4},{4,5},{5,6},{6,7},{7,8},{8,9},{9,1... | collective-permute-start | bytes 3538952 | tf_op jit(solution)/shard_map/ppermute | solution.py:12
  111.1 0.7 copy-start.18
  112.9 102.4 %collective-permute-start.7 = (f32[256,1152]{1,0:T(8,128)S(1)}, f32[256,1152]{1,0:T(8,128)S(1)}, u32[]{:S(2)}, u32[]{:S(2)}) collective-permute-start(f32[256,1152]{1,0:T(8,128)S(1)} %convolution_multiply_fusion.6), channel_id=1, source_target_pairs={{1,0},{2,1},{3,2},{4,3},{5,4},{6,5},{7,6},{8,7},{9,8},{10,9},{11,1... | collective-permute-start | bytes 3538952 | tf_op jit(solution)/shard_map/ppermute | solution.py:12
  128.8 32.1 %copy-start.6 = (f32[256,1152]{1,0:T(8,128)}, f32[256,1152]{1,0:T(8,128)S(1)}, u32[]{:S(2)}) copy-start(f32[256,1152]{1,0:T(8,128)S(1)} %collective-permute-done.4) | copy-start | bytes 3538948
  128.8 28.9 %collective-permute-start.5 = (f32[256,1152]{1,0:T(8,128)S(1)}, f32[256,1152]{1,0:T(8,128)S(1)}, u32[]{:S(2)}, u32[]{:S(2)}) collective-permute-start(f32[256,1152]{1,0:T(8,128)S(1)} %collective-permute-done.4), channel_id=1, source_target_pairs={{127,0},{0,1},{1,2},{2,3},{3,4},{4,5},{5,6},{6,7},{7,8},{8,9},{9,1... | collective-permute-start | bytes 3538952 | tf_op jit(solution)/shard_map/ppermute | solution.py:12
  130.1 0.7 copy-start.19
  131.9 83.5 %collective-permute-start.8 = (f32[256,1152]{1,0:T(8,128)S(1)}, f32[256,1152]{1,0:T(8,128)S(1)}, u32[]{:S(2)}, u32[]{:S(2)}) collective-permute-start(f32[256,1152]{1,0:T(8,128)S(1)} %convolution_multiply_fusion.5), channel_id=1, source_target_pairs={{2,0},{3,1},{4,2},{5,3},{6,4},{7,5},{8,6},{9,7},{10,8},{11,9},{12,... | collective-permute-start | bytes 3538952 | tf_op jit(solution)/shard_map/ppermute | solution.py:12
  154.2 3.5 copy-start.21
  156.4 64.5 %collective-permute-start.9 = (f32[256,1152]{1,0:T(8,128)}, f32[256,1152]{1,0:T(8,128)}, u32[]{:S(2)}, u32[]{:S(2)}) collective-permute-start(f32[256,1152]{1,0:T(8,128)} %convolution_multiply_fusion.4), channel_id=1, source_target_pairs={{3,0},{4,1},{5,2},{6,3},{7,4},{8,5},{9,6},{10,7},{11,8},{12,9},{13... | collective-permute-start | bytes 3538952 | tf_op jit(solution)/shard_map/ppermute | solution.py:12
  157.6 4.5 %copy-start.23 = (f32[128,256]{1,0:T(8,128)}, f32[128,256]{1,0:T(8,128)S(1)}, u32[]{:S(2)}) copy-start(f32[128,256]{1,0:T(8,128)S(1)} %fusion.27) | copy-start | bytes 393220
  157.7 6.7 %copy-start.9 = (f32[256,1152]{1,0:T(8,128)}, f32[256,1152]{1,0:T(8,128)S(1)}, u32[]{:S(2)}) copy-start(f32[256,1152]{1,0:T(8,128)S(1)} %collective-permute-done.5) | copy-start | bytes 3538948
  157.7 16.5 %collective-permute-start.6 = (f32[256,1152]{1,0:T(8,128)S(1)}, f32[256,1152]{1,0:T(8,128)S(1)}, u32[]{:S(2)}, u32[]{:S(2)}) collective-permute-start(f32[256,1152]{1,0:T(8,128)S(1)} %collective-permute-done.5), channel_id=1, source_target_pairs={{127,0},{0,1},{1,2},{2,3},{3,4},{4,5},{5,6},{6,7},{7,8},{8,9},{9,1... | collective-permute-start | bytes 3538952 | tf_op jit(solution)/shard_map/ppermute | solution.py:12
  160.9 80.4 %collective-permute-start.10 = (f32[256,1152]{1,0:T(8,128)}, f32[256,1152]{1,0:T(8,128)}, u32[]{:S(2)}, u32[]{:S(2)}) collective-permute-start(f32[256,1152]{1,0:T(8,128)} %convolution_multiply_fusion.3), channel_id=1, source_target_pairs={{4,0},{5,1},{6,2},{7,3},{8,4},{9,5},{10,6},{11,7},{12,8},{13,9},{1... | collective-permute-start | bytes 3538952 | tf_op jit(solution)/shard_map/ppermute | solution.py:12
  162.2 3.5 copy-start.27
  165.7 47.4 %copy-start.25 = (f32[128,256]{1,0:T(8,128)}, f32[128,256]{1,0:T(8,128)S(1)}, u32[]{:S(2)}) copy-start(f32[128,256]{1,0:T(8,128)S(1)} %fusion.17) | copy-start | bytes 393220
  174.2 41.1 %copy-start.11 = (f32[256,1152]{1,0:T(8,128)}, f32[256,1152]{1,0:T(8,128)S(1)}, u32[]{:S(2)}) copy-start(f32[256,1152]{1,0:T(8,128)S(1)} %collective-permute-done.6) | copy-start | bytes 3538948
  174.2 92.3 %collective-permute-start.11 = (f32[256,1152]{1,0:T(8,128)}, f32[256,1152]{1,0:T(8,128)}, u32[]{:S(2)}, u32[]{:S(2)}) collective-permute-start(f32[256,1152]{1,0:T(8,128)} %convolution_multiply_fusion.2), channel_id=1, source_target_pairs={{5,0},{6,1},{7,2},{8,3},{9,4},{10,5},{11,6},{12,7},{13,8},{14,9},{... | collective-permute-start | bytes 3538952 | tf_op jit(solution)/shard_map/ppermute | solution.py:12
  213.0 3.3 copy-start.29
  215.3 1.0 copy-start.14
  215.3 76.5 %collective-permute-start.12 = (f32[256,1152]{1,0:T(8,128)}, f32[256,1152]{1,0:T(8,128)}, u32[]{:S(2)}, u32[]{:S(2)}) collective-permute-start(f32[256,1152]{1,0:T(8,128)} %convolution_multiply_fusion.1), channel_id=1, source_target_pairs={{6,0},{7,1},{8,2},{9,3},{10,4},{11,5},{12,6},{13,7},{14,8},{15,9},... | collective-permute-start | bytes 3538952 | tf_op jit(solution)/shard_map/ppermute | solution.py:12
  216.3 1.0 copy-start.16
  216.3 96.6 %collective-permute-start.13 = (f32[256,1152]{1,0:T(8,128)}, f32[256,1152]{1,0:T(8,128)}, u32[]{:S(2)}, u32[]{:S(2)}) collective-permute-start(f32[256,1152]{1,0:T(8,128)} %convolution_multiply_fusion), channel_id=1, source_target_pairs={{7,0},{8,1},{9,2},{10,3},{11,4},{12,5},{13,6},{14,7},{15,8},{16,9}... | collective-permute-start | bytes 3538952 | tf_op jit(solution)/shard_map/ppermute | solution.py:12
  217.3 2.7 copy-start.8
  217.3 95.6 %copy-start.17 = (f32[256,1152]{1,0:T(8,128)S(1)}, f32[256,1152]{1,0:T(8,128)}, u32[]{:S(2)}) copy-start(f32[256,1152]{1,0:T(8,128)} %copy-done.16) | copy-start | bytes 3538948
  220.0 92.9 %copy-start.15 = (f32[256,1152]{1,0:T(8,128)S(1)}, f32[256,1152]{1,0:T(8,128)}, u32[]{:S(2)}) copy-start(f32[256,1152]{1,0:T(8,128)} %copy-done.14) | copy-start | bytes 3538948
  318.3 1.8 copy-start.20
  320.1 1.3 copy-start.3
  320.1 1.3 copy-start.22
  321.3 1.3 copy-start.5
  321.3 1.3 copy-start.24
  322.6 1.3 copy-start.7
  322.6 1.3 copy-start.28
  323.9 1.3 copy-start.10
  323.9 1.3 copy-start.26
  325.2 1.3 copy-start.12
  325.2 1.3 copy-start.30
  327.4 48.1 %copy-start.1 = (f32[128,1152]{1,0:T(8,128)S(1)}, f32[128,1152]{1,0:T(8,128)}, u32[]{:S(2)}) copy-start(f32[128,1152]{1,0:T(8,128)} %param.5) | copy-start | bytes 1769476
  375.5 1.3 copy-start.13
Sparse Core Ops, SparseCore 0:
  10.6 33.1 all-gather.1
  318.4 57.0 reduce-scatter.1
where the time goes:
time: 385 us
  waiting for transfers between devices  233 us (61%)
  starting transfers between devices  86.3 us (22%)
  matrix products  37.8 us (10%)
  between operations  15.8 us (4%)
  other arithmetic  6.67 us (2%)
  local copies, waits for them, and re-layouts  5.62 us (1%)
    ppermute x14, waiting for transfers between devices, shifted(): return lax.ppermute(block, axis, route)  152 us
    ppermute x14, starting transfers between devices, shifted(): return lax.ppermute(block, axis, route)  86.2 us
    reduce_scatter x1, waiting for transfers between devices, local(): lax.psum_scatter(text_sums, 'cuts', scatter_dimension=0, tiled=True)  47.1 us
    all_gather x1, waiting for transfers between devices, local(): visiting = lax.all_gather(y_rows, 'cuts', axis=0, tiled=True)  33.3 us
    dot_general x8, matrix products, local(): to_text = scale * jnp.dot(grads.T, x_rows, precision=hp)  18.8 us
    dot_general x8, matrix products, local(): logits = scale * jnp.dot(x_rows, visiting.T, precision=hp) + shift_bias  11.5 us
  transfers between devices with their start and end apart: 16, of which 11 were waited for; matrix products, arithmetic and copies ran while one was open for 9% of the time, Pallas kernels for 0%

commit v1 on v0

v1 whole, which is shorter than its diff:
```python
import jax
import jax.numpy as jnp
from jax import lax
from jax.sharding import PartitionSpec as P

GROUPS, BLOCKS = 2, 128
HIGH = lax.Precision.HIGH


def moved(block, place):
    pairs = []
    for group in range(GROUPS):
        for position in range(BLOCKS):
            to_group, to_position = place(group, position)
            pairs.append((group * BLOCKS + position, to_group * BLOCKS + to_position % BLOCKS))
    return lax.ppermute(block, ("cuts", "blk"), pairs)


def along(distance):
    return lambda group, position: (group, position + distance)


def other_core(group, position):
    return group, position ^ 1


def other_group(group, position):
    return 1 - group, position


def odd_along(distance):
    return lambda group, position: (group, position + distance * (position % 2))


def normalize(rows_in):
    inverse = lax.rsqrt(jnp.sum(rows_in * rows_in, axis=-1, keepdims=True) + 1e-06)
    return (rows_in * inverse, inverse)


def local(image_embed, text_embed, log_scale, bias):
    x_own, x_inv = normalize(image_embed)
    y_own, y_inv = normalize(text_embed)
    scale = jnp.exp(log_scale[0])
    shift = bias[0]
    rows = x_own.shape[0]
    y_far = [moved(y_own, along(2 * d)) for d in (1, 2, 3)]
    x_cut = moved(x_own, other_group)
    y_alt = moved(y_own, odd_along(8))
    x_here = jnp.concatenate([x_own, x_cut])
    x_near = moved(x_here, other_core)
    x_all = jnp.concatenate([x_here, x_near])

    def pair_terms(x_rows, y_rows, own):
        logits = scale * jnp.dot(x_rows, y_rows.T, precision=HIGH) + shift
        if own:
            row_ids = lax.broadcasted_iota(jnp.int32, logits.shape, 0)
            col_ids = lax.broadcasted_iota(jnp.int32, logits.shape, 1)
            positive = row_ids == col_ids
            signed = jax.nn.sigmoid(jnp.where(positive, -logits, logits))
            grads = jnp.where(positive, -signed, signed)
        else:
            grads = jax.nn.sigmoid(logits)
        to_image = jnp.dot(grads, y_rows, precision=HIGH)
        to_text = jnp.dot(grads.T, x_rows, precision=HIGH)
        return to_image, to_text

    gx_here, gy_own = pair_terms(x_here, y_own, True)
    gx_near, gy_alt = pair_terms(x_near, y_alt, False)
    gx_all = jnp.concatenate([gx_here, gx_near])
    for d, y_rows in zip((1, 2, 3), y_far):
        to_image, to_text = pair_terms(x_all, y_rows, False)
        gx_all = gx_all + to_image
        gy_own = gy_own + moved(to_text, along(-2 * d))
    gy_own = gy_own + moved(gy_alt, odd_along(-8))
    gx = gx_all[: 2 * rows] + moved(gx_all[2 * rows :], other_core)
    gx_own = gx[:rows] + moved(gx[rows:], other_group)
    image_part = scale * gx_own
    text_part = scale * gy_own
    image_grad = x_inv * (image_part - x_own * jnp.sum(x_own * image_part, axis=-1, keepdims=True))
    text_grad = y_inv * (text_part - y_own * jnp.sum(y_own * text_part, axis=-1, keepdims=True))
    return (image_grad, text_grad)


def solution(mesh):
    rows = P(("cuts", "blk"), None)
    return jax.shard_map(
        local, mesh=mesh, in_specs=(rows, rows, P(), P()), out_specs=(rows, rows), check_vma=False
    )
```

time: 385 us -> 189 us (0.49)
  waiting for transfers between devices: 233 us -> 118 us
  starting transfers between devices: 86.3 us -> 48.2 us
  matrix products: 37.8 us -> 13.8 us
  between operations: 15.8 us -> 2.19 us
  local copies, waits for them, and re-layouts: 5.62 us -> 0.13 us
    reduce_scatter x1 -> x0, waiting for transfers between devices: 47.1 us -> none  [local(): lax.psum_scatter(text_sums, 'cuts', scatter_dimension=0, tiled=True)]
    ppermute x14 -> x12, starting transfers between devices: 86.2 us -> 48.2 us  [moved(): return lax.ppermute(block, ('cuts', 'blk'), pairs)]
    ppermute x14 -> x12, waiting for transfers between devices: 152 us -> 118 us  [moved(): return lax.ppermute(block, ('cuts', 'blk'), pairs)]
    all_gather x1 -> x0, waiting for transfers between devices: 33.3 us -> none  [local(): visiting = lax.all_gather(y_rows, 'cuts', axis=0, tiled=True)]
    dot_general x24 -> x15, matrix products: 37.8 us -> 13.8 us  [the longest x5 4.85 us: pair_terms(): to_image = jnp.dot(grads, y_rows, precision=HIGH)]
    unnamed x62 -> x4, local copies, waits for them, and re-layouts: 5.62 us -> 0.01 us
  transfers between devices with their start and end apart: 16 -> 12, of which waited for: 11 -> 8; matrix products, arithmetic and copies ran while one was open for 9% -> 7% of each run, Pallas kernels for 0% -> 0%
where the time goes in v1:
time: 189 us
  waiting for transfers between devices  118 us (62%)
  starting transfers between devices  48.2 us (26%)
  matrix products  13.8 us (7%)
  other arithmetic  6.15 us (3%)
  between operations  2.19 us (1%)
    ppermute x12, waiting for transfers between devices, moved(): return lax.ppermute(block, ('cuts', 'blk'), pairs)  118 us
    ppermute x12, starting transfers between devices, moved(): return lax.ppermute(block, ('cuts', 'blk'), pairs)  48.2 us
    dot_general x5, matrix products, pair_terms(): to_image = jnp.dot(grads, y_rows, precision=HIGH)  4.85 us
    dot_general x5, matrix products, pair_terms(): logits = scale * jnp.dot(x_rows, y_rows.T, precision=HIGH) + shift  4.76 us
    dot_general x5, matrix products, pair_terms(): to_text = jnp.dot(grads.T, x_rows, precision=HIGH)  4.17 us
  transfers between devices with their start and end apart: 12, of which 8 were waited for; matrix products, arithmetic and copies ran while one was open for 7% of the time, Pallas kernels for 0%

profile of v1, /device:TPU:1, one launch (start us, length us, event | category | flops | bytes accessed | tf_op | source)
XLA Modules:
  0.0 188.5 jit_solution(18142403656011168673)
XLA Ops:
  0.6 0.0 copy-start.1
  0.6 1.2 multiply_reduce_fusion.3
  1.9 1.2 broadcast_multiply_fusion.1
  3.1 3.8 %collective-permute-start = (f32[128,1152]{1,0:T(8,128)S(1)}, f32[128,1152]{1,0:T(8,128)S(1)}, u32[]{:S(2)}, u32[]{:S(2)}) collective-permute-start(f32[128,1152]{1,0:T(8,128)S(1)} %broadcast_multiply_fusion.1), channel_id=1, source_target_pairs={{0,128},{1,129},{2,130},{3,131},{4,132},{5,133},{6,134},{7,135},{8... | collective-permute-start | bytes 1769480 | tf_op jit(solution)/shard_map/ppermute | solution.py:16
  6.9 1.2 multiply_reduce_fusion.2
  8.1 10.8 %collective-permute-done = f32[128,1152]{1,0:T(8,128)S(1)} collective-permute-done((f32[128,1152]{1,0:T(8,128)S(1)}, f32[128,1152]{1,0:T(8,128)S(1)}, u32[]{:S(2)}, u32[]{:S(2)}) %collective-permute-start) | collective-permute-done | bytes 589856 | tf_op jit(solution)/shard_map/ppermute | solution.py:16
  18.9 0.1 pad_maximum_fusion.1
  19.0 2.4 %collective-permute-start.1 = (f32[256,1152]{1,0:T(8,128)S(1)}, f32[256,1152]{1,0:T(8,128)S(1)}, u32[]{:S(2)}, u32[]{:S(2)}) collective-permute-start(f32[256,1152]{1,0:T(8,128)S(1)} %pad_maximum_fusion.1), channel_id=1, source_target_pairs={{0,1},{1,0},{2,3},{3,2},{4,5},{5,4},{6,7},{7,6},{8,9},{9,8},{10,11... | collective-permute-start | bytes 3538952 | tf_op jit(solution)/shard_map/ppermute | solution.py:16
  21.4 0.0 copy-done.1
  21.4 0.1 broadcast_multiply_fusion
  21.5 2.9 %collective-permute-start.4 = (f32[128,1152]{1,0:T(8,128)S(1)}, f32[128,1152]{1,0:T(8,128)S(1)}, u32[]{:S(2)}, u32[]{:S(2)}) collective-permute-start(f32[128,1152]{1,0:T(8,128)S(1)} %broadcast_multiply_fusion), channel_id=1, source_target_pairs={{0,4},{1,5},{2,6},{3,7},{4,8},{5,9},{6,10},{7,11},{8,12},{9,13},{1... | collective-permute-start | bytes 1769480 | tf_op jit(solution)/shard_map/ppermute | solution.py:16
  24.4 0.3 collective-permute-start.3
  24.7 3.4 %collective-permute-start.5 = (f32[128,1152]{1,0:T(8,128)S(1)}, f32[128,1152]{1,0:T(8,128)S(1)}, u32[]{:S(2)}, u32[]{:S(2)}) collective-permute-start(f32[128,1152]{1,0:T(8,128)S(1)} %broadcast_multiply_fusion), channel_id=1, source_target_pairs={{0,6},{1,7},{2,8},{3,9},{4,10},{5,11},{6,12},{7,13},{8,14},{9,15},... | collective-permute-start | bytes 1769480 | tf_op jit(solution)/shard_map/ppermute | solution.py:16
  28.0 3.6 %collective-permute-start.2 = (f32[128,1152]{1,0:T(8,128)S(1)}, f32[128,1152]{1,0:T(8,128)S(1)}, u32[]{:S(2)}, u32[]{:S(2)}) collective-permute-start(f32[128,1152]{1,0:T(8,128)S(1)} %broadcast_multiply_fusion), channel_id=1, source_target_pairs={{0,0},{1,9},{2,2},{3,11},{4,4},{5,13},{6,6},{7,15},{8,8},{9,17},{1... | collective-permute-start | bytes 1769480 | tf_op jit(solution)/shard_map/ppermute | solution.py:16
  33.0 0.7 negate_select_fusion
  33.7 0.6 fusion.35
  34.3 32.0 %collective-permute-done.4 = f32[128,1152]{1,0:T(8,128)S(1)} collective-permute-done((f32[128,1152]{1,0:T(8,128)S(1)}, f32[128,1152]{1,0:T(8,128)S(1)}, u32[]{:S(2)}, u32[]{:S(2)}) %collective-permute-start.4) | collective-permute-done | bytes 589856 | tf_op jit(solution)/shard_map/ppermute | solution.py:16
  66.3 0.0 collective-permute-done.1
  66.3 1.1 fusion.15
  67.5 2.6 %collective-permute-done.2 = f32[128,1152]{1,0:T(8,128)S(1)} collective-permute-done((f32[128,1152]{1,0:T(8,128)S(1)}, f32[128,1152]{1,0:T(8,128)S(1)}, u32[]{:S(2)}, u32[]{:S(2)}) %collective-permute-start.2) | collective-permute-done | bytes 589856 | tf_op jit(solution)/shard_map/ppermute | solution.py:16
  70.1 0.7 fusion.25
  70.7 1.1 fusion.37
  71.8 0.0 collective-permute-done.5
  71.9 1.1 fusion.20
  73.0 0.6 fusion.36
  73.6 1.1 fusion.38
  74.7 1.2 collective-permute-done.3
  75.9 1.1 fusion.10
  77.1 1.4 fusion.1
  78.5 0.1 slice.17
  78.6 0.9 collective-permute-start.6
  79.5 0.9 fusion.34
  80.4 23.8 %collective-permute-start.8 = (f32[128,1152]{1,0:T(8,128)S(1)}, f32[128,1152]{1,0:T(8,128)S(1)}, u32[]{:S(2)}, u32[]{:S(2)}) collective-permute-start(f32[128,1152]{1,0:T(8,128)S(1)} %fusion.34), channel_id=1, source_target_pairs={{0,126},{1,127},{2,0},{3,1},{4,2},{5,3},{6,4},{7,5},{8,6},{9,7},{1... | collective-permute-start | bytes 1769480 | tf_op jit(solution)/shard_map/ppermute | solution.py:16
  104.2 0.9 fusion.33
  105.2 0.1 collective-permute-start.9
  105.3 0.9 fusion.32
  106.2 2.1 %collective-permute-start.10 = (f32[128,1152]{1,0:T(8,128)S(1)}, f32[128,1152]{1,0:T(8,128)S(1)}, u32[]{:S(2)}, u32[]{:S(2)}) collective-permute-start(f32[128,1152]{1,0:T(8,128)S(1)} %fusion.32), channel_id=1, source_target_pairs={{0,122},{1,123},{2,124},{3,125},{4,126},{5,127},{6,0},{7,1},{8,2},... | collective-permute-start | bytes 1769480 | tf_op jit(solution)/shard_map/ppermute | solution.py:16
  108.3 0.5 fusion.39
  108.9 1.9 %collective-permute-start.11 = (f32[128,1152]{1,0:T(8,128)S(1)}, f32[128,1152]{1,0:T(8,128)S(1)}, u32[]{:S(2)}, u32[]{:S(2)}) collective-permute-start(f32[128,1152]{1,0:T(8,128)S(1)} %fusion.39), channel_id=1, source_target_pairs={{0,0},{1,121},{2,2},{3,123},{4,4},{5,125},{6,6},{7,127},{8,8},{9,1... | collective-permute-start | bytes 1769480 | tf_op jit(solution)/shard_map/ppermute | solution.py:16
  110.8 0.0 collective-permute-done.6
  110.8 0.1 slice_add_fusion
  111.0 0.0 copy-start
  111.0 3.0 %collective-permute-start.7 = (f32[128,1152]{1,0:T(8,128)S(1)}, f32[128,1152]{1,0:T(8,128)S(1)}, u32[]{:S(2)}, u32[]{:S(2)}) collective-permute-start(f32[128,1152]{1,0:T(8,128)S(1)} %slice.19), channel_id=1, source_target_pairs={{0,128},{1,129},{2,130},{3,131},{4,132},{5,133},{6,134},{7,135},{8... | collective-permute-start | bytes 1769480 | tf_op jit(solution)/shard_map/ppermute | solution.py:16
  114.0 21.5 %collective-permute-done.8 = f32[128,1152]{1,0:T(8,128)S(1)} collective-permute-done((f32[128,1152]{1,0:T(8,128)S(1)}, f32[128,1152]{1,0:T(8,128)S(1)}, u32[]{:S(2)}, u32[]{:S(2)}) %collective-permute-start.8) | collective-permute-done | bytes 589856 | tf_op jit(solution)/shard_map/ppermute | solution.py:16
  135.5 24.6 %collective-permute-done.9 = f32[128,1152]{1,0:T(8,128)S(1)} collective-permute-done((f32[128,1152]{1,0:T(8,128)S(1)}, f32[128,1152]{1,0:T(8,128)S(1)}, u32[]{:S(2)}, u32[]{:S(2)}) %collective-permute-start.9) | collective-permute-done | bytes 589856 | tf_op jit(solution)/shard_map/ppermute | solution.py:16
  160.1 18.1 %collective-permute-done.10 = f32[128,1152]{1,0:T(8,128)S(1)} collective-permute-done((f32[128,1152]{1,0:T(8,128)S(1)}, f32[128,1152]{1,0:T(8,128)S(1)}, u32[]{:S(2)}, u32[]{:S(2)}) %collective-permute-start.10) | collective-permute-done | bytes 589856 | tf_op jit(solution)/shard_map/ppermute | solution.py:16
  178.2 7.3 %collective-permute-done.11 = f32[128,1152]{1,0:T(8,128)S(1)} collective-permute-done((f32[128,1152]{1,0:T(8,128)S(1)}, f32[128,1152]{1,0:T(8,128)S(1)}, u32[]{:S(2)}, u32[]{:S(2)}) %collective-permute-start.11) | collective-permute-done | bytes 589856 | tf_op jit(solution)/shard_map/ppermute | solution.py:16
  185.5 0.8 multiply_reduce_fusion
  186.3 1.0 subtract_multiply_fusion
  187.3 0.0 collective-permute-done.7
  187.3 0.0 copy-done
  187.3 0.2 multiply_reduce_fusion.1
  187.5 1.0 subtract_multiply_fusion.1
  (3 shorter events, 0.1 us)
Async XLA Ops:
  0.6 20.7 %copy-start.1 = (f32[128,1152]{1,0:T(8,128)S(1)}, f32[128,1152]{1,0:T(8,128)}, u32[]{:S(2)}) copy-start(f32[128,1152]{1,0:T(8,128)} %param.5) | copy-start | bytes 1769476
  3.1 15.8 %collective-permute-start = (f32[128,1152]{1,0:T(8,128)S(1)}, f32[128,1152]{1,0:T(8,128)S(1)}, u32[]{:S(2)}, u32[]{:S(2)}) collective-permute-start(f32[128,1152]{1,0:T(8,128)S(1)} %broadcast_multiply_fusion.1), channel_id=1, source_target_pairs={{0,128},{1,129},{2,130},{3,131},{4,132},{5,133},{6,134},{7,135},{8... | collective-permute-start | bytes 1769480 | tf_op jit(solution)/shard_map/ppermute | solution.py:16
  19.0 47.4 %collective-permute-start.1 = (f32[256,1152]{1,0:T(8,128)S(1)}, f32[256,1152]{1,0:T(8,128)S(1)}, u32[]{:S(2)}, u32[]{:S(2)}) collective-permute-start(f32[256,1152]{1,0:T(8,128)S(1)} %pad_maximum_fusion.1), channel_id=1, source_target_pairs={{0,1},{1,0},{2,3},{3,2},{4,5},{5,4},{6,7},{7,6},{8,9},{9,8},{10,11... | collective-permute-start | bytes 3538952 | tf_op jit(solution)/shard_map/ppermute | solution.py:16
  21.5 44.9 %collective-permute-start.4 = (f32[128,1152]{1,0:T(8,128)S(1)}, f32[128,1152]{1,0:T(8,128)S(1)}, u32[]{:S(2)}, u32[]{:S(2)}) collective-permute-start(f32[128,1152]{1,0:T(8,128)S(1)} %broadcast_multiply_fusion), channel_id=1, source_target_pairs={{0,4},{1,5},{2,6},{3,7},{4,8},{5,9},{6,10},{7,11},{8,12},{9,13},{1... | collective-permute-start | bytes 1769480 | tf_op jit(solution)/shard_map/ppermute | solution.py:16
  24.4 51.6 %collective-permute-start.3 = (f32[128,1152]{1,0:T(8,128)S(1)}, f32[128,1152]{1,0:T(8,128)S(1)}, u32[]{:S(2)}, u32[]{:S(2)}) collective-permute-start(f32[128,1152]{1,0:T(8,128)S(1)} %broadcast_multiply_fusion), channel_id=1, source_target_pairs={{0,2},{1,3},{2,4},{3,5},{4,6},{5,7},{6,8},{7,9},{8,10},{9,11},{10,... | collective-permute-start | bytes 1769480 | tf_op jit(solution)/shard_map/ppermute | solution.py:16
  24.7 47.2 %collective-permute-start.5 = (f32[128,1152]{1,0:T(8,128)S(1)}, f32[128,1152]{1,0:T(8,128)S(1)}, u32[]{:S(2)}, u32[]{:S(2)}) collective-permute-start(f32[128,1152]{1,0:T(8,128)S(1)} %broadcast_multiply_fusion), channel_id=1, source_target_pairs={{0,6},{1,7},{2,8},{3,9},{4,10},{5,11},{6,12},{7,13},{8,14},{9,15},... | collective-permute-start | bytes 1769480 | tf_op jit(solution)/shard_map/ppermute | solution.py:16
  28.0 42.0 %collective-permute-start.2 = (f32[128,1152]{1,0:T(8,128)S(1)}, f32[128,1152]{1,0:T(8,128)S(1)}, u32[]{:S(2)}, u32[]{:S(2)}) collective-permute-start(f32[128,1152]{1,0:T(8,128)S(1)} %broadcast_multiply_fusion), channel_id=1, source_target_pairs={{0,0},{1,9},{2,2},{3,11},{4,4},{5,13},{6,6},{7,15},{8,8},{9,17},{1... | collective-permute-start | bytes 1769480 | tf_op jit(solution)/shard_map/ppermute | solution.py:16
  78.6 32.2 %collective-permute-start.6 = (f32[256,1152]{1,0:T(8,128)S(1)}, f32[256,1152]{1,0:T(8,128)S(1)}, u32[]{:S(2)}, u32[]{:S(2)}) collective-permute-start(f32[256,1152]{1,0:T(8,128)S(1)} %slice.17), channel_id=1, source_target_pairs={{0,1},{1,0},{2,3},{3,2},{4,5},{5,4},{6,7},{7,6},{8,9},{9,8},{10,11... | collective-permute-start | bytes 3538952 | tf_op jit(solution)/shard_map/ppermute | solution.py:16
  80.4 55.1 %collective-permute-start.8 = (f32[128,1152]{1,0:T(8,128)S(1)}, f32[128,1152]{1,0:T(8,128)S(1)}, u32[]{:S(2)}, u32[]{:S(2)}) collective-permute-start(f32[128,1152]{1,0:T(8,128)S(1)} %fusion.34), channel_id=1, source_target_pairs={{0,126},{1,127},{2,0},{3,1},{4,2},{5,3},{6,4},{7,5},{8,6},{9,7},{1... | collective-permute-start | bytes 1769480 | tf_op jit(solution)/shard_map/ppermute | solution.py:16
  105.2 54.9 %collective-permute-start.9 = (f32[128,1152]{1,0:T(8,128)S(1)}, f32[128,1152]{1,0:T(8,128)S(1)}, u32[]{:S(2)}, u32[]{:S(2)}) collective-permute-start(f32[128,1152]{1,0:T(8,128)S(1)} %fusion.33), channel_id=1, source_target_pairs={{0,124},{1,125},{2,126},{3,127},{4,0},{5,1},{6,2},{7,3},{8,4},{9,5... | collective-permute-start | bytes 1769480 | tf_op jit(solution)/shard_map/ppermute | solution.py:16
  106.2 72.0 %collective-permute-start.10 = (f32[128,1152]{1,0:T(8,128)S(1)}, f32[128,1152]{1,0:T(8,128)S(1)}, u32[]{:S(2)}, u32[]{:S(2)}) collective-permute-start(f32[128,1152]{1,0:T(8,128)S(1)} %fusion.32), channel_id=1, source_target_pairs={{0,122},{1,123},{2,124},{3,125},{4,126},{5,127},{6,0},{7,1},{8,2},... | collective-permute-start | bytes 1769480 | tf_op jit(solution)/shard_map/ppermute | solution.py:16
  108.9 76.6 %collective-permute-start.11 = (f32[128,1152]{1,0:T(8,128)S(1)}, f32[128,1152]{1,0:T(8,128)S(1)}, u32[]{:S(2)}, u32[]{:S(2)}) collective-permute-start(f32[128,1152]{1,0:T(8,128)S(1)} %fusion.39), channel_id=1, source_target_pairs={{0,0},{1,121},{2,2},{3,123},{4,4},{5,125},{6,6},{7,127},{8,8},{9,1... | collective-permute-start | bytes 1769480 | tf_op jit(solution)/shard_map/ppermute | solution.py:16
  111.0 76.3 %copy-start = (f32[128,1152]{1,0:T(8,128)S(1)}, f32[128,1152]{1,0:T(8,128)}, u32[]{:S(2)}) copy-start(f32[128,1152]{1,0:T(8,128)} %param.4) | copy-start | bytes 1769476
  111.0 76.3 %collective-permute-start.7 = (f32[128,1152]{1,0:T(8,128)S(1)}, f32[128,1152]{1,0:T(8,128)S(1)}, u32[]{:S(2)}, u32[]{:S(2)}) collective-permute-start(f32[128,1152]{1,0:T(8,128)S(1)} %slice.19), channel_id=1, source_target_pairs={{0,128},{1,129},{2,130},{3,131},{4,132},{5,133},{6,134},{7,135},{8... | collective-permute-start | bytes 1769480 | tf_op jit(solution)/shard_map/ppermute | solution.py:16

commit v2 on v1

--- a/solution.py
+++ b/solution.py
@@ -3,7 +3,7 @@
 from jax import lax
 from jax.sharding import PartitionSpec as P
 
-GROUPS, BLOCKS = 2, 128
+GROUPS, BLOCKS, ROW = 2, 128, 8
 HIGH = lax.Precision.HIGH
 
 
@@ -16,8 +16,19 @@
     return lax.ppermute(block, ("cuts", "blk"), pairs)
 
 
-def along(distance):
-    return lambda group, position: (group, position + distance)
+def next_row(group, position):
+    return (group, position + ROW) if position % 2 == 0 else (1 - group, position + ROW)
+
+
+def last_row(group, position):
+    return (group, position - ROW) if position % 2 == 0 else (1 - group, position - ROW)
+
+
+def in_row(chips):
+    return lambda group, position: (
+        group,
+        position // ROW * ROW + (position + 2 * chips) % ROW,
+    )
 
 
 def other_core(group, position):
@@ -26,10 +37,6 @@
 
 def other_group(group, position):
     return 1 - group, position
-
-
-def odd_along(distance):
-    return lambda group, position: (group, position + distance * (position % 2))
 
 
 def normalize(rows_in):
@@ -43,9 +50,17 @@
     scale = jnp.exp(log_scale[0])
     shift = bias[0]
     rows = x_own.shape[0]
-    y_far = [moved(y_own, along(2 * d)) for d in (1, 2, 3)]
+    position = lax.axis_index("blk")
+    column = position % ROW // 2
+    odd = position % 2 == 1
+    y_last = moved(y_own, next_row)
+    hops = (1, 2, -1)
+    from_last = [column >= 3, column >= 2, column >= 1]
+    y_far = [
+        moved(jnp.where(last, y_last, y_own), in_row(hop)) for hop, last in zip(hops, from_last)
+    ]
     x_cut = moved(x_own, other_group)
-    y_alt = moved(y_own, odd_along(8))
+    y_alt = jnp.where(odd, y_last, y_own)
     x_here = jnp.concatenate([x_own, x_cut])
     x_near = moved(x_here, other_core)
     x_all = jnp.concatenate([x_here, x_near])
@@ -67,11 +82,15 @@
     gx_here, gy_own = pair_terms(x_here, y_own, True)
     gx_near, gy_alt = pair_terms(x_near, y_alt, False)
     gx_all = jnp.concatenate([gx_here, gx_near])
-    for d, y_rows in zip((1, 2, 3), y_far):
+    gy_last = jnp.where(odd, gy_alt, 0.0)
+    gy_own = gy_own + jnp.where(odd, 0.0, gy_alt)
+    for hop, last, y_rows in zip(hops, from_last, y_far):
         to_image, to_text = pair_terms(x_all, y_rows, False)
         gx_all = gx_all + to_image
-        gy_own = gy_own + moved(to_text, along(-2 * d))
-    gy_own = gy_own + moved(gy_alt, odd_along(-8))
+        back = moved(to_text, in_row(-hop))
+        gy_last = gy_last + jnp.where(last, back, 0.0)
+        gy_own = gy_own + jnp.where(last, 0.0, back)
+    gy_own = gy_own + moved(gy_last, last_row)
     gx = gx_all[: 2 * rows] + moved(gx_all[2 * rows :], other_core)
     gx_own = gx[:rows] + moved(gx[rows:], other_group)
     image_part = scale * gx_own

time: 189 us -> 135 us (0.71)
  waiting for transfers between devices: 118 us -> 65.3 us
  starting transfers between devices: 48.2 us -> 34.9 us
  matrix products: 13.8 us -> 23.7 us
  other arithmetic: 6.15 us -> 8.61 us
    ppermute x12, waiting for transfers between devices: 118 us -> 65.3 us  [moved(): return lax.ppermute(block, ('cuts', 'blk'), pairs)]
    ppermute x12, starting transfers between devices: 48.2 us -> 34.9 us  [moved(): return lax.ppermute(block, ('cuts', 'blk'), pairs)]
    dot_general x5, matrix products: 4.76 us -> 9.78 us  [pair_terms(): logits = scale * jnp.dot(x_rows, y_rows.T, precision=HIGH) + shift]
    dot_general x5, matrix products: 4.17 us -> 9.15 us  [pair_terms(): to_text = jnp.dot(grads.T, x_rows, precision=HIGH)]
  transfers between devices with their start and end apart: 12 -> 12, of which waited for: 8 -> 8; matrix products, arithmetic and copies ran while one was open for 7% -> 21% of each run, Pallas kernels for 0% -> 0%
where the time goes in v2:
time: 135 us
  waiting for transfers between devices  65.3 us (48%)
  starting transfers between devices  34.9 us (26%)
  matrix products  23.7 us (18%)
  other arithmetic  8.61 us (6%)
  between operations  2.16 us (2%)
    ppermute x12, waiting for transfers between devices, moved(): return lax.ppermute(block, ('cuts', 'blk'), pairs)  65.3 us
    ppermute x12, starting transfers between devices, moved(): return lax.ppermute(block, ('cuts', 'blk'), pairs)  34.9 us
    dot_general x5, matrix products, pair_terms(): logits = scale * jnp.dot(x_rows, y_rows.T, precision=HIGH) + shift  9.78 us
    dot_general x5, matrix products, pair_terms(): to_text = jnp.dot(grads.T, x_rows, precision=HIGH)  9.15 us
    dot_general x5, matrix products, pair_terms(): to_image = jnp.dot(grads, y_rows, precision=HIGH)  4.81 us
  transfers between devices with their start and end apart: 12, of which 8 were waited for; matrix products, arithmetic and copies ran while one was open for 21% of the time, Pallas kernels for 0%

profile of v2, /device:TPU:1, one launch (start us, length us, event | category | flops | bytes accessed | tf_op | source)
XLA Modules:
  0.0 134.9 jit_solution(10929031300528667130)
XLA Ops:
  0.6 0.0 copy-start
  0.6 1.2 multiply_reduce_fusion.3
  1.9 1.2 broadcast_multiply_fusion.1
  3.1 3.8 %collective-permute-start = (f32[128,1152]{1,0:T(8,128)S(1)}, f32[128,1152]{1,0:T(8,128)S(1)}, u32[]{:S(2)}, u32[]{:S(2)}) collective-permute-start(f32[128,1152]{1,0:T(8,128)S(1)} %broadcast_multiply_fusion.1), channel_id=1, source_target_pairs={{0,128},{1,129},{2,130},{3,131},{4,132},{5,133},{6,134},{7,135},{8... | collective-permute-start | bytes 1769480 | tf_op jit(solution)/shard_map/ppermute | solution.py:16
  6.9 1.2 multiply_reduce_fusion.2
  8.1 0.0 copy-done
  8.1 0.1 broadcast_multiply_fusion
  8.2 0.9 collective-permute-start.2
  9.1 14.5 %collective-permute-done = f32[128,1152]{1,0:T(8,128)S(1)} collective-permute-done((f32[128,1152]{1,0:T(8,128)S(1)}, f32[128,1152]{1,0:T(8,128)S(1)}, u32[]{:S(2)}, u32[]{:S(2)}) %collective-permute-start) | collective-permute-done | bytes 589856 | tf_op jit(solution)/shard_map/ppermute | solution.py:16
  23.6 1.1 pad_maximum_fusion.1
  24.7 2.9 %collective-permute-start.1 = (f32[256,1152]{1,0:T(8,128)}, f32[256,1152]{1,0:T(8,128)}, u32[]{:S(2)}, u32[]{:S(2)}) collective-permute-start(f32[256,1152]{1,0:T(8,128)} %pad_maximum_fusion.1), channel_id=1, source_target_pairs={{0,1},{1,0},{2,3},{3,2},{4,5},{5,4},{6,7},{7,6},{8,9},{9,8},{10,11... | collective-permute-start | bytes 3538952 | tf_op jit(solution)/shard_map/ppermute | solution.py:16
  27.6 0.0 collective-permute-done.2
  27.6 1.4 %broadcast_select_fusion.2 = (f32[128,1152]{1,0:T(8,128)}, f32[128,1152]{1,0:T(8,128)}, f32[128,1152]{1,0:T(8,128)}) fusion(f32[128,1152]{1,0:T(8,128)S(1)} %collective-permute-done.2, pred[]{:T(512)S(6)} %ge.9, pred[]{:T(512)S(6)} %ge.11, pred[]{:T(512)S(6)} %ge.10, f32[128,1152]{1,0:T(8,128)S(1)} %copy-done, f32[128]{0:T(128)S(1)} %add_rsqrt_fusion), kind=kLoop, calls=%fused_computation.51 | loop fusion | flops 589824 | bytes 2949635 | tf_op jit(solution)/shard_map/jit(_where)/select_n | solution.py:60
  29.0 1.3 collective-permute-start.3
  31.7 2.5 %collective-permute-start.4 = (f32[128,1152]{1,0:T(8,128)}, f32[128,1152]{1,0:T(8,128)S(1)}, u32[]{:S(2)}, u32[]{:S(2)}) collective-permute-start(f32[128,1152]{1,0:T(8,128)} %get-tuple-element.4), channel_id=1, source_target_pairs={{0,4},{1,5},{2,6},{3,7},{4,0},{5,1},{6,2},{7,3},{8,12},{9,13},{10,... | collective-permute-start | bytes 1769480 | tf_op jit(solution)/shard_map/ppermute | solution.py:16
  34.2 1.2 collective-permute-start.5
  35.4 0.7 negate_select_fusion
  36.0 0.6 fusion.37
  36.6 3.6 %collective-permute-done.3 = f32[128,1152]{1,0:T(8,128)S(1)} collective-permute-done((f32[128,1152]{1,0:T(8,128)}, f32[128,1152]{1,0:T(8,128)S(1)}, u32[]{:S(2)}, u32[]{:S(2)}) %collective-permute-start.3) | collective-permute-done | bytes 589856 | tf_op jit(solution)/shard_map/ppermute | solution.py:16
  40.2 0.0 collective-permute-done.1
  40.2 2.4 %fusion.11 = f32[512,128]{1,0:T(8,128)S(1)} fusion(f32[128,1152]{1,0:T(8,128)S(1)} %collective-permute-done.3, f32[]{:T(128)} %bitcast.23, f32[]{:T(128)} %bitcast, f32[256,1152]{1,0:T(8,128)} %collective-permute-done.1, f32[128,1152]{1,0:T(8,128)S(1)} %collective-permute-done, f32[128,1152]{1,0:T(8,128)S(1)} %broadcast_multiply_fusion.1), kind=kOutput, calls=%fused_computation.19 | convolution fusion | flops 454492160 | bytes 3211272 | tf_op jit(solution)/shard_map/dot_general | solution.py:69
  42.6 2.1 %fusion.36 = f32[128,1152]{1,0:T(8,128)S(1)} fusion(f32[512,128]{1,0:T(8,128)S(1)} %fusion.11, f32[256,1152]{1,0:T(8,128)} %collective-permute-done.1, f32[128,1152]{1,0:T(8,128)S(1)} %collective-permute-done, f32[128,1152]{1,0:T(8,128)S(1)} %broadcast_multiply_fusion.1), kind=kOutput, calls=%fused_computation.65 | convolution fusion | flops 454164480 | bytes 3211264 | tf_op jit(solution)/shard_map/dot_general | solution.py:79
  44.8 1.7 %collective-permute-start.8 = (f32[128,1152]{1,0:T(8,128)S(1)}, f32[128,1152]{1,0:T(8,128)S(1)}, u32[]{:S(2)}, u32[]{:S(2)}) collective-permute-start(f32[128,1152]{1,0:T(8,128)S(1)} %fusion.36), channel_id=1, source_target_pairs={{0,6},{1,7},{2,0},{3,1},{4,2},{5,3},{6,4},{7,5},{8,14},{9,15},{10,... | collective-permute-start | bytes 1769480 | tf_op jit(solution)/shard_map/ppermute | solution.py:16
  46.5 7.6 %collective-permute-done.4 = f32[128,1152]{1,0:T(8,128)S(1)} collective-permute-done((f32[128,1152]{1,0:T(8,128)}, f32[128,1152]{1,0:T(8,128)S(1)}, u32[]{:S(2)}, u32[]{:S(2)}) %collective-permute-start.4) | collective-permute-done | bytes 589856 | tf_op jit(solution)/shard_map/ppermute | solution.py:16
  54.1 2.4 %fusion.16 = f32[512,128]{1,0:T(8,128)S(1)} fusion(f32[128,1152]{1,0:T(8,128)S(1)} %collective-permute-done.4, f32[]{:T(128)} %bitcast.25, f32[]{:T(128)} %bitcast, f32[256,1152]{1,0:T(8,128)} %collective-permute-done.1, f32[128,1152]{1,0:T(8,128)S(1)} %collective-permute-done, f32[128,1152]{1,0:T(8,128)S(1)} %broadcast_multiply_fusion.1), kind=kOutput, calls=%fused_computation.24 | convolution fusion | flops 454492160 | bytes 3211272 | tf_op jit(solution)/shard_map/dot_general | solution.py:69
  56.5 1.1 fusion.38
  57.6 1.4 %collective-permute-done.5 = f32[128,1152]{1,0:T(8,128)S(1)} collective-permute-done((f32[128,1152]{1,0:T(8,128)}, f32[128,1152]{1,0:T(8,128)S(1)}, u32[]{:S(2)}, u32[]{:S(2)}) %collective-permute-start.5) | collective-permute-done | bytes 589856 | tf_op jit(solution)/shard_map/ppermute | solution.py:16
  58.9 2.4 %fusion.21 = f32[512,128]{1,0:T(8,128)S(1)} fusion(f32[128,1152]{1,0:T(8,128)S(1)} %collective-permute-done.5, f32[]{:T(128)} %bitcast.24, f32[]{:T(128)} %bitcast, f32[256,1152]{1,0:T(8,128)} %collective-permute-done.1, f32[128,1152]{1,0:T(8,128)S(1)} %collective-permute-done, f32[128,1152]{1,0:T(8,128)S(1)} %broadcast_multiply_fusion.1), kind=kOutput, calls=%fused_computation.29 | convolution fusion | flops 454492160 | bytes 3211272 | tf_op jit(solution)/shard_map/dot_general | solution.py:69
  61.3 1.1 fusion.39
  62.4 1.9 %fusion.26 = f32[256,128]{1,0:T(8,128)S(1)} fusion(f32[256,1152]{1,0:T(8,128)} %collective-permute-done.1, f32[128,1152]{1,0:T(8,128)S(1)} %collective-permute-done.2, f32[128,1152]{1,0:T(8,128)S(1)} %broadcast_multiply_fusion, pred[]{:T(512)S(6)} %eq.12, f32[]{:T(128)} %bitcast.26, f32[]{:T(128)} %bitcast), kind=kOutput, calls=%fused_computation.35 | convolution fusion | flops 226803712 | bytes 2490377 | tf_op jit(solution)/shard_map/dot_general | solution.py:69
  64.4 0.6 fusion.29
  65.0 1.4 %fusion.1 = f32[512,1152]{1,0:T(8,128)S(1)} fusion(f32[512,1152]{1,0:T(8,128)S(1)} %fusion.39, f32[512,1152]{1,0:T(8,128)S(1)} %fusion.38, f32[512,128]{1,0:T(8,128)S(1)} %fusion.11, f32[128,1152]{1,0:T(8,128)S(1)} %collective-permute-done.3, f32[256,1152]{1,0:T(8,128)S(1)} %fusion.29, f32[256,1152]{1,0:T(8,128)S(1)} %fusion.37), kind=kOutput, calls=%fused_computation.2 | convolution fusion | flops 455344128 | bytes 10289152 | tf_op jit(solution)/shard_map/dot_general | solution.py:78
  66.4 0.1 slice.17
  66.5 7.8 %collective-permute-start.6 = (f32[256,1152]{1,0:T(8,128)S(1)}, f32[256,1152]{1,0:T(8,128)S(1)}, u32[]{:S(2)}, u32[]{:S(2)}) collective-permute-start(f32[256,1152]{1,0:T(8,128)S(1)} %slice.17), channel_id=1, source_target_pairs={{0,1},{1,0},{2,3},{3,2},{4,5},{5,4},{6,7},{7,6},{8,9},{9,8},{10,11... | collective-permute-start | bytes 3538952 | tf_op jit(solution)/shard_map/ppermute | solution.py:16
  74.3 2.1 %fusion.35 = f32[128,1152]{1,0:T(8,128)S(1)} fusion(f32[512,128]{1,0:T(8,128)S(1)} %fusion.16, f32[256,1152]{1,0:T(8,128)} %collective-permute-done.1, f32[128,1152]{1,0:T(8,128)S(1)} %collective-permute-done, f32[128,1152]{1,0:T(8,128)S(1)} %broadcast_multiply_fusion.1), kind=kOutput, calls=%fused_computation.64 | convolution fusion | flops 454164480 | bytes 3211264 | tf_op jit(solution)/shard_map/dot_general | solution.py:79
  76.4 2.8 %collective-permute-start.9 = (f32[128,1152]{1,0:T(8,128)S(1)}, f32[128,1152]{1,0:T(8,128)S(1)}, u32[]{:S(2)}, u32[]{:S(2)}) collective-permute-start(f32[128,1152]{1,0:T(8,128)S(1)} %fusion.35), channel_id=1, source_target_pairs={{0,4},{1,5},{2,6},{3,7},{4,0},{5,1},{6,2},{7,3},{8,12},{9,13},{10,... | collective-permute-start | bytes 1769480 | tf_op jit(solution)/shard_map/ppermute | solution.py:16
  79.3 2.1 %fusion.34 = f32[128,1152]{1,0:T(8,128)S(1)} fusion(f32[512,128]{1,0:T(8,128)S(1)} %fusion.21, f32[256,1152]{1,0:T(8,128)} %collective-permute-done.1, f32[128,1152]{1,0:T(8,128)S(1)} %collective-permute-done, f32[128,1152]{1,0:T(8,128)S(1)} %broadcast_multiply_fusion.1), kind=kOutput, calls=%fused_computation.63 | convolution fusion | flops 454164480 | bytes 3211264 | tf_op jit(solution)/shard_map/dot_general | solution.py:79
  81.4 0.1 collective-permute-start.10
  81.5 0.0 collective-permute-done.8
  81.5 11.5 %collective-permute-done.9 = f32[128,1152]{1,0:T(8,128)S(1)} collective-permute-done((f32[128,1152]{1,0:T(8,128)S(1)}, f32[128,1152]{1,0:T(8,128)S(1)}, u32[]{:S(2)}, u32[]{:S(2)}) %collective-permute-start.9) | collective-permute-done | bytes 589856 | tf_op jit(solution)/shard_map/ppermute | solution.py:16
  93.0 12.9 %collective-permute-done.10 = f32[128,1152]{1,0:T(8,128)S(1)} collective-permute-done((f32[128,1152]{1,0:T(8,128)S(1)}, f32[128,1152]{1,0:T(8,128)S(1)}, u32[]{:S(2)}, u32[]{:S(2)}) %collective-permute-start.10) | collective-permute-done | bytes 589856 | tf_op jit(solution)/shard_map/ppermute | solution.py:16
  105.9 1.9 %select_add_fusion = (f32[128,1152]{1,0:T(8,128)S(1)}, f32[128,1152]{1,0:T(8,128)S(1)}) fusion(f32[128,1152]{1,0:T(8,128)S(1)} %collective-permute-done.10, f32[128,1152]{1,0:T(8,128)S(1)} %collective-permute-done.9, f32[128,1152]{1,0:T(8,128)S(1)} %collective-permute-done.8, pred[]{:T(512)S(6)} %ge.11, pred[]{:T(512)S(6)} %ge.10, pred[]{:T(512)S(6)} %ge.9, ...), kind=kOutput, calls=%fused_computation.42 | convolution fusion | flops 227524608 | bytes 4259844 | tf_op jit(solution)/shard_map/dot_general | solution.py:79
  107.8 6.4 %collective-permute-start.11 = (f32[128,1152]{1,0:T(8,128)S(1)}, f32[128,1152]{1,0:T(8,128)S(1)}, u32[]{:S(2)}, u32[]{:S(2)}) collective-permute-start(f32[128,1152]{1,0:T(8,128)S(1)} %get-tuple-element.5), channel_id=1, source_target_pairs={{0,120},{1,249},{2,122},{3,251},{4,124},{5,253},{6,126},{7,255},{8... | collective-permute-start | bytes 1769480 | tf_op jit(solution)/shard_map/ppermute | solution.py:16
  114.2 0.0 collective-permute-done.6
  114.2 0.2 slice_add_fusion
  114.4 3.5 %collective-permute-start.7 = (f32[128,1152]{1,0:T(8,128)S(1)}, f32[128,1152]{1,0:T(8,128)S(1)}, u32[]{:S(2)}, u32[]{:S(2)}) collective-permute-start(f32[128,1152]{1,0:T(8,128)S(1)} %slice.19), channel_id=1, source_target_pairs={{0,128},{1,129},{2,130},{3,131},{4,132},{5,133},{6,134},{7,135},{8... | collective-permute-start | bytes 1769480 | tf_op jit(solution)/shard_map/ppermute | solution.py:16
  117.9 6.8 %collective-permute-done.11 = f32[128,1152]{1,0:T(8,128)S(1)} collective-permute-done((f32[128,1152]{1,0:T(8,128)S(1)}, f32[128,1152]{1,0:T(8,128)S(1)}, u32[]{:S(2)}, u32[]{:S(2)}) %collective-permute-start.11) | collective-permute-done | bytes 589856 | tf_op jit(solution)/shard_map/ppermute | solution.py:16
  124.7 0.0 copy-start.1
  124.7 0.9 multiply_reduce_fusion
  125.6 1.0 subtract_multiply_fusion
  126.6 7.0 %collective-permute-done.7 = f32[128,1152]{1,0:T(8,128)S(1)} collective-permute-done((f32[128,1152]{1,0:T(8,128)S(1)}, f32[128,1152]{1,0:T(8,128)S(1)}, u32[]{:S(2)}, u32[]{:S(2)}) %collective-permute-start.7) | collective-permute-done | bytes 589856 | tf_op jit(solution)/shard_map/ppermute | solution.py:16
  133.6 0.0 copy-done.1
  133.6 0.2 multiply_reduce_fusion.1
  133.9 1.0 subtract_multiply_fusion.1
  (3 shorter events, 0.1 us)
Async XLA Ops:
  0.6 7.5 %copy-start = (f32[128,1152]{1,0:T(8,128)S(1)}, f32[128,1152]{1,0:T(8,128)}, u32[]{:S(2)}) copy-start(f32[128,1152]{1,0:T(8,128)} %param.5) | copy-start | bytes 1769476
  3.1 20.5 %collective-permute-start = (f32[128,1152]{1,0:T(8,128)S(1)}, f32[128,1152]{1,0:T(8,128)S(1)}, u32[]{:S(2)}, u32[]{:S(2)}) collective-permute-start(f32[128,1152]{1,0:T(8,128)S(1)} %broadcast_multiply_fusion.1), channel_id=1, source_target_pairs={{0,128},{1,129},{2,130},{3,131},{4,132},{5,133},{6,134},{7,135},{8... | collective-permute-start | bytes 1769480 | tf_op jit(solution)/shard_map/ppermute | solution.py:16
  8.2 19.4 %collective-permute-start.2 = (f32[128,1152]{1,0:T(8,128)S(1)}, f32[128,1152]{1,0:T(8,128)S(1)}, u32[]{:S(2)}, u32[]{:S(2)}) collective-permute-start(f32[128,1152]{1,0:T(8,128)S(1)} %broadcast_multiply_fusion), channel_id=1, source_target_pairs={{0,8},{1,137},{2,10},{3,139},{4,12},{5,141},{6,14},{7,143},{8,16},... | collective-permute-start | bytes 1769480 | tf_op jit(solution)/shard_map/ppermute | solution.py:16
  24.7 15.5 %collective-permute-start.1 = (f32[256,1152]{1,0:T(8,128)}, f32[256,1152]{1,0:T(8,128)}, u32[]{:S(2)}, u32[]{:S(2)}) collective-permute-start(f32[256,1152]{1,0:T(8,128)} %pad_maximum_fusion.1), channel_id=1, source_target_pairs={{0,1},{1,0},{2,3},{3,2},{4,5},{5,4},{6,7},{7,6},{8,9},{9,8},{10,11... | collective-permute-start | bytes 3538952 | tf_op jit(solution)/shard_map/ppermute | solution.py:16
  29.0 11.2 %collective-permute-start.3 = (f32[128,1152]{1,0:T(8,128)}, f32[128,1152]{1,0:T(8,128)S(1)}, u32[]{:S(2)}, u32[]{:S(2)}) collective-permute-start(f32[128,1152]{1,0:T(8,128)} %get-tuple-element.2), channel_id=1, source_target_pairs={{0,2},{1,3},{2,4},{3,5},{4,6},{5,7},{6,0},{7,1},{8,10},{9,11},{10,... | collective-permute-start | bytes 1769480 | tf_op jit(solution)/shard_map/ppermute | solution.py:16
  31.7 22.4 %collective-permute-start.4 = (f32[128,1152]{1,0:T(8,128)}, f32[128,1152]{1,0:T(8,128)S(1)}, u32[]{:S(2)}, u32[]{:S(2)}) collective-permute-start(f32[128,1152]{1,0:T(8,128)} %get-tuple-element.4), channel_id=1, source_target_pairs={{0,4},{1,5},{2,6},{3,7},{4,0},{5,1},{6,2},{7,3},{8,12},{9,13},{10,... | collective-permute-start | bytes 1769480 | tf_op jit(solution)/shard_map/ppermute | solution.py:16
  34.2 24.7 %collective-permute-start.5 = (f32[128,1152]{1,0:T(8,128)}, f32[128,1152]{1,0:T(8,128)S(1)}, u32[]{:S(2)}, u32[]{:S(2)}) collective-permute-start(f32[128,1152]{1,0:T(8,128)} %get-tuple-element.3), channel_id=1, source_target_pairs={{0,6},{1,7},{2,0},{3,1},{4,2},{5,3},{6,4},{7,5},{8,14},{9,15},{10,... | collective-permute-start | bytes 1769480 | tf_op jit(solution)/shard_map/ppermute | solution.py:16
  44.8 36.7 %collective-permute-start.8 = (f32[128,1152]{1,0:T(8,128)S(1)}, f32[128,1152]{1,0:T(8,128)S(1)}, u32[]{:S(2)}, u32[]{:S(2)}) collective-permute-start(f32[128,1152]{1,0:T(8,128)S(1)} %fusion.36), channel_id=1, source_target_pairs={{0,6},{1,7},{2,0},{3,1},{4,2},{5,3},{6,4},{7,5},{8,14},{9,15},{10,... | collective-permute-start | bytes 1769480 | tf_op jit(solution)/shard_map/ppermute | solution.py:16
  66.5 47.7 %collective-permute-start.6 = (f32[256,1152]{1,0:T(8,128)S(1)}, f32[256,1152]{1,0:T(8,128)S(1)}, u32[]{:S(2)}, u32[]{:S(2)}) collective-permute-start(f32[256,1152]{1,0:T(8,128)S(1)} %slice.17), channel_id=1, source_target_pairs={{0,1},{1,0},{2,3},{3,2},{4,5},{5,4},{6,7},{7,6},{8,9},{9,8},{10,11... | collective-permute-start | bytes 3538952 | tf_op jit(solution)/shard_map/ppermute | solution.py:16
  76.4 16.6 %collective-permute-start.9 = (f32[128,1152]{1,0:T(8,128)S(1)}, f32[128,1152]{1,0:T(8,128)S(1)}, u32[]{:S(2)}, u32[]{:S(2)}) collective-permute-start(f32[128,1152]{1,0:T(8,128)S(1)} %fusion.35), channel_id=1, source_target_pairs={{0,4},{1,5},{2,6},{3,7},{4,0},{5,1},{6,2},{7,3},{8,12},{9,13},{10,... | collective-permute-start | bytes 1769480 | tf_op jit(solution)/shard_map/ppermute | solution.py:16
  81.4 24.5 %collective-permute-start.10 = (f32[128,1152]{1,0:T(8,128)S(1)}, f32[128,1152]{1,0:T(8,128)S(1)}, u32[]{:S(2)}, u32[]{:S(2)}) collective-permute-start(f32[128,1152]{1,0:T(8,128)S(1)} %fusion.34), channel_id=1, source_target_pairs={{0,2},{1,3},{2,4},{3,5},{4,6},{5,7},{6,0},{7,1},{8,10},{9,11},{10,... | collective-permute-start | bytes 1769480 | tf_op jit(solution)/shard_map/ppermute | solution.py:16
  107.8 16.9 %collective-permute-start.11 = (f32[128,1152]{1,0:T(8,128)S(1)}, f32[128,1152]{1,0:T(8,128)S(1)}, u32[]{:S(2)}, u32[]{:S(2)}) collective-permute-start(f32[128,1152]{1,0:T(8,128)S(1)} %get-tuple-element.5), channel_id=1, source_target_pairs={{0,120},{1,249},{2,122},{3,251},{4,124},{5,253},{6,126},{7,255},{8... | collective-permute-start | bytes 1769480 | tf_op jit(solution)/shard_map/ppermute | solution.py:16
  114.4 19.2 %collective-permute-start.7 = (f32[128,1152]{1,0:T(8,128)S(1)}, f32[128,1152]{1,0:T(8,128)S(1)}, u32[]{:S(2)}, u32[]{:S(2)}) collective-permute-start(f32[128,1152]{1,0:T(8,128)S(1)} %slice.19), channel_id=1, source_target_pairs={{0,128},{1,129},{2,130},{3,131},{4,132},{5,133},{6,134},{7,135},{8... | collective-permute-start | bytes 1769480 | tf_op jit(solution)/shard_map/ppermute | solution.py:16
  124.7 8.9 %copy-start.1 = (f32[128,1152]{1,0:T(8,128)S(1)}, f32[128,1152]{1,0:T(8,128)}, u32[]{:S(2)}) copy-start(f32[128,1152]{1,0:T(8,128)} %param.4) | copy-start | bytes 1769476

commit v3 on v2

v3 whole, which is shorter than its diff:
```python
import jax
import jax.numpy as jnp
from jax import lax
from jax.experimental import pallas as pl
from jax.experimental.pallas import tpu as pltpu
from jax.sharding import PartitionSpec as P

GROUPS, BLOCKS, ROW = 2, 128, 8
WEIGHT = 40_000_000


def moved(block, place):
    pairs = []
    for group in range(GROUPS):
        for position in range(BLOCKS):
            to_group, to_position = place(group, position)
            pairs.append((group * BLOCKS + position, to_group * BLOCKS + to_position % BLOCKS))
    return lax.ppermute(block, ("cuts", "blk"), pairs)


def next_row(group, position):
    return (group, position + ROW) if position % 2 == 0 else (1 - group, position + ROW)


def last_row(group, position):
    return (group, position - ROW) if position % 2 == 0 else (1 - group, position - ROW)


def in_row(chips):
    return lambda group, position: (
        group,
        position // ROW * ROW + (position + 2 * chips) % ROW,
    )


def other_core(group, position):
    return group, position ^ 1


def other_group(group, position):
    return 1 - group, position


def together(*values):
    return lax.optimization_barrier(values)


def split(values):
    high = values.astype(jnp.bfloat16)
    return high, (values - high.astype(jnp.float32)).astype(jnp.bfloat16)


def dot3(a, b, b_dim):
    dims = (((1,), (b_dim,)), ((), ()))
    (a_high, a_low), (b_high, b_low) = a, b

    def one(u, v):
        return lax.dot_general(u, v, dims, preferred_element_type=jnp.float32)

    return one(a_high, b_high) + (one(a_low, b_high) + one(a_high, b_low))


def sigmoid(values):
    return 1.0 / (1.0 + jnp.exp(-values))


def normalize_kernel(in_ref, out_ref, inverse_ref, *halves):
    values = in_ref[...]
    inverse = lax.rsqrt(jnp.sum(values * values, axis=-1, keepdims=True) + 1e-06)
    inverse_ref[...] = inverse
    values = values * inverse
    out_ref[...] = values
    for at, half in enumerate(halves):
        half[...] = values[at * half.shape[0] : (at + 1) * half.shape[0], :]


def far_kernel(params, *refs):
    images, (y_1, y_3, y_2) = refs[:6], refs[6:9]
    high_ref, low_ref, grads_ref, *outs = refs[9:]
    rows = y_1.shape[0]
    at = 0
    for image in images:
        high, low = split(image[...])
        high_ref[at : at + image.shape[0], :] = high
        low_ref[at : at + image.shape[0], :] = low
        at += image.shape[0]
    image = (high_ref[...], low_ref[...])
    text = split(jnp.concatenate([y_1[...], y_3[...], y_2[...]], axis=0))
    grads = sigmoid(params[0] * dot3(text, image, 1) + params[1])
    grads_ref[...] = grads
    to_text = dot3(split(grads), image, 0)
    for at, out in enumerate(outs):
        out[...] = to_text[at * rows : (at + 1) * rows, :]


def near_kernel(params, places, *refs):
    (own, last, y_1, y_3, y_2, high_ref, low_ref, far_grads_ref), outs = refs[:8], refs[8:]
    double = high_ref.shape[0] // 2
    far = split(jnp.concatenate([y_1[...], y_3[...], y_2[...]], axis=0))
    for side, mine, other, to_text in ((0, *outs[:3]), (1, *outs[3:])):
        at = side * double
        image = (high_ref[at : at + double, :], low_ref[at : at + double, :])
        text = own[...]
        if side == 1:
            text = jnp.where(places[0] == 1, last[...], text)
        text = split(text)
        logits = params[0] * dot3(text, image, 1) + params[1]
        if side == 0:
            row_ids = lax.broadcasted_iota(jnp.int32, logits.shape, 0)
            col_ids = lax.broadcasted_iota(jnp.int32, logits.shape, 1)
            signs = jnp.where(row_ids == col_ids, -1.0, 1.0)
            grads = signs * sigmoid(signs * logits)
        else:
            grads = sigmoid(logits)
        to_text[...] = dot3(split(grads), image, 0)
        all_grads = jnp.concatenate([far_grads_ref[:, at : at + double], grads], axis=0)
        all_text = tuple(jnp.concatenate(parts, axis=0) for parts in zip(far, text))
        to_image = dot3(split(all_grads.T), all_text, 0)
        mine[...] = to_image[: double // 2, :]
        other[...] = to_image[double // 2 :, :]


def select_kernel(places, own, last, one_ref, three_ref):
    one_ref[...] = jnp.where(places[2] == 1, last[...], own[...])
    three_ref[...] = jnp.where(places[3] == 1, last[...], own[...])


def select_two_kernel(places, two, two_last, out_ref):
    out_ref[...] = jnp.where(places[1] == 1, two_last[...], two[...])


def last_kernel(places, near, back_1, back_3, out_ref):
    total = jnp.where(places[0] == 1, near[...], 0.0)
    total = total + jnp.where(places[2] == 1, back_1[...], 0.0)
    out_ref[...] = total + jnp.where(places[3] == 1, back_3[...], 0.0)


def own_kernel(places, here, near, back_1, back_3, out_ref):
    total = here[...] + jnp.where(places[0] == 1, 0.0, near[...])
    total = total + jnp.where(places[2] == 1, 0.0, back_1[...])
    out_ref[...] = total + jnp.where(places[3] == 1, 0.0, back_3[...])


def add_kernel(here, beside, *halves):
    total = here[...] + beside[...]
    for at, half in enumerate(halves):
        half[...] = total[at * half.shape[0] : (at + 1) * half.shape[0], :]


def finish_kernel(params, rows_ref, inverse_ref, *refs):
    *parts, out_ref = refs
    rows = rows_ref[...]
    count = rows.shape[0]
    halves = [part[...] for part in parts if part.shape[0] < count]
    total = sum(part[...] for part in parts if part.shape[0] == count)
    if halves:
        total = total + jnp.concatenate(halves, axis=0)
    total = params[0] * total
    along = jnp.sum(rows * total, axis=-1, keepdims=True)
    out_ref[...] = inverse_ref[...] * (total - rows * along)


def call(kernel, outs, scalars, *arrays, out_memory=pltpu.VMEM, weight=0):
    vmem = pl.BlockSpec(memory_space=pltpu.VMEM)
    smem = pl.BlockSpec(memory_space=pltpu.SMEM)
    result = pl.BlockSpec(memory_space=out_memory) if out_memory else pl.BlockSpec()
    return pl.pallas_call(
        kernel,
        out_shape=[jax.ShapeDtypeStruct(shape, dtype) for shape, dtype in outs],
        in_specs=[smem] * len(scalars) + [vmem] * len(arrays),
        out_specs=[result] * len(outs),
        compiler_params=pltpu.CompilerParams(vmem_limit_bytes=16 * 2**20),
        cost_estimate=pl.CostEstimate(flops=0, transcendentals=0, bytes_accessed=weight),
    )(*scalars, *arrays)


def normalize(rows_in, halves=0):
    rows, width = rows_in.shape
    outs = [((rows, width), jnp.float32), ((rows, 1), jnp.float32)]
    outs += [((rows // 2, width), jnp.float32)] * halves
    return call(normalize_kernel, outs, (), rows_in)


def finish(params, rows_in, inverse, *parts, weight=0):
    outs = [(rows_in.shape, jnp.float32)]
    arrays = (rows_in, inverse, *parts)
    return call(finish_kernel, outs, (params,), *arrays, out_memory=None, weight=weight)[0]


def local(image_embed, text_embed, log_scale, bias):
    rows, width = image_embed.shape
    f32, bf16 = jnp.float32, jnp.bfloat16
    block = ((rows, width), f32)
    position = lax.axis_index("blk")
    column = position % ROW // 2
    odd = position % 2 == 1
    params = jnp.concatenate([jnp.exp(log_scale), bias])
    places = jnp.stack([odd, column < 2, column >= 3, column >= 1]).astype(jnp.int32)
    half = ((rows // 2, width), f32)

    y_own, y_inv = normalize(text_embed)
    y_last = moved(y_own, next_row)
    x_own, x_inv, x_0, x_1 = normalize(together(image_embed, y_own)[0], 2)
    x_cut_0 = moved(x_0, other_group)
    y_2 = moved(y_own, in_row(2))
    x_beside = moved(x_own, other_core)
    y_last, y_own, x_own, x_1, x_cut_0 = together(y_last, y_own, x_own, x_1, x_cut_0)
    for_1, for_3 = call(select_kernel, [block] * 2, (places,), y_own, y_last, weight=WEIGHT)
    y_2, x_beside, for_1, for_3, x_1 = together(y_2, x_beside, for_1, for_3, x_1)

    y_2_last = moved(y_2, next_row)
    x_cut_1 = moved(x_1, other_group)
    y_1 = moved(for_1, in_row(1))
    y_3 = moved(for_3, in_row(-1))
    x_cut_beside_0 = moved(x_cut_0, other_core)
    y_2_last, x_cut_1 = together(y_2_last, x_cut_1)
    y_2 = call(select_two_kernel, [block], (places,), y_2, y_2_last, weight=WEIGHT)[0]
    y_1, y_3, y_2, x_cut_1, x_cut_beside_0 = together(y_1, y_3, y_2, x_cut_1, x_cut_beside_0)

    x_cut_beside_1 = moved(x_cut_1, other_core)
    images = (x_own, x_cut_0, x_cut_1, x_beside, x_cut_beside_0, x_cut_beside_1)
    outs = [((4 * rows, width), bf16)] * 2 + [((3 * rows, 4 * rows), f32)] + [block] * 3
    far = call(far_kernel, outs, (params,), *images, y_1, y_3, y_2)
    x_high, x_low, g_far, gy_1, gy_3, gy_2 = together(*far)

    gy_2_last = moved(gy_2, last_row)
    back_1 = moved(gy_1, in_row(-1))
    back_3 = moved(gy_3, in_row(1))
    arrays = (y_own, y_last, y_1, y_3, y_2, x_high, x_low, g_far)
    near = call(near_kernel, [block] * 6, (params, places), *arrays)
    gx_own, gx_other, gy_here, gx_near_own, gx_near_other, gy_near = near
    gx_beside_other = moved(gx_near_other, other_core)
    gx_0, gx_1 = call(add_kernel, [half] * 2, (), gx_other, gx_beside_other)
    gx_cut_0 = moved(gx_0, other_group)
    gx_beside_own = moved(gx_near_own, other_core)
    back_1, back_3, gy_2, gy_2_last, gy_near = together(back_1, back_3, gy_2, gy_2_last, gy_near)
    gy_last = call(last_kernel, [block], (places,), gy_near, back_1, back_3, weight=WEIGHT)[0]
    for_2 = call(select_two_kernel, [block], (places,), gy_2, gy_2_last, weight=WEIGHT)[0]
    gy_last, for_2, gx_cut_0, gx_1, gx_beside_own = together(
        gy_last, for_2, gx_cut_0, gx_1, gx_beside_own
    )

    home = moved(gy_last, last_row)
    gx_cut_1 = moved(gx_1, other_group)
    back_2 = moved(for_2, in_row(2))
    gy_own = call(own_kernel, [block], (places,), gy_here, gy_near, back_1, back_3)[0]
    parts = (gx_own, gx_beside_own, gx_cut_0, gx_cut_1)
    image_grad = finish(params, x_own, x_inv, *parts, weight=WEIGHT)
    home, back_2, image_grad = together(home, back_2, image_grad)
    text_grad = finish(params, y_own, y_inv, gy_own, back_2, home)
    return (image_grad, text_grad)


def solution(mesh):
    rows = P(("cuts", "blk"), None)
    return jax.shard_map(
        local, mesh=mesh, in_specs=(rows, rows, P(), P()), out_specs=(rows, rows), check_vma=False
    )
```

time: 135 us -> 104 us (0.77)
  matrix products: 23.7 us -> 0 us
  waiting for transfers between devices: 65.3 us -> 47.4 us
  Pallas kernels: 0 us -> 17.4 us
  other arithmetic: 8.61 us -> 0.15 us
  local copies, waits for them, and re-layouts: 0.13 us -> 2.84 us
    dot_general x15 -> x0, matrix products: 23.7 us -> none  [the longest x5 9.78 us: pair_terms(): logits = scale * jnp.dot(x_rows, y_rows.T, precision=HIGH) + shift]
    ppermute x12 -> x19, waiting for transfers between devices: 65.3 us -> 47.4 us  [moved(): return lax.ppermute(block, ('cuts', 'blk'), pairs)]
    pallas_call x0 -> x12, Pallas kernels: none -> 17.4 us  [call(): pl.pallas_call(kernel, out_shape=[jax.ShapeDtypeStruct(shape, dtype) for...]
    mul x4 -> x0, other arithmetic: 3.27 us -> none  [the longest x2 1.28 us: normalize(): return (rows_in * inverse, inverse)]
    unnamed x4 -> x8, local copies, waits for them, and re-layouts: 0.01 us -> 2.84 us
    reduce_sum x3 -> x0, other arithmetic: 2.66 us -> none  [the longest x2 2.43 us: normalize(): jnp.sum(rows_in * rows_in, axis=-1, keepdims=True) + 1e-06]
    select_n x1 -> x0, other arithmetic: 1.39 us -> none  [local(): jnp.where(last, y_last, y_own)]
    ppermute x12 -> x19, starting transfers between devices: 34.9 us -> 34 us  [moved(): return lax.ppermute(block, ('cuts', 'blk'), pairs)]
  transfers between devices with their start and end apart: 12 -> 19, of which waited for: 8 -> 9; matrix products, arithmetic and copies ran while one was open for 21% -> 0% of each run, Pallas kernels for 0% -> 6%
where the time goes in v3:
time: 104 us
  waiting for transfers between devices  47.4 us (46%)
  starting transfers between devices  34 us (33%)
  Pallas kernels  17.4 us (17%)
  local copies, waits for them, and re-layouts  2.84 us (3%)
  between operations  2.1 us (2%)
    ppermute x19, waiting for transfers between devices, moved(): return lax.ppermute(block, ('cuts', 'blk'), pairs)  47.4 us
    ppermute x19, starting transfers between devices, moved(): return lax.ppermute(block, ('cuts', 'blk'), pairs)  34 us
    pallas_call x12, Pallas kernels, call(): pl.pallas_call(kernel, out_shape=[jax.ShapeDtypeStruct(shape, dtype) for...  17.4 us
    unnamed x8, local copies, waits for them, and re-layouts  2.84 us
  transfers between devices with their start and end apart: 19, of which 9 were waited for; matrix products, arithmetic and copies ran while one was open for 0% of the time, Pallas kernels for 6%

profile of v3, /device:TPU:1, one launch (start us, length us, event | category | flops | bytes accessed | tf_op | source)
XLA Modules:
  0.0 104.0 jit_solution(11510637690192407857)
XLA Ops:
  0.6 0.0 copy-start
  0.6 1.1 %copy-done = f32[128,1152]{1,0:T(8,128)S(1)} copy-done((f32[128,1152]{1,0:T(8,128)S(1)}, f32[128,1152]{1,0:T(8,128)}, u32[]{:S(2)}) %copy-start) | copy-done | bytes 589848
  1.7 0.1 shard_map.59
  1.8 3.6 %collective-permute-start = (f32[128,1152]{1,0:T(8,128)S(1)}, f32[128,1152]{1,0:T(8,128)S(1)}, u32[]{:S(2)}, u32[]{:S(2)}) collective-permute-start(f32[128,1152]{1,0:T(8,128)S(1)} %get-tuple-element.62.own.refs_0_.rows_ref), channel_id=1, source_target_pairs={{0,8},{1,137},{2,10},{3,139},{4,12},{5,141},{6,14},{7,143},{8,16},... | collective-permute-start | bytes 1769480 | tf_op jit(solution)/shard_map/ppermute | solution.py:18
  5.5 0.0 copy-start.1
  5.5 1.1 %copy-done.1 = f32[128,1152]{1,0:T(8,128)S(1)} copy-done((f32[128,1152]{1,0:T(8,128)S(1)}, f32[128,1152]{1,0:T(8,128)}, u32[]{:S(2)}) %copy-start.1) | copy-done | bytes 589848
  6.5 0.8 shard_map.60
  7.4 0.0 copy-start.2
  7.4 0.7 copy-done.2
  8.1 0.0 collective-permute-start.3
  8.1 2.7 %collective-permute-start.2 = (f32[128,1152]{1,0:T(8,128)S(1)}, f32[128,1152]{1,0:T(8,128)S(1)}, u32[]{:S(2)}, u32[]{:S(2)}) collective-permute-start(f32[128,1152]{1,0:T(8,128)S(1)} %get-tuple-element.62.own.refs_0_.rows_ref), channel_id=1, source_target_pairs={{0,4},{1,5},{2,6},{3,7},{4,0},{5,1},{6,2},{7,3},{8,12},{9,13},{10,... | collective-permute-start | bytes 1769480 | tf_op jit(solution)/shard_map/ppermute | solution.py:18
  10.8 2.1 %collective-permute-start.1 = (f32[64,1152]{1,0:T(8,128)}, f32[64,1152]{1,0:T(8,128)S(1)}, u32[]{:S(2)}, u32[]{:S(2)}) collective-permute-start(f32[64,1152]{1,0:T(8,128)} %get-tuple-element.59), channel_id=1, source_target_pairs={{0,128},{1,129},{2,130},{3,131},{4,132},{5,133},{6,134},{7,135},{8... | collective-permute-start | bytes 884744 | tf_op jit(solution)/shard_map/ppermute | solution.py:18
  13.0 0.0 copy-start.3
  13.0 0.1 add_convert_fusion.places
  13.1 11.3 %collective-permute-done.1.refs_1_ = f32[64,1152]{1,0:T(8,128)S(1)} collective-permute-done((f32[64,1152]{1,0:T(8,128)}, f32[64,1152]{1,0:T(8,128)S(1)}, u32[]{:S(2)}, u32[]{:S(2)}) %collective-permute-start.1) | collective-permute-done | bytes 294944 | tf_op jit(solution)/shard_map/ppermute | solution.py:18
  24.3 0.2 collective-permute-done.last.refs_1_
  24.5 0.7 shard_map.61
  25.2 0.0 collective-permute-done.3.refs_3_
  25.2 0.0 collective-permute-done.2.two
  25.2 3.8 %collective-permute-start.6 = (f32[128,1152]{1,0:T(8,128)S(1)}, f32[128,1152]{1,0:T(8,128)S(1)}, u32[]{:S(2)}, u32[]{:S(2)}) collective-permute-start(f32[128,1152]{1,0:T(8,128)S(1)} %collective-permute-done.2.two), channel_id=1, source_target_pairs={{0,8},{1,137},{2,10},{3,139},{4,12},{5,141},{6,14},{7,143},{8,16},... | collective-permute-start | bytes 1769480 | tf_op jit(solution)/shard_map/ppermute | solution.py:18
  29.0 0.8 collective-permute-start.4
  29.8 1.9 %collective-permute-start.5 = (f32[128,1152]{1,0:T(8,128)S(1)}, f32[128,1152]{1,0:T(8,128)S(1)}, u32[]{:S(2)}, u32[]{:S(2)}) collective-permute-start(f32[128,1152]{1,0:T(8,128)S(1)} %get-tuple-element.68), channel_id=1, source_target_pairs={{0,6},{1,7},{2,0},{3,1},{4,2},{5,3},{6,4},{7,5},{8,14},{9,15},{10,... | collective-permute-start | bytes 1769480 | tf_op jit(solution)/shard_map/ppermute | solution.py:18
  31.7 0.0 copy-done.3
  31.7 0.5 collective-permute-start.7
  32.2 2.5 %collective-permute-start.8 = (f32[64,1152]{1,0:T(8,128)S(1)}, f32[64,1152]{1,0:T(8,128)S(1)}, u32[]{:S(2)}, u32[]{:S(2)}) collective-permute-start(f32[64,1152]{1,0:T(8,128)S(1)} %collective-permute-done.1.refs_1_), channel_id=1, source_target_pairs={{0,1},{1,0},{2,3},{3,2},{4,5},{5,4},{6,7},{7,6},{8,9},{9,8},{10,11... | collective-permute-start | bytes 884744 | tf_op jit(solution)/shard_map/ppermute | solution.py:18
  34.7 7.6 %collective-permute-done.7.refs_2_ = f32[64,1152]{1,0:T(8,128)S(1)} collective-permute-done((f32[64,1152]{1,0:T(8,128)S(1)}, f32[64,1152]{1,0:T(8,128)S(1)}, u32[]{:S(2)}, u32[]{:S(2)}) %collective-permute-start.7) | collective-permute-done | bytes 294944 | tf_op jit(solution)/shard_map/ppermute | solution.py:18
  42.3 2.5 %collective-permute-done.6.two_last = f32[128,1152]{1,0:T(8,128)S(1)} collective-permute-done((f32[128,1152]{1,0:T(8,128)S(1)}, f32[128,1152]{1,0:T(8,128)S(1)}, u32[]{:S(2)}, u32[]{:S(2)}) %collective-permute-start.6) | collective-permute-done | bytes 589856 | tf_op jit(solution)/shard_map/ppermute | solution.py:18
  44.7 0.6 shard_map.62.refs_8_.refs_4_
  45.3 0.0 collective-permute-done.8.refs_4_
  45.4 0.0 collective-permute-done.4.refs_6_.refs_2_
  45.4 0.0 collective-permute-done.5.refs_7_.refs_3_
  45.4 2.4 %collective-permute-start.9 = (f32[64,1152]{1,0:T(8,128)S(1)}, f32[64,1152]{1,0:T(8,128)S(1)}, u32[]{:S(2)}, u32[]{:S(2)}) collective-permute-start(f32[64,1152]{1,0:T(8,128)S(1)} %collective-permute-done.7.refs_2_), channel_id=1, source_target_pairs={{0,1},{1,0},{2,3},{3,2},{4,5},{5,4},{6,7},{7,6},{8,9},{9,8},{10,11... | collective-permute-start | bytes 884744 | tf_op jit(solution)/shard_map/ppermute | solution.py:18
  49.1 0.1 pad_maximum_fusion.params
  49.2 0.0 collective-permute-done.9.refs_5_
  49.2 4.5 %shard_map.63 = (bf16[512,1152]{1,0:T(8,128)(2,1)S(1)}, bf16[512,1152]{1,0:T(8,128)(2,1)S(1)}, f32[384,512]{1,0:T(8,128)S(1)}, f32[128,1152]{1,0:T(8,128)S(1)}, ...) custom-call(f32[2]{0:T(128)S(1)} %pad_maximum_fusion.params, f32[128,1152]{1,0:T(8,128)S(1)} %get-tuple-element.60.refs_0_.rows_ref, ...), custom_call_target="tpu_custom_call" | custom-call | tf_op jit(solution)/shard_map/pallas_call | solution.py:167
  53.6 5.3 %shard_map.64 = (f32[128,1152]{1,0:T(8,128)S(1)}, f32[128,1152]{1,0:T(8,128)S(1)}, f32[128,1152]{1,0:T(8,128)S(1)}, f32[128,1152]{1,0:T(8,128)S(1)}, f32[128,1152]{1,0:T(8,128)S(1)}, /*index=5*/f32[128,1152]{1,0:T(8,128)S(1)}) custom-call(f32[2]{0:T(128)S(1)} %pad_maximum_fusion.params, s32[4]{0:T(128)S(1)} %add_convert_fusion.places, ...), custom_call_target="tpu_custom_call" | custom-call | tf_op jit(solution)/shard_map/pallas_call | solution.py:167
  59.0 0.2 collective-permute-start.13
  59.2 1.6 %collective-permute-start.10 = (f32[128,1152]{1,0:T(8,128)S(1)}, f32[128,1152]{1,0:T(8,128)S(1)}, u32[]{:S(2)}, u32[]{:S(2)}) collective-permute-start(f32[128,1152]{1,0:T(8,128)S(1)} %get-tuple-element.79), channel_id=1, source_target_pairs={{0,6},{1,7},{2,0},{3,1},{4,2},{5,3},{6,4},{7,5},{8,14},{9,15},{10,... | collective-permute-start | bytes 1769480 | tf_op jit(solution)/shard_map/ppermute | solution.py:18
  60.8 0.0 collective-permute-start.11
  60.8 3.8 %collective-permute-start.12 = (f32[128,1152]{1,0:T(8,128)S(1)}, f32[128,1152]{1,0:T(8,128)S(1)}, u32[]{:S(2)}, u32[]{:S(2)}) collective-permute-start(f32[128,1152]{1,0:T(8,128)S(1)} %get-tuple-element.89.two), channel_id=1, source_target_pairs={{0,120},{1,249},{2,122},{3,251},{4,124},{5,253},{6,126},{7,255},{8... | collective-permute-start | bytes 1769480 | tf_op jit(solution)/shard_map/ppermute | solution.py:18
  64.6 0.4 collective-permute-start.15
  65.0 0.0 collective-permute-done.13.beside
  65.0 0.1 shard_map.67
  65.1 2.0 %collective-permute-start.14 = (f32[64,1152]{1,0:T(8,128)S(1)}, f32[64,1152]{1,0:T(8,128)S(1)}, u32[]{:S(2)}, u32[]{:S(2)}) collective-permute-start(f32[64,1152]{1,0:T(8,128)S(1)} %get-tuple-element.93), channel_id=1, source_target_pairs={{0,128},{1,129},{2,130},{3,131},{4,132},{5,133},{6,134},{7,135},{8... | collective-permute-start | bytes 884744 | tf_op jit(solution)/shard_map/ppermute | solution.py:18
  67.1 6.7 %collective-permute-done.10.back_1 = f32[128,1152]{1,0:T(8,128)S(1)} collective-permute-done((f32[128,1152]{1,0:T(8,128)S(1)}, f32[128,1152]{1,0:T(8,128)S(1)}, u32[]{:S(2)}, u32[]{:S(2)}) %collective-permute-start.10) | collective-permute-done | bytes 589856 | tf_op jit(solution)/shard_map/ppermute | solution.py:18
  73.8 2.5 %collective-permute-done.11.back_3 = f32[128,1152]{1,0:T(8,128)S(1)} collective-permute-done((f32[128,1152]{1,0:T(8,128)S(1)}, f32[128,1152]{1,0:T(8,128)S(1)}, u32[]{:S(2)}, u32[]{:S(2)}) %collective-permute-start.11) | collective-permute-done | bytes 589856 | tf_op jit(solution)/shard_map/ppermute | solution.py:18
  76.3 0.9 collective-permute-done.12.two_last
  77.2 0.6 shard_map.66
  77.8 0.7 shard_map.65
  78.5 0.0 collective-permute-done.15.refs_1_
  78.5 2.2 %collective-permute-done.14.refs_2_ = f32[64,1152]{1,0:T(8,128)S(1)} collective-permute-done((f32[64,1152]{1,0:T(8,128)S(1)}, f32[64,1152]{1,0:T(8,128)S(1)}, u32[]{:S(2)}, u32[]{:S(2)}) %collective-permute-start.14) | collective-permute-done | bytes 294944 | tf_op jit(solution)/shard_map/ppermute | solution.py:18
  80.7 4.0 %collective-permute-start.16 = (f32[128,1152]{1,0:T(8,128)S(1)}, f32[128,1152]{1,0:T(8,128)S(1)}, u32[]{:S(2)}, u32[]{:S(2)}) collective-permute-start(f32[128,1152]{1,0:T(8,128)S(1)} %shard_map.65), channel_id=1, source_target_pairs={{0,120},{1,249},{2,122},{3,251},{4,124},{5,253},{6,126},{7,255},{8... | collective-permute-start | bytes 1769480 | tf_op jit(solution)/shard_map/ppermute | solution.py:18
  84.7 1.6 %collective-permute-start.17 = (f32[128,1152]{1,0:T(8,128)S(1)}, f32[128,1152]{1,0:T(8,128)S(1)}, u32[]{:S(2)}, u32[]{:S(2)}) collective-permute-start(f32[128,1152]{1,0:T(8,128)S(1)} %shard_map.66), channel_id=1, source_target_pairs={{0,4},{1,5},{2,6},{3,7},{4,0},{5,1},{6,2},{7,3},{8,12},{9,13},{10,... | collective-permute-start | bytes 1769480 | tf_op jit(solution)/shard_map/ppermute | solution.py:18
  86.3 0.0 collective-permute-start.18
  86.3 0.7 shard_map.69.refs_0_
  87.0 13.7 %collective-permute-done.18.refs_3_ = f32[64,1152]{1,0:T(8,128)S(1)} collective-permute-done((f32[64,1152]{1,0:T(8,128)S(1)}, f32[64,1152]{1,0:T(8,128)S(1)}, u32[]{:S(2)}, u32[]{:S(2)}) %collective-permute-start.18) | collective-permute-done | bytes 294944 | tf_op jit(solution)/shard_map/ppermute | solution.py:18
  100.7 1.6 %shard_map.68 = f32[128,1152]{1,0:T(8,128)} custom-call(f32[2]{0:T(128)S(1)} %pad_maximum_fusion.params, f32[128,1152]{1,0:T(8,128)S(1)} %get-tuple-element.60.refs_0_.rows_ref, f32[128,1]{1,0:T(8,128)S(1)} %get-tuple-element.98.inverse_ref, f32[128,1152]{1,0:T(8,128)S(1)} %get-tuple-element.99.refs_0_, f32[128,1152]{1,0:T(8,128)S(1)} %collective-permute-done.15.refs_1_, ...), custom_call_target="tpu_custom_call" | custom-call | bytes 40000000 | tf_op jit(solution)/shard_map/pallas_call | solution.py:167
  102.3 0.0 collective-permute-done.16.refs_2_
  102.3 0.0 collective-permute-done.17.refs_1_
  102.3 1.6 %shard_map.70 = f32[128,1152]{1,0:T(8,128)} custom-call(f32[2]{0:T(128)S(1)} %pad_maximum_fusion.params, f32[128,1152]{1,0:T(8,128)S(1)} %get-tuple-element.62.own.refs_0_.rows_ref, f32[128,1]{1,0:T(8,128)S(1)} %get-tuple-element.104.inverse_ref, f32[128,1152]{1,0:T(8,128)S(1)} %shard_map.69.refs_0_, f32[128,1152]{1,0:T(8,128)S(1)} %collective-permute-done.17.refs_1_, ...), custom_call_target="tpu_custom_call" | custom-call | tf_op jit(solution)/shard_map/pallas_call | solution.py:167
Async XLA Ops:
  0.6 1.1 %copy-start = (f32[128,1152]{1,0:T(8,128)S(1)}, f32[128,1152]{1,0:T(8,128)}, u32[]{:S(2)}) copy-start(f32[128,1152]{1,0:T(8,128)} %in_ref.1) | copy-start | bytes 1769476
  1.8 22.7 %collective-permute-start = (f32[128,1152]{1,0:T(8,128)S(1)}, f32[128,1152]{1,0:T(8,128)S(1)}, u32[]{:S(2)}, u32[]{:S(2)}) collective-permute-start(f32[128,1152]{1,0:T(8,128)S(1)} %get-tuple-element.62.own.refs_0_.rows_ref), channel_id=1, source_target_pairs={{0,8},{1,137},{2,10},{3,139},{4,12},{5,141},{6,14},{7,143},{8,16},... | collective-permute-start | bytes 1769480 | tf_op jit(solution)/shard_map/ppermute | solution.py:18
  5.5 1.1 %copy-start.1 = (f32[128,1152]{1,0:T(8,128)S(1)}, f32[128,1152]{1,0:T(8,128)}, u32[]{:S(2)}) copy-start(f32[128,1152]{1,0:T(8,128)} %in_ref.2) | copy-start | bytes 1769476
  7.4 0.7 copy-start.2
  8.1 17.1 %collective-permute-start.3 = (f32[128,1152]{1,0:T(8,128)S(1)}, f32[128,1152]{1,0:T(8,128)S(1)}, u32[]{:S(2)}, u32[]{:S(2)}) collective-permute-start(f32[128,1152]{1,0:T(8,128)S(1)} %get-tuple-element.60.refs_0_.rows_ref), channel_id=1, source_target_pairs={{0,1},{1,0},{2,3},{3,2},{4,5},{5,4},{6,7},{7,6},{8,9},{9,8},{10,11... | collective-permute-start | bytes 1769480 | tf_op jit(solution)/shard_map/ppermute | solution.py:18
  8.1 17.1 %collective-permute-start.2 = (f32[128,1152]{1,0:T(8,128)S(1)}, f32[128,1152]{1,0:T(8,128)S(1)}, u32[]{:S(2)}, u32[]{:S(2)}) collective-permute-start(f32[128,1152]{1,0:T(8,128)S(1)} %get-tuple-element.62.own.refs_0_.rows_ref), channel_id=1, source_target_pairs={{0,4},{1,5},{2,6},{3,7},{4,0},{5,1},{6,2},{7,3},{8,12},{9,13},{10,... | collective-permute-start | bytes 1769480 | tf_op jit(solution)/shard_map/ppermute | solution.py:18
  10.8 13.5 %collective-permute-start.1 = (f32[64,1152]{1,0:T(8,128)}, f32[64,1152]{1,0:T(8,128)S(1)}, u32[]{:S(2)}, u32[]{:S(2)}) collective-permute-start(f32[64,1152]{1,0:T(8,128)} %get-tuple-element.59), channel_id=1, source_target_pairs={{0,128},{1,129},{2,130},{3,131},{4,132},{5,133},{6,134},{7,135},{8... | collective-permute-start | bytes 884744 | tf_op jit(solution)/shard_map/ppermute | solution.py:18
  13.0 18.7 %copy-start.3 = (f32[64,1152]{1,0:T(8,128)S(1)}, f32[64,1152]{1,0:T(8,128)}, u32[]{:S(2)}) copy-start(f32[64,1152]{1,0:T(8,128)} %copy-done.2) | copy-start | bytes 884740
  25.2 19.5 %collective-permute-start.6 = (f32[128,1152]{1,0:T(8,128)S(1)}, f32[128,1152]{1,0:T(8,128)S(1)}, u32[]{:S(2)}, u32[]{:S(2)}) collective-permute-start(f32[128,1152]{1,0:T(8,128)S(1)} %collective-permute-done.2.two), channel_id=1, source_target_pairs={{0,8},{1,137},{2,10},{3,139},{4,12},{5,141},{6,14},{7,143},{8,16},... | collective-permute-start | bytes 1769480 | tf_op jit(solution)/shard_map/ppermute | solution.py:18
  29.0 16.4 %collective-permute-start.4 = (f32[128,1152]{1,0:T(8,128)S(1)}, f32[128,1152]{1,0:T(8,128)S(1)}, u32[]{:S(2)}, u32[]{:S(2)}) collective-permute-start(f32[128,1152]{1,0:T(8,128)S(1)} %get-tuple-element.67), channel_id=1, source_target_pairs={{0,2},{1,3},{2,4},{3,5},{4,6},{5,7},{6,0},{7,1},{8,10},{9,11},{10,... | collective-permute-start | bytes 1769480 | tf_op jit(solution)/shard_map/ppermute | solution.py:18
  29.8 15.6 %collective-permute-start.5 = (f32[128,1152]{1,0:T(8,128)S(1)}, f32[128,1152]{1,0:T(8,128)S(1)}, u32[]{:S(2)}, u32[]{:S(2)}) collective-permute-start(f32[128,1152]{1,0:T(8,128)S(1)} %get-tuple-element.68), channel_id=1, source_target_pairs={{0,6},{1,7},{2,0},{3,1},{4,2},{5,3},{6,4},{7,5},{8,14},{9,15},{10,... | collective-permute-start | bytes 1769480 | tf_op jit(solution)/shard_map/ppermute | solution.py:18
  31.7 10.6 %collective-permute-start.7 = (f32[64,1152]{1,0:T(8,128)S(1)}, f32[64,1152]{1,0:T(8,128)S(1)}, u32[]{:S(2)}, u32[]{:S(2)}) collective-permute-start(f32[64,1152]{1,0:T(8,128)S(1)} %copy-done.3), channel_id=1, source_target_pairs={{0,128},{1,129},{2,130},{3,131},{4,132},{5,133},{6,134},{7,135},{8... | collective-permute-start | bytes 884744 | tf_op jit(solution)/shard_map/ppermute | solution.py:18
  32.2 13.2 %collective-permute-start.8 = (f32[64,1152]{1,0:T(8,128)S(1)}, f32[64,1152]{1,0:T(8,128)S(1)}, u32[]{:S(2)}, u32[]{:S(2)}) collective-permute-start(f32[64,1152]{1,0:T(8,128)S(1)} %collective-permute-done.1.refs_1_), channel_id=1, source_target_pairs={{0,1},{1,0},{2,3},{3,2},{4,5},{5,4},{6,7},{7,6},{8,9},{9,8},{10,11... | collective-permute-start | bytes 884744 | tf_op jit(solution)/shard_map/ppermute | solution.py:18
  45.4 3.8 %collective-permute-start.9 = (f32[64,1152]{1,0:T(8,128)S(1)}, f32[64,1152]{1,0:T(8,128)S(1)}, u32[]{:S(2)}, u32[]{:S(2)}) collective-permute-start(f32[64,1152]{1,0:T(8,128)S(1)} %collective-permute-done.7.refs_2_), channel_id=1, source_target_pairs={{0,1},{1,0},{2,3},{3,2},{4,5},{5,4},{6,7},{7,6},{8,9},{9,8},{10,11... | collective-permute-start | bytes 884744 | tf_op jit(solution)/shard_map/ppermute | solution.py:18
  59.0 6.0 %collective-permute-start.13 = (f32[128,1152]{1,0:T(8,128)S(1)}, f32[128,1152]{1,0:T(8,128)S(1)}, u32[]{:S(2)}, u32[]{:S(2)}) collective-permute-start(f32[128,1152]{1,0:T(8,128)S(1)} %get-tuple-element.92), channel_id=1, source_target_pairs={{0,1},{1,0},{2,3},{3,2},{4,5},{5,4},{6,7},{7,6},{8,9},{9,8},{10,11... | collective-permute-start | bytes 1769480 | tf_op jit(solution)/shard_map/ppermute | solution.py:18
  59.2 14.6 %collective-permute-start.10 = (f32[128,1152]{1,0:T(8,128)S(1)}, f32[128,1152]{1,0:T(8,128)S(1)}, u32[]{:S(2)}, u32[]{:S(2)}) collective-permute-start(f32[128,1152]{1,0:T(8,128)S(1)} %get-tuple-element.79), channel_id=1, source_target_pairs={{0,6},{1,7},{2,0},{3,1},{4,2},{5,3},{6,4},{7,5},{8,14},{9,15},{10,... | collective-permute-start | bytes 1769480 | tf_op jit(solution)/shard_map/ppermute | solution.py:18
  60.8 15.5 %collective-permute-start.11 = (f32[128,1152]{1,0:T(8,128)S(1)}, f32[128,1152]{1,0:T(8,128)S(1)}, u32[]{:S(2)}, u32[]{:S(2)}) collective-permute-start(f32[128,1152]{1,0:T(8,128)S(1)} %get-tuple-element.80), channel_id=1, source_target_pairs={{0,2},{1,3},{2,4},{3,5},{4,6},{5,7},{6,0},{7,1},{8,10},{9,11},{10,... | collective-permute-start | bytes 1769480 | tf_op jit(solution)/shard_map/ppermute | solution.py:18
  60.8 16.3 %collective-permute-start.12 = (f32[128,1152]{1,0:T(8,128)S(1)}, f32[128,1152]{1,0:T(8,128)S(1)}, u32[]{:S(2)}, u32[]{:S(2)}) collective-permute-start(f32[128,1152]{1,0:T(8,128)S(1)} %get-tuple-element.89.two), channel_id=1, source_target_pairs={{0,120},{1,249},{2,122},{3,251},{4,124},{5,253},{6,126},{7,255},{8... | collective-permute-start | bytes 1769480 | tf_op jit(solution)/shard_map/ppermute | solution.py:18
  64.6 13.9 %collective-permute-start.15 = (f32[128,1152]{1,0:T(8,128)S(1)}, f32[128,1152]{1,0:T(8,128)S(1)}, u32[]{:S(2)}, u32[]{:S(2)}) collective-permute-start(f32[128,1152]{1,0:T(8,128)S(1)} %get-tuple-element.95), channel_id=1, source_target_pairs={{0,1},{1,0},{2,3},{3,2},{4,5},{5,4},{6,7},{7,6},{8,9},{9,8},{10,11... | collective-permute-start | bytes 1769480 | tf_op jit(solution)/shard_map/ppermute | solution.py:18
  65.1 15.6 %collective-permute-start.14 = (f32[64,1152]{1,0:T(8,128)S(1)}, f32[64,1152]{1,0:T(8,128)S(1)}, u32[]{:S(2)}, u32[]{:S(2)}) collective-permute-start(f32[64,1152]{1,0:T(8,128)S(1)} %get-tuple-element.93), channel_id=1, source_target_pairs={{0,128},{1,129},{2,130},{3,131},{4,132},{5,133},{6,134},{7,135},{8... | collective-permute-start | bytes 884744 | tf_op jit(solution)/shard_map/ppermute | solution.py:18
  80.7 21.6 %collective-permute-start.16 = (f32[128,1152]{1,0:T(8,128)S(1)}, f32[128,1152]{1,0:T(8,128)S(1)}, u32[]{:S(2)}, u32[]{:S(2)}) collective-permute-start(f32[128,1152]{1,0:T(8,128)S(1)} %shard_map.65), channel_id=1, source_target_pairs={{0,120},{1,249},{2,122},{3,251},{4,124},{5,253},{6,126},{7,255},{8... | collective-permute-start | bytes 1769480 | tf_op jit(solution)/shard_map/ppermute | solution.py:18
  84.7 17.6 %collective-permute-start.17 = (f32[128,1152]{1,0:T(8,128)S(1)}, f32[128,1152]{1,0:T(8,128)S(1)}, u32[]{:S(2)}, u32[]{:S(2)}) collective-permute-start(f32[128,1152]{1,0:T(8,128)S(1)} %shard_map.66), channel_id=1, source_target_pairs={{0,4},{1,5},{2,6},{3,7},{4,0},{5,1},{6,2},{7,3},{8,12},{9,13},{10,... | collective-permute-start | bytes 1769480 | tf_op jit(solution)/shard_map/ppermute | solution.py:18
  86.3 14.4 %collective-permute-start.18 = (f32[64,1152]{1,0:T(8,128)S(1)}, f32[64,1152]{1,0:T(8,128)S(1)}, u32[]{:S(2)}, u32[]{:S(2)}) collective-permute-start(f32[64,1152]{1,0:T(8,128)S(1)} %get-tuple-element.102), channel_id=1, source_target_pairs={{0,128},{1,129},{2,130},{3,131},{4,132},{5,133},{6,134},{7,135},{8... | collective-permute-start | bytes 884744 | tf_op jit(solution)/shard_map/ppermute | solution.py:18

commit v4 on v3

v4 whole, which is shorter than its diff:
```python
import jax
import jax.numpy as jnp
from jax import lax
from jax.experimental import pallas as pl
from jax.experimental.pallas import tpu as pltpu
from jax.sharding import PartitionSpec as P

GROUPS, BLOCKS, ROW = 2, 128, 8
CHUNKS = 4
W_ONE = 0
W_HOP = 300_000_000
W_LAST = 0
W_BACK = 0
W_ADD = 500_000_000
W_END = 200_000_000


def moved(block, place):
    pairs = []
    for group in range(GROUPS):
        for position in range(BLOCKS):
            to_group, to_position = place(group, position)
            pairs.append((group * BLOCKS + position, to_group * BLOCKS + to_position % BLOCKS))
    return lax.ppermute(block, ("cuts", "blk"), pairs)


def next_row(group, position):
    return (group, position + ROW) if position % 2 == 0 else (1 - group, position + ROW)


def last_row(group, position):
    return (group, position - ROW) if position % 2 == 0 else (1 - group, position - ROW)


def in_row(chips):
    return lambda group, position: (
        group,
        position // ROW * ROW + (position + 2 * chips) % ROW,
    )


def other_core(group, position):
    return group, position ^ 1


def other_group(group, position):
    return 1 - group, position


def together(*values):
    return lax.optimization_barrier(values)


def split(values):
    high = values.astype(jnp.bfloat16)
    return high, (values - high.astype(jnp.float32)).astype(jnp.bfloat16)


def dot3(a, b, b_dim):
    dims = (((1,), (b_dim,)), ((), ()))
    (a_high, a_low), (b_high, b_low) = a, b

    def one(u, v):
        return lax.dot_general(u, v, dims, preferred_element_type=jnp.float32)

    return one(a_high, b_high) + (one(a_low, b_high) + one(a_high, b_low))


def sigmoid(values):
    return 1.0 / (1.0 + jnp.exp(-values))


def normalize_kernel(in_ref, inverse_ref, *outs):
    values = in_ref[...]
    inverse = lax.rsqrt(jnp.sum(values * values, axis=-1, keepdims=True) + 1e-06)
    inverse_ref[...] = inverse
    values = values * inverse
    for at, out in enumerate(outs):
        out[...] = values[at * out.shape[0] : (at + 1) * out.shape[0], :]


def split_kernel(*refs):
    *images, high_ref, low_ref = refs
    at = 0
    for image in images:
        high, low = split(image[...])
        high_ref[at : at + image.shape[0], :] = high
        low_ref[at : at + image.shape[0], :] = low
        at += image.shape[0]


def join_kernel(first_high, first_low, *refs):
    *images, high_ref, low_ref = refs
    at = first_high.shape[0]
    high_ref[:at, :] = first_high[...]
    low_ref[:at, :] = first_low[...]
    for image in images:
        high, low = split(image[...])
        high_ref[at : at + image.shape[0], :] = high
        low_ref[at : at + image.shape[0], :] = low
        at += image.shape[0]


def far_kernel(params, *refs):
    count = (len(refs) - 3) // 2
    texts, (high_ref, low_ref, grads_ref), outs = refs[:count], refs[count:-count], refs[-count:]
    rows = texts[0].shape[0]
    image = (high_ref[...], low_ref[...])
    text = split(jnp.concatenate([ref[...] for ref in texts], axis=0))
    grads = sigmoid(params[0] * dot3(text, image, 1) + params[1])
    grads_ref[...] = grads
    to_text = dot3(split(grads), image, 0)
    for at, out in enumerate(outs):
        out[...] = to_text[at * rows : (at + 1) * rows, :]


def near_kernel(first, params, places, *refs):
    (own, last, high_ref, low_ref), outs = refs[:4], refs[4:]
    rows = own.shape[0]
    for side, grads_ref, to_text in ((0, *outs[:2]), (1, *outs[2:])):
        span = pl.ds(first + side * rows, rows)
        image = (high_ref[span, :], low_ref[span, :])
        text = own[...]
        if side == 1:
            text = jnp.where(places[0] == 1, last[...], text)
        logits = params[0] * dot3(split(text), image, 1) + params[1]
        if side == 0 and first == 0:
            row_ids = lax.broadcasted_iota(jnp.int32, logits.shape, 0)
            col_ids = lax.broadcasted_iota(jnp.int32, logits.shape, 1)
            signs = jnp.where(row_ids == col_ids, -1.0, 1.0)
            grads = signs * sigmoid(signs * logits)
        else:
            grads = sigmoid(logits)
        grads_ref[...] = grads
        to_text[...] = dot3(split(grads), image, 0)


def image_kernel(first, places, own, last, y_1, y_3, y_2, g_here, g_near, g_13, g_2, *outs):
    rows = own.shape[0]
    far = [y_1[...], y_3[...], y_2[...]]
    here = own[...]
    near = jnp.where(places[0] == 1, last[...], here)
    for side, text, mine in ((0, here, g_here), (1, near, g_near)):
        columns = pl.ds(first + side * rows, rows)
        grads = [g_13[:, columns], g_2[:, columns], mine[...]]
        grads = split(jnp.concatenate(grads, axis=0).T)
        to_image = dot3(grads, split(jnp.concatenate([*far, text], axis=0)), 0)
        mine_outs = outs[side * len(outs) // 2 : (side + 1) * len(outs) // 2]
        for at, out in enumerate(mine_outs):
            out[...] = to_image[at * out.shape[0] : (at + 1) * out.shape[0], :]


def select_kernel(places, own, last, one_ref, three_ref):
    one_ref[...] = jnp.where(places[2] == 1, last[...], own[...])
    three_ref[...] = jnp.where(places[3] == 1, last[...], own[...])


def select_two_kernel(places, two, two_last, out_ref):
    out_ref[...] = jnp.where(places[1] == 1, two_last[...], two[...])


def last_kernel(places, near_a, near_b, back_1, back_3, out_ref):
    total = jnp.where(places[0] == 1, near_a[...] + near_b[...], 0.0)
    total = total + jnp.where(places[2] == 1, back_1[...], 0.0)
    out_ref[...] = total + jnp.where(places[3] == 1, back_3[...], 0.0)


def own_kernel(places, here_a, here_b, near_a, near_b, back_1, back_3, out_ref):
    total = here_a[...] + here_b[...]
    total = total + jnp.where(places[0] == 1, 0.0, near_a[...] + near_b[...])
    total = total + jnp.where(places[2] == 1, 0.0, back_1[...])
    out_ref[...] = total + jnp.where(places[3] == 1, 0.0, back_3[...])


def add_kernel(here, beside, out_ref):
    out_ref[...] = here[...] + beside[...]


def finish_kernel(params, rows_parts, inverse_ref, *refs):
    *parts, out_ref, held, left = refs
    count = held.shape[0]
    rows = count // CHUNKS
    copies = []

    def chunk(refs, at):
        size = refs[0].shape[0]
        return refs[at * rows // size][pl.ds(at * rows % size, rows), :]

    for at in range(CHUNKS):
        span = pl.ds(at * rows, rows)
        normal = chunk(rows_parts, at)
        total = params[0] * sum(chunk(part, at) for part in parts)
        along = jnp.sum(normal * total, axis=-1, keepdims=True)
        held[span, :] = inverse_ref[span, :] * (total - normal * along)
        copies.append(
            pltpu.make_async_copy(held.at[span, :], out_ref.at[span, :], left.at[at])
        )
        copies[-1].start()
    for copy in copies:
        copy.wait()


def call(kernel, outs, scalars, *arrays, weight=0):
    vmem = pl.BlockSpec(memory_space=pltpu.VMEM)
    smem = pl.BlockSpec(memory_space=pltpu.SMEM)
    return pl.pallas_call(
        kernel,
        out_shape=[jax.ShapeDtypeStruct(shape, dtype) for shape, dtype in outs],
        in_specs=[smem] * len(scalars) + [vmem] * len(arrays),
        out_specs=[vmem] * len(outs),
        compiler_params=pltpu.CompilerParams(vmem_limit_bytes=16 * 2**20),
        cost_estimate=pl.CostEstimate(flops=weight, transcendentals=0, bytes_accessed=0),
    )(*scalars, *arrays)


def normalize(rows_in, parts):
    rows, width = rows_in.shape
    outs = [((rows, 1), jnp.float32)] + [((rows // parts, width), jnp.float32)] * parts
    return call(normalize_kernel, outs, (), rows_in)


def finish(params, rows_in, inverse, *parts, weight=0):
    groups = [part if isinstance(part, tuple) else (part,) for part in (rows_in, *parts)]
    shape = (inverse.shape[0], groups[0][0].shape[1])
    vmem = pl.BlockSpec(memory_space=pltpu.VMEM)
    arrays = [array for group in groups for array in group]

    def kernel(params_ref, inverse_ref, *refs):
        refs = list(refs)
        taken = [tuple(refs.pop(0) for _ in group) for group in groups]
        finish_kernel(params_ref, taken[0], inverse_ref, *taken[1:], *refs)

    return pl.pallas_call(
        kernel,
        out_shape=jax.ShapeDtypeStruct(shape, jnp.float32),
        in_specs=[pl.BlockSpec(memory_space=pltpu.SMEM)] + [vmem] * (1 + len(arrays)),
        out_specs=pl.BlockSpec(memory_space=pltpu.HBM),
        scratch_shapes=[pltpu.VMEM(shape, jnp.float32), pltpu.SemaphoreType.DMA((CHUNKS,))],
        compiler_params=pltpu.CompilerParams(vmem_limit_bytes=16 * 2**20),
        cost_estimate=pl.CostEstimate(flops=weight, transcendentals=0, bytes_accessed=0),
    )(params, inverse, *arrays)


def local(image_embed, text_embed, log_scale, bias):
    rows, width = image_embed.shape
    f32, bf16 = jnp.float32, jnp.bfloat16
    block = ((rows, width), f32)
    position = lax.axis_index("blk")
    column = position % ROW // 2
    odd = position % 2 == 1
    params = jnp.concatenate([jnp.exp(log_scale), bias])
    places = jnp.stack([odd, column < 2, column >= 3, column >= 1]).astype(jnp.int32)
    half = ((rows // 2, width), f32)

    square = ((rows, rows), f32)
    pair = ((2 * rows, width), bf16)

    y_inv, y_own = normalize(text_embed, 1)
    y_last = moved(y_own, next_row)
    y_2 = moved(y_own, in_row(2))
    x_inv, x_0, x_1 = normalize(together(image_embed, y_own)[0], 2)
    x_cut_0 = moved(x_0, other_group)
    x_beside_0 = moved(x_0, other_core)
    x_beside_1 = moved(x_1, other_core)
    y_2_last = moved(y_2, next_row)
    y_last, y_own, y_2, x_0, x_1, x_beside_0, x_beside_1, x_cut_0 = together(
        y_last, y_own, y_2, x_0, x_1, x_beside_0, x_beside_1, x_cut_0
    )
    for_1, for_3 = call(select_kernel, [block] * 2, (places,), y_own, y_last, weight=W_ONE)
    y_1 = moved(for_1, in_row(1))
    y_3 = moved(for_3, in_row(-1))
    x_cut_0, x_1, y_own, _ = together(x_cut_0, x_1, y_own, for_1)
    x_cut_1 = moved(x_1, other_group)
    x_cut_beside_0 = moved(x_cut_0, other_core)
    xa_high, xa_low = call(split_kernel, [pair] * 2, (), x_0, x_1, x_beside_0, x_beside_1)
    arrays = (y_own, y_last, xa_high, xa_low)
    kernel = lambda *refs: near_kernel(0, *refs)
    near = call(kernel, [square, block] * 2, (params, places), *arrays)
    ga_here, gya_here, ga_near, gya_near = near
    y_2 = call(select_two_kernel, [block], (places,), y_2, y_2_last, weight=W_HOP)[0]
    y_1, y_3, y_2, x_cut_1, x_cut_beside_0, ga_here = together(
        y_1, y_3, y_2, x_cut_1, x_cut_beside_0, ga_here
    )

    x_cut_beside_1 = moved(x_cut_1, other_core)
    images = (x_cut_0, x_cut_1, x_cut_beside_0, x_cut_beside_1)
    outs = [((4 * rows, width), bf16)] * 2
    x_high, x_low = call(join_kernel, outs, (), xa_high, xa_low, *images)
    outs = [((rows, 4 * rows), f32), block]
    g_2, gy_2 = call(far_kernel, outs, (params,), y_2, x_high, x_low)
    gy_2_last = moved(gy_2, last_row)
    g_2, y_1, y_3 = together(g_2, y_1, y_3)
    outs = [((2 * rows, 4 * rows), f32)] + [block] * 2
    g_13, gy_1, gy_3 = call(far_kernel, outs, (params,), y_1, y_3, x_high, x_low)
    back_1 = moved(gy_1, in_row(-1))
    back_3 = moved(gy_3, in_row(1))

    g_13, x_high = together(g_13, x_high)
    arrays = (y_own, y_last, x_high, x_low)
    kernel = lambda *refs: near_kernel(2 * rows, *refs)
    near = call(kernel, [square, block] * 2, (params, places), *arrays)
    gb_here, gyb_here, gb_near, gyb_near = near
    arrays = (y_own, y_last, y_1, y_3, y_2, gb_here, gb_near, g_13, g_2)
    kernel = lambda *refs: image_kernel(2 * rows, *refs)
    gx_0, gx_1, gx_near_0, gx_near_1 = call(kernel, [half] * 4, (places,), *arrays)
    gx_beside_0 = moved(gx_near_0, other_core)
    gx_beside_1 = moved(gx_near_1, other_core)
    gx_0 = call(add_kernel, [half], (), gx_0, gx_beside_0)[0]
    gx_cut_0 = moved(gx_0, other_group)
    gx_1, y_1, y_3 = together(gx_1, y_1, y_3)
    arrays = (y_own, y_last, y_1, y_3, y_2, ga_here, ga_near, g_13, g_2)
    kernel = lambda *refs: image_kernel(0, *refs)
    gx_own, gx_near_own = call(kernel, [block] * 2, (places,), *arrays)
    gx_near_own, gx_1 = together(gx_near_own, gx_1)

    gy_2, gy_2_last = together(gy_2, gy_2_last)
    for_2 = call(select_two_kernel, [block], (places,), gy_2, gy_2_last, weight=W_BACK)[0]
    back_1, back_3, for_2, gx_near_own, gx_1, gx_beside_1 = together(
        back_1, back_3, for_2, gx_near_own, gx_1, gx_beside_1
    )
    arrays = (gya_near, gyb_near, back_1, back_3)
    gy_last = call(last_kernel, [block], (places,), *arrays, weight=W_LAST)[0]
    arrays = (gya_here, gyb_here, *arrays)
    gy_own = call(own_kernel, [block], (places,), *arrays)[0]
    home = moved(gy_last, last_row)
    back_2 = moved(for_2, in_row(2))
    gx_beside_own = moved(gx_near_own, other_core)
    gx_cut_0, gx_1 = together(gx_cut_0, gx_1)
    gx_1 = call(add_kernel, [half], (), gx_1, gx_beside_1, weight=W_ADD)[0]
    gx_cut_1 = moved(gx_1, other_group)
    home, gx_cut_1, gy_own = together(home, gx_cut_1, gy_own)
    parts = (gx_own, gx_beside_own, (gx_cut_0, gx_cut_1))
    image_grad = finish(params, (x_0, x_1), x_inv, *parts, weight=W_END)
    back_2, image_grad, gy_own = together(back_2, image_grad, gy_own)
    text_grad = finish(params, y_own, y_inv, gy_own, back_2, home)
    return (image_grad, text_grad)


def solution(mesh):
    rows = P(("cuts", "blk"), None)
    return jax.shard_map(
        local, mesh=mesh, in_specs=(rows, rows, P(), P()), out_specs=(rows, rows), check_vma=False
    )
```

time: 104 us -> 95 us (0.913)
  waiting for transfers between devices: 47.4 us -> 37.7 us
  Pallas kernels: 17.4 us -> 21 us
  starting transfers between devices: 34 us -> 31.5 us
    ppermute x19 -> x21, waiting for transfers between devices: 47.4 us -> 37.7 us  [moved(): return lax.ppermute(block, ('cuts', 'blk'), pairs)]
    pallas_call x0 -> x2, Pallas kernels: none -> 3.27 us  [finish(): pl.pallas_call(kernel, out_shape=jax.ShapeDtypeStruct(shape, jnp.float32)...]
    ppermute x19 -> x21, starting transfers between devices: 34 us -> 31.5 us  [moved(): return lax.ppermute(block, ('cuts', 'blk'), pairs)]
    unnamed x8 -> x4, local copies, waits for them, and re-layouts: 2.84 us -> 2.12 us
    pallas_call x12 -> x17, Pallas kernels: 17.4 us -> 17.8 us  [call(): pl.pallas_call(kernel, out_shape=[jax.ShapeDtypeStruct(shape, dtype) for...]
  transfers between devices with their start and end apart: 19 -> 21, of which waited for: 9 -> 10; matrix products, arithmetic and copies ran while one was open for 0% -> 0% of each run, Pallas kernels for 6% -> 17%
where the time goes in v4:
time: 95 us; the launch traced here: 94.8 us
  waiting for transfers between devices  37.7 us (40%)
  starting transfers between devices  31.5 us (33%)
  Pallas kernels  21 us (22%)
  between operations  2.3 us (2%)
  local copies, waits for them, and re-layouts  2.12 us (2%)
    ppermute x21, waiting for transfers between devices, moved(): return lax.ppermute(block, ('cuts', 'blk'), pairs)  37.7 us
    ppermute x21, starting transfers between devices, moved(): return lax.ppermute(block, ('cuts', 'blk'), pairs)  31.5 us
    pallas_call x17, Pallas kernels, call(): pl.pallas_call(kernel, out_shape=[jax.ShapeDtypeStruct(shape, dtype) for...  17.8 us
    pallas_call x2, Pallas kernels, finish(): pl.pallas_call(kernel, out_shape=jax.ShapeDtypeStruct(shape, jnp.float32)...  3.27 us
    unnamed x4, local copies, waits for them, and re-layouts  2.12 us
  transfers between devices with their start and end apart: 21, of which 10 were waited for; matrix products, arithmetic and copies ran while one was open for 0% of the time, Pallas kernels for 17%

profile of v4, /device:TPU:1, one launch (start us, length us, event | category | flops | bytes accessed | tf_op | source)
XLA Modules:
  0.0 94.8 jit_solution(826713617746735793)
XLA Ops:
  0.6 0.0 copy-start
  0.6 1.1 %copy-done = f32[128,1152]{1,0:T(8,128)S(1)} copy-done((f32[128,1152]{1,0:T(8,128)S(1)}, f32[128,1152]{1,0:T(8,128)}, u32[]{:S(2)}) %copy-start) | copy-done | bytes 589848
  1.7 0.1 shard_map.59
  1.8 3.7 %collective-permute-start.1 = (f32[128,1152]{1,0:T(8,128)S(1)}, f32[128,1152]{1,0:T(8,128)S(1)}, u32[]{:S(2)}, u32[]{:S(2)}) collective-permute-start(f32[128,1152]{1,0:T(8,128)S(1)} %get-tuple-element.89.own.refs_2_.refs_1_.refs_0_), channel_id=1, source_target_pairs={{0,4},{1,5},{2,6},{3,7},{4,0},{5,1},{6,2},{7,3},{8,12},{9,13},{10,... | collective-permute-start | bytes 1769480 | tf_op jit(solution)/shard_map/ppermute | solution.py:24
  5.5 2.7 %collective-permute-start = (f32[128,1152]{1,0:T(8,128)S(1)}, f32[128,1152]{1,0:T(8,128)S(1)}, u32[]{:S(2)}, u32[]{:S(2)}) collective-permute-start(f32[128,1152]{1,0:T(8,128)S(1)} %get-tuple-element.89.own.refs_2_.refs_1_.refs_0_), channel_id=1, source_target_pairs={{0,8},{1,137},{2,10},{3,139},{4,12},{5,141},{6,14},{7,143},{8,16},... | collective-permute-start | bytes 1769480 | tf_op jit(solution)/shard_map/ppermute | solution.py:24
  8.2 1.1 %copy-done.1 = f32[128,1152]{1,0:T(8,128)S(1)} copy-done((f32[128,1152]{1,0:T(8,128)S(1)}, f32[128,1152]{1,0:T(8,128)}, u32[]{:S(2)}) %copy-start.1) | copy-done | bytes 589848
  9.3 0.1 shard_map.60
  9.4 0.1 collective-permute-start.3
  9.5 2.4 %collective-permute-start.4 = (f32[64,1152]{1,0:T(8,128)S(1)}, f32[64,1152]{1,0:T(8,128)S(1)}, u32[]{:S(2)}, u32[]{:S(2)}) collective-permute-start(f32[64,1152]{1,0:T(8,128)S(1)} %get-tuple-element.90.refs_0_), channel_id=1, source_target_pairs={{0,128},{1,129},{2,130},{3,131},{4,132},{5,133},{6,134},{7,135},{8... | collective-permute-start | bytes 884744 | tf_op jit(solution)/shard_map/ppermute | solution.py:24
  12.0 0.4 collective-permute-start.2
  12.3 5.2 %collective-permute-done.1.two = f32[128,1152]{1,0:T(8,128)S(1)} collective-permute-done((f32[128,1152]{1,0:T(8,128)S(1)}, f32[128,1152]{1,0:T(8,128)S(1)}, u32[]{:S(2)}, u32[]{:S(2)}) %collective-permute-start.1) | collective-permute-done | bytes 589856 | tf_op jit(solution)/shard_map/ppermute | solution.py:24
  17.5 3.7 %collective-permute-start.7 = (f32[128,1152]{1,0:T(8,128)S(1)}, f32[128,1152]{1,0:T(8,128)S(1)}, u32[]{:S(2)}, u32[]{:S(2)}) collective-permute-start(f32[128,1152]{1,0:T(8,128)S(1)} %collective-permute-done.1.two), channel_id=1, source_target_pairs={{0,8},{1,137},{2,10},{3,139},{4,12},{5,141},{6,14},{7,143},{8,16},... | collective-permute-start | bytes 1769480 | tf_op jit(solution)/shard_map/ppermute | solution.py:24
  21.2 0.1 add_convert_fusion.places.refs_1_.refs_0_
  21.3 0.0 collective-permute-done.3.refs_3_
  21.3 0.0 collective-permute-done.4.refs_0_
  21.3 0.0 collective-permute-done.2.refs_2_
  21.3 5.5 %collective-permute-done.last.refs_3_.refs_2_ = f32[128,1152]{1,0:T(8,128)S(1)} collective-permute-done((f32[128,1152]{1,0:T(8,128)S(1)}, f32[128,1152]{1,0:T(8,128)S(1)}, u32[]{:S(2)}, u32[]{:S(2)}) %collective-permute-start) | collective-permute-done | bytes 589856 | tf_op jit(solution)/shard_map/ppermute | solution.py:24
  26.8 0.7 shard_map.61
  27.4 0.9 collective-permute-start.6
  28.4 0.6 collective-permute-start.5
  29.0 1.2 %collective-permute-start.9 = (f32[64,1152]{1,0:T(8,128)S(1)}, f32[64,1152]{1,0:T(8,128)S(1)}, u32[]{:S(2)}, u32[]{:S(2)}) collective-permute-start(f32[64,1152]{1,0:T(8,128)S(1)} %collective-permute-done.4.refs_0_), channel_id=1, source_target_pairs={{0,1},{1,0},{2,3},{3,2},{4,5},{5,4},{6,7},{7,6},{8,9},{9,8},{10,11... | collective-permute-start | bytes 884744 | tf_op jit(solution)/shard_map/ppermute | solution.py:24
  30.1 1.6 %collective-permute-start.8 = (f32[64,1152]{1,0:T(8,128)S(1)}, f32[64,1152]{1,0:T(8,128)S(1)}, u32[]{:S(2)}, u32[]{:S(2)}) collective-permute-start(f32[64,1152]{1,0:T(8,128)S(1)} %get-tuple-element.87.refs_1_), channel_id=1, source_target_pairs={{0,128},{1,129},{2,130},{3,131},{4,132},{5,133},{6,134},{7,135},{8... | collective-permute-start | bytes 884744 | tf_op jit(solution)/shard_map/ppermute | solution.py:24
  33.1 0.1 pad_maximum_fusion.refs_0_.params.params_ref
  33.2 0.2 shard_map.63
  33.4 2.2 %shard_map.64 = (f32[128,128]{1,0:T(8,128)S(1)}, f32[128,1152]{1,0:T(8,128)S(1)}, f32[128,128]{1,0:T(8,128)S(1)}, f32[128,1152]{1,0:T(8,128)S(1)}) custom-call(f32[2]{0:T(128)S(1)} %pad_maximum_fusion.refs_0_.params.params_ref, s32[4]{0:T(128)S(1)} %add_convert_fusion.places.refs_1_.refs_0_, f32[128,1152]{1,0:T(8,128)S(1)} %get-tuple-element.89.own.refs_2_.refs_1_.refs_0_, ...), custom_call_target="tpu_custom_call" | custom-call | tf_op jit(solution)/shard_map/pallas_call | solution.py:206
  35.6 3.5 %collective-permute-done.7.two_last = f32[128,1152]{1,0:T(8,128)S(1)} collective-permute-done((f32[128,1152]{1,0:T(8,128)S(1)}, f32[128,1152]{1,0:T(8,128)S(1)}, u32[]{:S(2)}, u32[]{:S(2)}) %collective-permute-start.7) | collective-permute-done | bytes 589856 | tf_op jit(solution)/shard_map/ppermute | solution.py:24
  39.2 0.6 shard_map.62.refs_0_.refs_5_
  39.8 0.0 collective-permute-done.9.refs_2_
  39.8 2.5 %collective-permute-done.8.refs_1_ = f32[64,1152]{1,0:T(8,128)S(1)} collective-permute-done((f32[64,1152]{1,0:T(8,128)S(1)}, f32[64,1152]{1,0:T(8,128)S(1)}, u32[]{:S(2)}, u32[]{:S(2)}) %collective-permute-start.8) | collective-permute-done | bytes 294944 | tf_op jit(solution)/shard_map/ppermute | solution.py:24
  42.3 0.0 collective-permute-done.6.refs_1_.refs_4_
  42.3 1.2 %collective-permute-done.5.refs_0_.refs_3_ = f32[128,1152]{1,0:T(8,128)S(1)} collective-permute-done((f32[128,1152]{1,0:T(8,128)S(1)}, f32[128,1152]{1,0:T(8,128)S(1)}, u32[]{:S(2)}, u32[]{:S(2)}) %collective-permute-start.5) | collective-permute-done | bytes 589856 | tf_op jit(solution)/shard_map/ppermute | solution.py:24
  43.5 1.8 %collective-permute-start.10 = (f32[64,1152]{1,0:T(8,128)S(1)}, f32[64,1152]{1,0:T(8,128)S(1)}, u32[]{:S(2)}, u32[]{:S(2)}) collective-permute-start(f32[64,1152]{1,0:T(8,128)S(1)} %collective-permute-done.8.refs_1_), channel_id=1, source_target_pairs={{0,1},{1,0},{2,3},{3,2},{4,5},{5,4},{6,7},{7,6},{8,9},{9,8},{10,11... | collective-permute-start | bytes 884744 | tf_op jit(solution)/shard_map/ppermute | solution.py:24
  45.3 1.2 %collective-permute-done.10.refs_3_ = f32[64,1152]{1,0:T(8,128)S(1)} collective-permute-done((f32[64,1152]{1,0:T(8,128)S(1)}, f32[64,1152]{1,0:T(8,128)S(1)}, u32[]{:S(2)}, u32[]{:S(2)}) %collective-permute-start.10) | collective-permute-done | bytes 294944 | tf_op jit(solution)/shard_map/ppermute | solution.py:24
  46.5 0.3 shard_map.65
  46.8 2.5 %shard_map.66 = (f32[128,512]{1,0:T(8,128)S(1)}, f32[128,1152]{1,0:T(8,128)S(1)}) custom-call(f32[2]{0:T(128)S(1)} %pad_maximum_fusion.refs_0_.params.params_ref, f32[128,1152]{1,0:T(8,128)S(1)} %shard_map.62.refs_0_.refs_5_, bf16[512,1152]{1,0:T(8,128)(2,1)S(1)} %get-tuple-element.112.refs_1_.refs_2_.refs_4_, ...), custom_call_target="tpu_custom_call" | custom-call | tf_op jit(solution)/shard_map/pallas_call | solution.py:206
  49.3 5.0 %collective-permute-start.13 = (f32[128,1152]{1,0:T(8,128)S(1)}, f32[128,1152]{1,0:T(8,128)S(1)}, u32[]{:S(2)}, u32[]{:S(2)}) collective-permute-start(f32[128,1152]{1,0:T(8,128)S(1)} %get-tuple-element.109.two), channel_id=1, source_target_pairs={{0,120},{1,249},{2,122},{3,251},{4,124},{5,253},{6,126},{7,255},{8... | collective-permute-start | bytes 1769480 | tf_op jit(solution)/shard_map/ppermute | solution.py:24
  54.3 2.9 %shard_map.67 = (f32[256,512]{1,0:T(8,128)S(1)}, f32[128,1152]{1,0:T(8,128)S(1)}, f32[128,1152]{1,0:T(8,128)S(1)}) custom-call(f32[2]{0:T(128)S(1)} %pad_maximum_fusion.refs_0_.params.params_ref, f32[128,1152]{1,0:T(8,128)S(1)} %collective-permute-done.5.refs_0_.refs_3_, f32[128,1152]{1,0:T(8,128)S(1)} %collective-permute-done.6.refs_1_.refs_4_, ...), custom_call_target="tpu_custom_call" | custom-call | tf_op jit(solution)/shard_map/pallas_call | solution.py:206
  57.2 0.8 collective-permute-start.11
  58.0 0.8 collective-permute-start.12
  58.8 2.2 %shard_map.69 = (f32[128,128]{1,0:T(8,128)S(1)}, f32[128,1152]{1,0:T(8,128)S(1)}, f32[128,128]{1,0:T(8,128)S(1)}, f32[128,1152]{1,0:T(8,128)S(1)}) custom-call(f32[2]{0:T(128)S(1)} %pad_maximum_fusion.refs_0_.params.params_ref, s32[4]{0:T(128)S(1)} %add_convert_fusion.places.refs_1_.refs_0_, f32[128,1152]{1,0:T(8,128)S(1)} %get-tuple-element.89.own.refs_2_.refs_1_.refs_0_, ...), custom_call_target="tpu_custom_call" | custom-call | tf_op jit(solution)/shard_map/pallas_call | solution.py:206
  61.0 1.9 %shard_map.70 = (f32[64,1152]{1,0:T(8,128)S(1)}, f32[64,1152]{1,0:T(8,128)S(1)}, f32[64,1152]{1,0:T(8,128)S(1)}, f32[64,1152]{1,0:T(8,128)S(1)}) custom-call(s32[4]{0:T(128)S(1)} %add_convert_fusion.places.refs_1_.refs_0_, f32[128,1152]{1,0:T(8,128)S(1)} %get-tuple-element.89.own.refs_2_.refs_1_.refs_0_, ...), custom_call_target="tpu_custom_call" | custom-call | tf_op jit(solution)/shard_map/pallas_call | solution.py:206
  62.9 0.6 collective-permute-start.17
  63.5 0.1 collective-permute-start.14
  63.6 1.1 %collective-permute-done.17.beside = f32[64,1152]{1,0:T(8,128)S(1)} collective-permute-done((f32[64,1152]{1,0:T(8,128)S(1)}, f32[64,1152]{1,0:T(8,128)S(1)}, u32[]{:S(2)}, u32[]{:S(2)}) %collective-permute-start.17) | collective-permute-done | bytes 294944 | tf_op jit(solution)/shard_map/ppermute | solution.py:24
  64.7 2.0 %collective-permute-start.18 = (f32[64,1152]{1,0:T(8,128)S(1)}, f32[64,1152]{1,0:T(8,128)S(1)}, u32[]{:S(2)}, u32[]{:S(2)}) collective-permute-start(f32[64,1152]{1,0:T(8,128)S(1)} %shard_map.72), channel_id=1, source_target_pairs={{0,128},{1,129},{2,130},{3,131},{4,132},{5,133},{6,134},{7,135},{8... | collective-permute-start | bytes 884744 | tf_op jit(solution)/shard_map/ppermute | solution.py:24
  66.7 1.9 %shard_map.71 = (f32[128,1152]{1,0:T(8,128)S(1)}, f32[128,1152]{1,0:T(8,128)S(1)}) custom-call(s32[4]{0:T(128)S(1)} %add_convert_fusion.places.refs_1_.refs_0_, f32[128,1152]{1,0:T(8,128)S(1)} %get-tuple-element.89.own.refs_2_.refs_1_.refs_0_, f32[128,1152]{1,0:T(8,128)S(1)} %collective-permute-done.last.refs_3_.refs_2_, ...), custom_call_target="tpu_custom_call" | custom-call | tf_op jit(solution)/shard_map/pallas_call | solution.py:206
  68.6 0.0 collective-permute-done.13.two_last
  68.6 0.6 shard_map.68
  69.2 0.0 collective-permute-done.14.beside
  69.2 3.1 %collective-permute-done.11.back_1 = f32[128,1152]{1,0:T(8,128)S(1)} collective-permute-done((f32[128,1152]{1,0:T(8,128)S(1)}, f32[128,1152]{1,0:T(8,128)S(1)}, u32[]{:S(2)}, u32[]{:S(2)}) %collective-permute-start.11) | collective-permute-done | bytes 589856 | tf_op jit(solution)/shard_map/ppermute | solution.py:24
  72.4 1.1 %collective-permute-done.12.back_3 = f32[128,1152]{1,0:T(8,128)S(1)} collective-permute-done((f32[128,1152]{1,0:T(8,128)S(1)}, f32[128,1152]{1,0:T(8,128)S(1)}, u32[]{:S(2)}, u32[]{:S(2)}) %collective-permute-start.12) | collective-permute-done | bytes 589856 | tf_op jit(solution)/shard_map/ppermute | solution.py:24
  73.5 0.7 shard_map.73
  74.2 0.6 collective-permute-start.19
  74.8 1.0 %collective-permute-start.16 = (f32[128,1152]{1,0:T(8,128)S(1)}, f32[128,1152]{1,0:T(8,128)S(1)}, u32[]{:S(2)}, u32[]{:S(2)}) collective-permute-start(f32[128,1152]{1,0:T(8,128)S(1)} %get-tuple-element.130), channel_id=1, source_target_pairs={{0,1},{1,0},{2,3},{3,2},{4,5},{5,4},{6,7},{7,6},{8,9},{9,8},{10,11... | collective-permute-start | bytes 1769480 | tf_op jit(solution)/shard_map/ppermute | solution.py:24
  75.8 0.0 collective-permute-start.15
  75.8 0.0 collective-permute-done.18.refs_4_
  75.9 1.6 %collective-permute-start.20 = (f32[64,1152]{1,0:T(8,128)S(1)}, f32[64,1152]{1,0:T(8,128)S(1)}, u32[]{:S(2)}, u32[]{:S(2)}) collective-permute-start(f32[64,1152]{1,0:T(8,128)S(1)} %shard_map.74), channel_id=1, source_target_pairs={{0,128},{1,129},{2,130},{3,131},{4,132},{5,133},{6,134},{7,135},{8... | collective-permute-start | bytes 884744 | tf_op jit(solution)/shard_map/ppermute | solution.py:24
  77.4 0.7 shard_map.75.refs_1_
  78.2 13.2 %collective-permute-done.20.refs_5_ = f32[64,1152]{1,0:T(8,128)S(1)} collective-permute-done((f32[64,1152]{1,0:T(8,128)S(1)}, f32[64,1152]{1,0:T(8,128)S(1)}, u32[]{:S(2)}, u32[]{:S(2)}) %collective-permute-start.20) | collective-permute-done | bytes 294944 | tf_op jit(solution)/shard_map/ppermute | solution.py:24
  91.3 0.0 collective-permute-done.19.refs_3_
  91.3 0.0 collective-permute-done.16.refs_3_
  91.3 1.6 %shard_map.76 = f32[128,1152]{1,0:T(8,128)} custom-call(f32[2]{0:T(128)S(1)} %pad_maximum_fusion.refs_0_.params.params_ref, f32[128,1]{1,0:T(8,128)S(1)} %get-tuple-element.128.inverse_ref, f32[64,1152]{1,0:T(8,128)S(1)} %get-tuple-element.90.refs_0_, f32[64,1152]{1,0:T(8,128)S(1)} %get-tuple-element.87.refs_1_, f32[128,1152]{1,0:T(8,128)S(1)} %get-tuple-element.129.refs_2_, ...), custom_call_target="tpu_custom_call" | custom-call | flops 200000000 | tf_op jit(solution)/shard_map/pallas_call | solution.py:233
  93.0 0.0 collective-permute-done.15.refs_2_
  93.0 1.6 %shard_map.77 = f32[128,1152]{1,0:T(8,128)} custom-call(f32[2]{0:T(128)S(1)} %pad_maximum_fusion.refs_0_.params.params_ref, f32[128,1]{1,0:T(8,128)S(1)} %get-tuple-element.146.inverse_ref, f32[128,1152]{1,0:T(8,128)S(1)} %get-tuple-element.89.own.refs_2_.refs_1_.refs_0_, f32[128,1152]{1,0:T(8,128)S(1)} %shard_map.75.refs_1_, ...), custom_call_target="tpu_custom_call" | custom-call | tf_op jit(solution)/shard_map/pallas_call | solution.py:233
  (3 shorter events, 0.1 us)
Async XLA Ops:
  0.6 1.1 %copy-start = (f32[128,1152]{1,0:T(8,128)S(1)}, f32[128,1152]{1,0:T(8,128)}, u32[]{:S(2)}) copy-start(f32[128,1152]{1,0:T(8,128)} %in_ref.1) | copy-start | bytes 1769476
  1.8 15.7 %collective-permute-start.1 = (f32[128,1152]{1,0:T(8,128)S(1)}, f32[128,1152]{1,0:T(8,128)S(1)}, u32[]{:S(2)}, u32[]{:S(2)}) collective-permute-start(f32[128,1152]{1,0:T(8,128)S(1)} %get-tuple-element.89.own.refs_2_.refs_1_.refs_0_), channel_id=1, source_target_pairs={{0,4},{1,5},{2,6},{3,7},{4,0},{5,1},{6,2},{7,3},{8,12},{9,13},{10,... | collective-permute-start | bytes 1769480 | tf_op jit(solution)/shard_map/ppermute | solution.py:24
  5.5 21.3 %collective-permute-start = (f32[128,1152]{1,0:T(8,128)S(1)}, f32[128,1152]{1,0:T(8,128)S(1)}, u32[]{:S(2)}, u32[]{:S(2)}) collective-permute-start(f32[128,1152]{1,0:T(8,128)S(1)} %get-tuple-element.89.own.refs_2_.refs_1_.refs_0_), channel_id=1, source_target_pairs={{0,8},{1,137},{2,10},{3,139},{4,12},{5,141},{6,14},{7,143},{8,16},... | collective-permute-start | bytes 1769480 | tf_op jit(solution)/shard_map/ppermute | solution.py:24
  8.2 1.1 %copy-start.1 = (f32[128,1152]{1,0:T(8,128)S(1)}, f32[128,1152]{1,0:T(8,128)}, u32[]{:S(2)}) copy-start(f32[128,1152]{1,0:T(8,128)} %in_ref.2) | copy-start | bytes 1769476
  9.4 11.8 %collective-permute-start.3 = (f32[64,1152]{1,0:T(8,128)S(1)}, f32[64,1152]{1,0:T(8,128)S(1)}, u32[]{:S(2)}, u32[]{:S(2)}) collective-permute-start(f32[64,1152]{1,0:T(8,128)S(1)} %get-tuple-element.87.refs_1_), channel_id=1, source_target_pairs={{0,1},{1,0},{2,3},{3,2},{4,5},{5,4},{6,7},{7,6},{8,9},{9,8},{10,11... | collective-permute-start | bytes 884744 | tf_op jit(solution)/shard_map/ppermute | solution.py:24
  9.5 11.7 %collective-permute-start.4 = (f32[64,1152]{1,0:T(8,128)S(1)}, f32[64,1152]{1,0:T(8,128)S(1)}, u32[]{:S(2)}, u32[]{:S(2)}) collective-permute-start(f32[64,1152]{1,0:T(8,128)S(1)} %get-tuple-element.90.refs_0_), channel_id=1, source_target_pairs={{0,128},{1,129},{2,130},{3,131},{4,132},{5,133},{6,134},{7,135},{8... | collective-permute-start | bytes 884744 | tf_op jit(solution)/shard_map/ppermute | solution.py:24
  12.0 9.3 %collective-permute-start.2 = (f32[64,1152]{1,0:T(8,128)S(1)}, f32[64,1152]{1,0:T(8,128)S(1)}, u32[]{:S(2)}, u32[]{:S(2)}) collective-permute-start(f32[64,1152]{1,0:T(8,128)S(1)} %get-tuple-element.90.refs_0_), channel_id=1, source_target_pairs={{0,1},{1,0},{2,3},{3,2},{4,5},{5,4},{6,7},{7,6},{8,9},{9,8},{10,11... | collective-permute-start | bytes 884744 | tf_op jit(solution)/shard_map/ppermute | solution.py:24
  17.5 21.7 %collective-permute-start.7 = (f32[128,1152]{1,0:T(8,128)S(1)}, f32[128,1152]{1,0:T(8,128)S(1)}, u32[]{:S(2)}, u32[]{:S(2)}) collective-permute-start(f32[128,1152]{1,0:T(8,128)S(1)} %collective-permute-done.1.two), channel_id=1, source_target_pairs={{0,8},{1,137},{2,10},{3,139},{4,12},{5,141},{6,14},{7,143},{8,16},... | collective-permute-start | bytes 1769480 | tf_op jit(solution)/shard_map/ppermute | solution.py:24
  27.4 14.9 %collective-permute-start.6 = (f32[128,1152]{1,0:T(8,128)S(1)}, f32[128,1152]{1,0:T(8,128)S(1)}, u32[]{:S(2)}, u32[]{:S(2)}) collective-permute-start(f32[128,1152]{1,0:T(8,128)S(1)} %get-tuple-element.83), channel_id=1, source_target_pairs={{0,6},{1,7},{2,0},{3,1},{4,2},{5,3},{6,4},{7,5},{8,14},{9,15},{10,... | collective-permute-start | bytes 1769480 | tf_op jit(solution)/shard_map/ppermute | solution.py:24
  28.4 15.2 %collective-permute-start.5 = (f32[128,1152]{1,0:T(8,128)S(1)}, f32[128,1152]{1,0:T(8,128)S(1)}, u32[]{:S(2)}, u32[]{:S(2)}) collective-permute-start(f32[128,1152]{1,0:T(8,128)S(1)} %get-tuple-element.82), channel_id=1, source_target_pairs={{0,2},{1,3},{2,4},{3,5},{4,6},{5,7},{6,0},{7,1},{8,10},{9,11},{10,... | collective-permute-start | bytes 1769480 | tf_op jit(solution)/shard_map/ppermute | solution.py:24
  29.0 10.8 %collective-permute-start.9 = (f32[64,1152]{1,0:T(8,128)S(1)}, f32[64,1152]{1,0:T(8,128)S(1)}, u32[]{:S(2)}, u32[]{:S(2)}) collective-permute-start(f32[64,1152]{1,0:T(8,128)S(1)} %collective-permute-done.4.refs_0_), channel_id=1, source_target_pairs={{0,1},{1,0},{2,3},{3,2},{4,5},{5,4},{6,7},{7,6},{8,9},{9,8},{10,11... | collective-permute-start | bytes 884744 | tf_op jit(solution)/shard_map/ppermute | solution.py:24
  30.1 12.2 %collective-permute-start.8 = (f32[64,1152]{1,0:T(8,128)S(1)}, f32[64,1152]{1,0:T(8,128)S(1)}, u32[]{:S(2)}, u32[]{:S(2)}) collective-permute-start(f32[64,1152]{1,0:T(8,128)S(1)} %get-tuple-element.87.refs_1_), channel_id=1, source_target_pairs={{0,128},{1,129},{2,130},{3,131},{4,132},{5,133},{6,134},{7,135},{8... | collective-permute-start | bytes 884744 | tf_op jit(solution)/shard_map/ppermute | solution.py:24
  43.5 3.0 %collective-permute-start.10 = (f32[64,1152]{1,0:T(8,128)S(1)}, f32[64,1152]{1,0:T(8,128)S(1)}, u32[]{:S(2)}, u32[]{:S(2)}) collective-permute-start(f32[64,1152]{1,0:T(8,128)S(1)} %collective-permute-done.8.refs_1_), channel_id=1, source_target_pairs={{0,1},{1,0},{2,3},{3,2},{4,5},{5,4},{6,7},{7,6},{8,9},{9,8},{10,11... | collective-permute-start | bytes 884744 | tf_op jit(solution)/shard_map/ppermute | solution.py:24
  49.3 19.3 %collective-permute-start.13 = (f32[128,1152]{1,0:T(8,128)S(1)}, f32[128,1152]{1,0:T(8,128)S(1)}, u32[]{:S(2)}, u32[]{:S(2)}) collective-permute-start(f32[128,1152]{1,0:T(8,128)S(1)} %get-tuple-element.109.two), channel_id=1, source_target_pairs={{0,120},{1,249},{2,122},{3,251},{4,124},{5,253},{6,126},{7,255},{8... | collective-permute-start | bytes 1769480 | tf_op jit(solution)/shard_map/ppermute | solution.py:24
  57.2 15.1 %collective-permute-start.11 = (f32[128,1152]{1,0:T(8,128)S(1)}, f32[128,1152]{1,0:T(8,128)S(1)}, u32[]{:S(2)}, u32[]{:S(2)}) collective-permute-start(f32[128,1152]{1,0:T(8,128)S(1)} %get-tuple-element.106), channel_id=1, source_target_pairs={{0,6},{1,7},{2,0},{3,1},{4,2},{5,3},{6,4},{7,5},{8,14},{9,15},{10,... | collective-permute-start | bytes 1769480 | tf_op jit(solution)/shard_map/ppermute | solution.py:24
  58.0 15.5 %collective-permute-start.12 = (f32[128,1152]{1,0:T(8,128)S(1)}, f32[128,1152]{1,0:T(8,128)S(1)}, u32[]{:S(2)}, u32[]{:S(2)}) collective-permute-start(f32[128,1152]{1,0:T(8,128)S(1)} %get-tuple-element.107), channel_id=1, source_target_pairs={{0,2},{1,3},{2,4},{3,5},{4,6},{5,7},{6,0},{7,1},{8,10},{9,11},{10,... | collective-permute-start | bytes 1769480 | tf_op jit(solution)/shard_map/ppermute | solution.py:24
  62.9 1.8 %collective-permute-start.17 = (f32[64,1152]{1,0:T(8,128)S(1)}, f32[64,1152]{1,0:T(8,128)S(1)}, u32[]{:S(2)}, u32[]{:S(2)}) collective-permute-start(f32[64,1152]{1,0:T(8,128)S(1)} %get-tuple-element.132), channel_id=1, source_target_pairs={{0,1},{1,0},{2,3},{3,2},{4,5},{5,4},{6,7},{7,6},{8,9},{9,8},{10,11... | collective-permute-start | bytes 884744 | tf_op jit(solution)/shard_map/ppermute | solution.py:24
  63.5 5.8 %collective-permute-start.14 = (f32[64,1152]{1,0:T(8,128)S(1)}, f32[64,1152]{1,0:T(8,128)S(1)}, u32[]{:S(2)}, u32[]{:S(2)}) collective-permute-start(f32[64,1152]{1,0:T(8,128)S(1)} %get-tuple-element.126), channel_id=1, source_target_pairs={{0,1},{1,0},{2,3},{3,2},{4,5},{5,4},{6,7},{7,6},{8,9},{9,8},{10,11... | collective-permute-start | bytes 884744 | tf_op jit(solution)/shard_map/ppermute | solution.py:24
  64.7 11.1 %collective-permute-start.18 = (f32[64,1152]{1,0:T(8,128)S(1)}, f32[64,1152]{1,0:T(8,128)S(1)}, u32[]{:S(2)}, u32[]{:S(2)}) collective-permute-start(f32[64,1152]{1,0:T(8,128)S(1)} %shard_map.72), channel_id=1, source_target_pairs={{0,128},{1,129},{2,130},{3,131},{4,132},{5,133},{6,134},{7,135},{8... | collective-permute-start | bytes 884744 | tf_op jit(solution)/shard_map/ppermute | solution.py:24
  74.2 17.2 %collective-permute-start.19 = (f32[128,1152]{1,0:T(8,128)S(1)}, f32[128,1152]{1,0:T(8,128)S(1)}, u32[]{:S(2)}, u32[]{:S(2)}) collective-permute-start(f32[128,1152]{1,0:T(8,128)S(1)} %shard_map.73), channel_id=1, source_target_pairs={{0,120},{1,249},{2,122},{3,251},{4,124},{5,253},{6,126},{7,255},{8... | collective-permute-start | bytes 1769480 | tf_op jit(solution)/shard_map/ppermute | solution.py:24
  74.8 16.6 %collective-permute-start.16 = (f32[128,1152]{1,0:T(8,128)S(1)}, f32[128,1152]{1,0:T(8,128)S(1)}, u32[]{:S(2)}, u32[]{:S(2)}) collective-permute-start(f32[128,1152]{1,0:T(8,128)S(1)} %get-tuple-element.130), channel_id=1, source_target_pairs={{0,1},{1,0},{2,3},{3,2},{4,5},{5,4},{6,7},{7,6},{8,9},{9,8},{10,11... | collective-permute-start | bytes 1769480 | tf_op jit(solution)/shard_map/ppermute | solution.py:24
  75.8 17.2 %collective-permute-start.15 = (f32[128,1152]{1,0:T(8,128)S(1)}, f32[128,1152]{1,0:T(8,128)S(1)}, u32[]{:S(2)}, u32[]{:S(2)}) collective-permute-start(f32[128,1152]{1,0:T(8,128)S(1)} %shard_map.68), channel_id=1, source_target_pairs={{0,4},{1,5},{2,6},{3,7},{4,0},{5,1},{6,2},{7,3},{8,12},{9,13},{10,... | collective-permute-start | bytes 1769480 | tf_op jit(solution)/shard_map/ppermute | solution.py:24
  75.9 15.5 %collective-permute-start.20 = (f32[64,1152]{1,0:T(8,128)S(1)}, f32[64,1152]{1,0:T(8,128)S(1)}, u32[]{:S(2)}, u32[]{:S(2)}) collective-permute-start(f32[64,1152]{1,0:T(8,128)S(1)} %shard_map.74), channel_id=1, source_target_pairs={{0,128},{1,129},{2,130},{3,131},{4,132},{5,133},{6,134},{7,135},{8... | collective-permute-start | bytes 884744 | tf_op jit(solution)/shard_map/ppermute | solution.py:24

commit v5 on v4

v5 whole, which is shorter than its diff:
```python
import jax
import jax.numpy as jnp
from jax import lax
from jax.experimental import pallas as pl
from jax.experimental.pallas import tpu as pltpu
from jax.sharding import PartitionSpec as P

GROUPS, BLOCKS, ROW = 2, 128, 8
W_ONE = 0
W_HOP = 300_000_000
W_CUT = 600_000_000
W_LAST = 0
W_BACK = 0
W_HALF = 1_000_000_000
W_END = 1_000_000_000
W_HOME = 100_000_000


def moved(block, place):
    pairs = []
    for group in range(GROUPS):
        for position in range(BLOCKS):
            to_group, to_position = place(group, position)
            pairs.append((group * BLOCKS + position, to_group * BLOCKS + to_position % BLOCKS))
    return lax.ppermute(block, ("cuts", "blk"), pairs)


def next_row(group, position):
    return (group, position + ROW) if position % 2 == 0 else (1 - group, position + ROW)


def last_row(group, position):
    return (group, position - ROW) if position % 2 == 0 else (1 - group, position - ROW)


def in_row(chips):
    return lambda group, position: (
        group,
        position // ROW * ROW + (position + 2 * chips) % ROW,
    )


def other_core(group, position):
    return group, position ^ 1


def other_group(group, position):
    return 1 - group, position


def together(*values):
    return lax.optimization_barrier(values)


def split(values):
    high = values.astype(jnp.bfloat16)
    return high, (values - high.astype(jnp.float32)).astype(jnp.bfloat16)


def dot3(a, b, b_dim):
    dims = (((1,), (b_dim,)), ((), ()))
    (a_high, a_low), (b_high, b_low) = a, b

    def one(u, v):
        return lax.dot_general(u, v, dims, preferred_element_type=jnp.float32)

    return one(a_high, b_high) + (one(a_low, b_high) + one(a_high, b_low))


def places():
    position = lax.axis_index("blk")
    column = position % ROW // 2
    return position % 2 == 1, column < 2, column >= 3, column >= 1


def sigmoid(values):
    return 1.0 / (1.0 + jnp.exp(-values))


def params_kernel(log_scale, bias, out_ref):
    row_ids = lax.broadcasted_iota(jnp.int32, out_ref.shape, 0)
    scale = jnp.exp(jnp.zeros(out_ref.shape, jnp.float32) + log_scale[0])
    out_ref[...] = jnp.where(row_ids == 0, scale, bias[0])


def normalize_kernel(_, in_ref, inverse_ref, *outs):
    values = in_ref[...]
    inverse = lax.rsqrt(jnp.sum(values * values, axis=-1, keepdims=True) + 1e-06)
    inverse_ref[...] = inverse
    values = values * inverse
    for at, out in enumerate(outs):
        out[...] = values[at * out.shape[0] : (at + 1) * out.shape[0], :]


def split_kernel(*refs):
    *images, high_ref, low_ref = refs
    at = 0
    for image in images:
        high, low = split(image[...])
        high_ref[at : at + image.shape[0], :] = high
        low_ref[at : at + image.shape[0], :] = low
        at += image.shape[0]


def join_kernel(first_high, first_low, second_high, second_low, *refs):
    *images, high_ref, low_ref = refs
    middle = first_high.shape[0]
    at = middle + second_high.shape[0]
    high_ref[:middle, :] = first_high[...]
    low_ref[:middle, :] = first_low[...]
    high_ref[middle:at, :] = second_high[...]
    low_ref[middle:at, :] = second_low[...]
    for image in images:
        high, low = split(image[...])
        high_ref[at : at + image.shape[0], :] = high
        low_ref[at : at + image.shape[0], :] = low
        at += image.shape[0]


def far_kernel(params, *refs):
    count = (len(refs) - 3) // 2
    texts, (high_ref, low_ref, grads_ref), outs = refs[:count], refs[count:-count], refs[-count:]
    rows = texts[0].shape[0]
    image = (high_ref[...], low_ref[...])
    text = split(jnp.concatenate([ref[...] for ref in texts], axis=0))
    grads = sigmoid(params[0:1, 0:1] * dot3(text, image, 1) + params[1:2, 0:1])
    grads_ref[...] = grads
    to_text = dot3(split(grads), image, 0)
    for at, out in enumerate(outs):
        out[...] = to_text[at * rows : (at + 1) * rows, :]


def near_kernel(first, params, *refs):
    (own, last, high_ref, low_ref), outs = refs[:4], refs[4:]
    rows = own.shape[0]
    for side, grads_ref, to_text in ((0, *outs[:2]), (1, *outs[2:])):
        span = pl.ds(first + side * rows, rows)
        image = (high_ref[span, :], low_ref[span, :])
        text = own[...]
        if side == 1:
            text = jnp.where(places()[0], last[...], text)
        logits = params[0:1, 0:1] * dot3(split(text), image, 1) + params[1:2, 0:1]
        if side == 0 and first == 0:
            row_ids = lax.broadcasted_iota(jnp.int32, logits.shape, 0)
            col_ids = lax.broadcasted_iota(jnp.int32, logits.shape, 1)
            signs = jnp.where(row_ids == col_ids, -1.0, 1.0)
            grads = signs * sigmoid(signs * logits)
        else:
            grads = sigmoid(logits)
        grads_ref[...] = grads
        to_text[...] = dot3(split(grads), image, 0)


def image_kernel(first, own, last, y_1, y_3, y_2, g_here, g_near, g_13, g_2, *outs):
    rows = own.shape[0]
    far = [y_1[...], y_3[...], y_2[...]]
    here = own[...]
    near = jnp.where(places()[0], last[...], here)
    for side, text, mine in ((0, here, g_here), (1, near, g_near)):
        columns = pl.ds(first + side * rows, rows)
        grads = [g_13[:, columns], g_2[:, columns], mine[...]]
        grads = split(jnp.concatenate(grads, axis=0).T)
        to_image = dot3(grads, split(jnp.concatenate([*far, text], axis=0)), 0)
        mine_outs = outs[side * len(outs) // 2 : (side + 1) * len(outs) // 2]
        for at, out in enumerate(mine_outs):
            out[...] = to_image[at * out.shape[0] : (at + 1) * out.shape[0], :]


def select_kernel(own, last, one_ref, three_ref):
    one_ref[...] = jnp.where(places()[2], last[...], own[...])
    three_ref[...] = jnp.where(places()[3], last[...], own[...])


def select_two_kernel(two, two_last, out_ref):
    out_ref[...] = jnp.where(places()[1], two_last[...], two[...])


def last_kernel(near_a, near_b, back_1, back_3, out_ref):
    total = jnp.where(places()[0], near_a[...] + near_b[...], 0.0)
    total = total + jnp.where(places()[2], back_1[...], 0.0)
    out_ref[...] = total + jnp.where(places()[3], back_3[...], 0.0)


def own_kernel(here_a, here_b, near_a, near_b, back_1, back_3, out_ref):
    total = here_a[...] + here_b[...]
    total = total + jnp.where(places()[0], 0.0, near_a[...] + near_b[...])
    total = total + jnp.where(places()[2], 0.0, back_1[...])
    out_ref[...] = total + jnp.where(places()[3], 0.0, back_3[...])


def add_three_kernel(one, two, three, out_ref):
    out_ref[...] = one[...] + two[...] + three[...]


def add_kernel(here, beside, out_ref):
    out_ref[...] = here[...] + beside[...]


def finish_kernel(params, y, y_inv, *refs):
    y_parts, x_halves, x_inv, x_totals, outs, (held, left) = (
        refs[:2],
        refs[2:4],
        refs[4],
        refs[5:7],
        refs[7:9],
        refs[9:],
    )
    rows = x_halves[0].shape[0]
    copies = []
    for at in range(4):
        side, first = at // 2, at % 2 * rows
        span = pl.ds(first, rows)
        if side == 0:
            normal, inverse = x_halves[at][...], x_inv[span, :]
            total = x_totals[at][...]
        else:
            normal, inverse = y[span, :], y_inv[span, :]
            total = y_parts[0][span, :] + y_parts[1][span, :]
        total = params[0:1, 0:1] * total
        along = jnp.sum(normal * total, axis=-1, keepdims=True)
        held[side, span, :] = inverse * (total - normal * along)
        copies.append(
            pltpu.make_async_copy(
                held.at[side, span, :], outs[side].at[span, :], left.at[at]
            )
        )
        copies[-1].start()
    for copy in copies:
        copy.wait()


def call(kernel, outs, *arrays, scalars=(), weight=0):
    vmem = pl.BlockSpec(memory_space=pltpu.VMEM)
    smem = pl.BlockSpec(memory_space=pltpu.SMEM)
    return pl.pallas_call(
        kernel,
        out_shape=[jax.ShapeDtypeStruct(shape, dtype) for shape, dtype in outs],
        in_specs=[smem] * len(scalars) + [vmem] * len(arrays),
        out_specs=[vmem] * len(outs),
        compiler_params=pltpu.CompilerParams(vmem_limit_bytes=16 * 2**20),
        cost_estimate=pl.CostEstimate(flops=weight, transcendentals=0, bytes_accessed=0),
    )(*scalars, *arrays)


def finish(*arrays):
    shape = arrays[1].shape
    hbm = pl.BlockSpec(memory_space=pltpu.HBM)
    return pl.pallas_call(
        finish_kernel,
        out_shape=[jax.ShapeDtypeStruct(shape, jnp.float32)] * 2,
        in_specs=[pl.BlockSpec(memory_space=pltpu.VMEM)] * len(arrays),
        out_specs=[hbm] * 2,
        scratch_shapes=[pltpu.VMEM((2, *shape), jnp.float32), pltpu.SemaphoreType.DMA((4,))],
        compiler_params=pltpu.CompilerParams(vmem_limit_bytes=16 * 2**20),
        cost_estimate=pl.CostEstimate(flops=0, transcendentals=0, bytes_accessed=0),
    )(*arrays)


def local(image_embed, text_embed, log_scale, bias):
    rows, width = image_embed.shape
    f32, bf16 = jnp.float32, jnp.bfloat16
    block = ((rows, width), f32)
    half = ((rows // 2, width), f32)

    square = ((rows, rows), f32)
    pair = ((2 * rows, width), bf16)

    outs = [((rows, 1), f32), block]
    y_inv, y_own = call(lambda *refs: normalize_kernel(None, *refs), outs, text_embed)
    outs = [((rows, 1), f32), half, half]
    x_inv, x_0, x_1 = call(normalize_kernel, outs, y_inv, image_embed)
    params = call(params_kernel, [((8, 128), f32)], scalars=(log_scale, bias))
    y_last = moved(y_own, next_row)
    y_2 = moved(y_own, in_row(2))
    x_cut_0 = moved(x_0, other_group)
    x_beside_0 = moved(x_0, other_core)
    x_beside_1 = moved(x_1, other_core)
    y_2_last = moved(y_2, next_row)
    y_last, y_own, y_2, x_0, x_1, x_beside_0, x_beside_1 = together(
        y_last, y_own, y_2, x_0, x_1, x_beside_0, x_beside_1
    )
    for_1, for_3 = call(select_kernel, [block] * 2, y_own, y_last, weight=W_ONE)
    y_1 = moved(for_1, in_row(1))
    y_3 = moved(for_3, in_row(-1))
    x_cut_0, x_1, y_own, _ = together(x_cut_0, x_1, y_own, for_1)
    xc_high, xc_low = call(
        split_kernel, [((rows // 2, width), bf16)] * 2, x_cut_0, weight=W_CUT
    )
    x_1, xc_high, x_cut_0 = together(x_1, xc_high, x_cut_0)
    x_cut_1 = moved(x_1, other_group)
    x_cut_beside_0 = moved(x_cut_0, other_core)
    xa_high, xa_low = call(split_kernel, [pair] * 2, x_0, x_1, x_beside_0, x_beside_1)
    arrays = (y_own, y_last, xa_high, xa_low)
    kernel = lambda *refs: near_kernel(0, *refs)
    near = call(kernel, [square, block] * 2, *params, *arrays)
    ga_here, gya_here, ga_near, gya_near = near
    y_2 = call(select_two_kernel, [block], y_2, y_2_last, weight=W_HOP)[0]
    y_1, y_3, y_2, x_cut_1, x_cut_beside_0, ga_here = together(
        y_1, y_3, y_2, x_cut_1, x_cut_beside_0, ga_here
    )

    x_cut_beside_1 = moved(x_cut_1, other_core)
    images = (x_cut_1, x_cut_beside_0, x_cut_beside_1)
    outs = [((4 * rows, width), bf16)] * 2
    x_high, x_low = call(join_kernel, outs, xa_high, xa_low, xc_high, xc_low, *images)
    outs = [((2 * rows, 4 * rows), f32)] + [block] * 2
    g_13, gy_1, gy_3 = call(far_kernel, outs, *params, y_1, y_3, x_high, x_low)
    back_1 = moved(gy_1, in_row(-1))
    back_3 = moved(gy_3, in_row(1))
    g_13, y_2 = together(g_13, y_2)
    outs = [((rows, 4 * rows), f32), block]
    g_2, gy_2 = call(far_kernel, outs, *params, y_2, x_high, x_low)
    gy_2_last = moved(gy_2, last_row)

    g_2, x_high = together(g_2, x_high)
    arrays = (y_own, y_last, x_high, x_low)
    kernel = lambda *refs: near_kernel(2 * rows, *refs)
    near = call(kernel, [square, block] * 2, *params, *arrays)
    gb_here, gyb_here, gb_near, gyb_near = near
    arrays = (y_own, y_last, y_1, y_3, y_2, gb_here, gb_near, g_13, g_2)
    kernel = lambda *refs: image_kernel(2 * rows, *refs)
    gx_0, gx_1, gx_near_0, gx_near_1 = call(kernel, [half] * 4, *arrays)
    gx_beside_0 = moved(gx_near_0, other_core)
    gx_beside_1 = moved(gx_near_1, other_core)
    gx_0 = call(add_kernel, [half], gx_0, gx_beside_0)[0]
    gx_cut_0 = moved(gx_0, other_group)
    gx_1, y_1, y_3 = together(gx_1, y_1, y_3)
    arrays = (y_own, y_last, y_1, y_3, y_2, ga_here, ga_near, g_13, g_2)
    kernel = lambda *refs: image_kernel(0, *refs)
    outs = call(kernel, [half] * 4, *arrays)
    gx_own_0, gx_own_1, gx_near_own_0, gx_near_own_1 = outs
    gx_1 = call(add_kernel, [half], gx_1, gx_beside_1)[0]
    back_1, back_3, gx_near_own_0, gx_near_own_1, gx_1 = together(
        back_1, back_3, gx_near_own_0, gx_near_own_1, gx_1
    )
    arrays = (gya_near, gyb_near, back_1, back_3)
    gy_last = call(last_kernel, [block], *arrays, weight=W_LAST)[0]
    home = moved(gy_last, last_row)
    gy_2, gy_2_last, gx_1, gx_near_own_0, gx_near_own_1, _ = together(
        gy_2, gy_2_last, gx_1, gx_near_own_0, gx_near_own_1, gy_last
    )
    for_2 = call(select_two_kernel, [block], gy_2, gy_2_last, weight=W_BACK)[0]
    back_2 = moved(for_2, in_row(2))
    gx_cut_1 = moved(gx_1, other_group)
    gx_beside_own_0 = moved(gx_near_own_0, other_core)
    gx_beside_own_1 = moved(gx_near_own_1, other_core)
    arrays = (gya_here, gyb_here, *arrays)
    gy_own = call(own_kernel, [block], *arrays)[0]
    gx_cut_0, gy_own = together(gx_cut_0, gy_own)
    parts = (gx_own_0, gx_beside_own_0, gx_cut_0)
    image_0 = call(add_three_kernel, [half], *parts, weight=W_HALF)[0]
    gx_cut_1, image_0 = together(gx_cut_1, image_0)
    parts = (gx_own_1, gx_beside_own_1, gx_cut_1)
    image_1 = call(add_three_kernel, [half], *parts, weight=W_END)[0]
    home, gy_own, image_0, image_1 = together(home, gy_own, image_0, image_1)
    gy_own = call(add_kernel, [block], gy_own, home, weight=W_HOME)[0]
    back_2, gy_own, image_0, image_1 = together(back_2, gy_own, image_0, image_1)
    return tuple(
        finish(*params, y_own, y_inv, gy_own, back_2, x_0, x_1, x_inv, image_0, image_1)
    )


def solution(mesh):
    rows = P(("cuts", "blk"), None)
    return jax.shard_map(
        local, mesh=mesh, in_specs=(rows, rows, P(), P()), out_specs=(rows, rows), check_vma=False
    )
```

time: 95 us -> 87.7 us (0.923)
  Pallas kernels: 21 us -> 13.5 us
  starting transfers between devices: 31.5 us -> 33.2 us
  waiting for transfers between devices: 37.7 us -> 36.5 us
    pallas_call x17 -> x22, Pallas kernels: 17.8 us -> 12.1 us  [call(): pl.pallas_call(kernel, out_shape=[jax.ShapeDtypeStruct(shape, dtype) for...]
    pallas_call x2 -> x1, Pallas kernels: 3.27 us -> 1.4 us  [finish(): pl.pallas_call(finish_kernel, out_shape=[jax.ShapeDtypeStruct(shape, jnp....]
    ppermute x21 -> x22, starting transfers between devices: 31.5 us -> 33.2 us  [moved(): return lax.ppermute(block, ('cuts', 'blk'), pairs)]
    ppermute x21 -> x22, waiting for transfers between devices: 37.7 us -> 36.5 us  [moved(): return lax.ppermute(block, ('cuts', 'blk'), pairs)]
  transfers between devices with their start and end apart: 21 -> 22, of which waited for: 10 -> 11; matrix products, arithmetic and copies ran while one was open for 0% -> 0% of each run, Pallas kernels for 17% -> 11%
where the time goes in v5:
time: 87.7 us; the launch traced here: 87.5 us
  waiting for transfers between devices  36.5 us (42%)
  starting transfers between devices  33.2 us (38%)
  Pallas kernels  13.5 us (15%)
  between operations  2.27 us (3%)
  local copies, waits for them, and re-layouts  2.12 us (2%)
    ppermute x22, waiting for transfers between devices, moved(): return lax.ppermute(block, ('cuts', 'blk'), pairs)  36.5 us
    ppermute x22, starting transfers between devices, moved(): return lax.ppermute(block, ('cuts', 'blk'), pairs)  33.2 us
    pallas_call x22, Pallas kernels, call(): pl.pallas_call(kernel, out_shape=[jax.ShapeDtypeStruct(shape, dtype) for...  12.1 us
    unnamed x4, local copies, waits for them, and re-layouts  2.12 us
  transfers between devices with their start and end apart: 22, of which 11 were waited for; matrix products, arithmetic and copies ran while one was open for 0% of the time, Pallas kernels for 11%

profile of v5, /device:TPU:1, one launch (start us, length us, event | category | flops | bytes accessed | tf_op | source)
XLA Modules:
  0.0 87.5 jit_solution(17933860460675829280)
XLA Ops:
  0.6 1.1 %copy-done.1 = f32[128,1152]{1,0:T(8,128)S(1)} copy-done((f32[128,1152]{1,0:T(8,128)S(1)}, f32[128,1152]{1,0:T(8,128)}, u32[]{:S(2)}) %copy-start.1) | copy-done | bytes 589848
  1.7 0.1 shard_map.60
  1.8 3.7 %collective-permute-start.2 = (f32[128,1152]{1,0:T(8,128)S(1)}, f32[128,1152]{1,0:T(8,128)S(1)}, u32[]{:S(2)}, u32[]{:S(2)}) collective-permute-start(f32[128,1152]{1,0:T(8,128)S(1)} %get-tuple-element.92.own.refs_1_.refs_0_.y), channel_id=1, source_target_pairs={{0,4},{1,5},{2,6},{3,7},{4,0},{5,1},{6,2},{7,3},{8,12},{9,13},{10,... | collective-permute-start | bytes 1769480 | tf_op jit(solution)/shard_map/ppermute | solution.py:25
  5.5 2.7 %collective-permute-start.1 = (f32[128,1152]{1,0:T(8,128)S(1)}, f32[128,1152]{1,0:T(8,128)S(1)}, u32[]{:S(2)}, u32[]{:S(2)}) collective-permute-start(f32[128,1152]{1,0:T(8,128)S(1)} %get-tuple-element.92.own.refs_1_.refs_0_.y), channel_id=1, source_target_pairs={{0,8},{1,137},{2,10},{3,139},{4,12},{5,141},{6,14},{7,143},{8,16},... | collective-permute-start | bytes 1769480 | tf_op jit(solution)/shard_map/ppermute | solution.py:25
  8.2 1.1 %copy-done = f32[128,1152]{1,0:T(8,128)S(1)} copy-done((f32[128,1152]{1,0:T(8,128)S(1)}, f32[128,1152]{1,0:T(8,128)}, u32[]{:S(2)}) %copy-start) | copy-done | bytes 589848
  9.3 0.1 shard_map.61
  9.4 0.1 collective-permute-start.3
  9.5 0.5 collective-permute-start.4
  10.0 2.0 %collective-permute-start = (f32[64,1152]{1,0:T(8,128)S(1)}, f32[64,1152]{1,0:T(8,128)S(1)}, u32[]{:S(2)}, u32[]{:S(2)}) collective-permute-start(f32[64,1152]{1,0:T(8,128)S(1)} %get-tuple-element.100.refs_0_.refs_2_), channel_id=1, source_target_pairs={{0,128},{1,129},{2,130},{3,131},{4,132},{5,133},{6,134},{7,135},{8... | collective-permute-start | bytes 884744 | tf_op jit(solution)/shard_map/ppermute | solution.py:25
  12.0 5.5 %collective-permute-done.2.two = f32[128,1152]{1,0:T(8,128)S(1)} collective-permute-done((f32[128,1152]{1,0:T(8,128)S(1)}, f32[128,1152]{1,0:T(8,128)S(1)}, u32[]{:S(2)}, u32[]{:S(2)}) %collective-permute-start.2) | collective-permute-done | bytes 589856 | tf_op jit(solution)/shard_map/ppermute | solution.py:25
  17.5 3.7 %collective-permute-start.7 = (f32[128,1152]{1,0:T(8,128)S(1)}, f32[128,1152]{1,0:T(8,128)S(1)}, u32[]{:S(2)}, u32[]{:S(2)}) collective-permute-start(f32[128,1152]{1,0:T(8,128)S(1)} %collective-permute-done.2.two), channel_id=1, source_target_pairs={{0,8},{1,137},{2,10},{3,139},{4,12},{5,141},{6,14},{7,143},{8,16},... | collective-permute-start | bytes 1769480 | tf_op jit(solution)/shard_map/ppermute | solution.py:25
  21.2 0.0 collective-permute-done.3.refs_2_
  21.2 0.0 collective-permute-done.4.refs_3_
  21.2 5.7 %collective-permute-done.1.last.refs_2_.refs_1_ = f32[128,1152]{1,0:T(8,128)S(1)} collective-permute-done((f32[128,1152]{1,0:T(8,128)S(1)}, f32[128,1152]{1,0:T(8,128)S(1)}, u32[]{:S(2)}, u32[]{:S(2)}) %collective-permute-start.1) | collective-permute-done | bytes 589856 | tf_op jit(solution)/shard_map/ppermute | solution.py:25
  26.9 0.1 shard_map.62
  27.0 0.4 collective-permute-start.5
  27.4 2.4 %collective-permute-start.6 = (f32[128,1152]{1,0:T(8,128)S(1)}, f32[128,1152]{1,0:T(8,128)S(1)}, u32[]{:S(2)}, u32[]{:S(2)}) collective-permute-start(f32[128,1152]{1,0:T(8,128)S(1)} %get-tuple-element.93), channel_id=1, source_target_pairs={{0,6},{1,7},{2,0},{3,1},{4,2},{5,3},{6,4},{7,5},{8,14},{9,15},{10,... | collective-permute-start | bytes 1769480 | tf_op jit(solution)/shard_map/ppermute | solution.py:25
  29.8 0.0 collective-permute-done.refs_0_
  29.8 0.1 shard_map.64
  29.8 0.5 collective-permute-start.8
  30.3 2.7 %collective-permute-start.9 = (f32[64,1152]{1,0:T(8,128)S(1)}, f32[64,1152]{1,0:T(8,128)S(1)}, u32[]{:S(2)}, u32[]{:S(2)}) collective-permute-start(f32[64,1152]{1,0:T(8,128)S(1)} %collective-permute-done.refs_0_), channel_id=1, source_target_pairs={{0,1},{1,0},{2,3},{3,2},{4,5},{5,4},{6,7},{7,6},{8,9},{9,8},{10,11... | collective-permute-start | bytes 884744 | tf_op jit(solution)/shard_map/ppermute | solution.py:25
  34.3 0.2 shard_map.65
  34.5 1.7 %shard_map.66 = (f32[128,128]{1,0:T(8,128)S(1)}, f32[128,1152]{1,0:T(8,128)S(1)}, f32[128,128]{1,0:T(8,128)S(1)}, f32[128,1152]{1,0:T(8,128)S(1)}) custom-call(f32[8,128]{1,0:T(8,128)S(1)} %shard_map.59.refs_0_.params, f32[128,1152]{1,0:T(8,128)S(1)} %get-tuple-element.92.own.refs_1_.refs_0_.y, f32[128,1152]{1,0:T(8,128)S(1)} %collective-permute-done.1.last.refs_2_.refs_1_, ...), custom_call_target="tpu_custom_call" | custom-call | tf_op jit(solution)/shard_map/pallas_call | solution.py:235
  36.2 3.0 %collective-permute-done.7.two_last = f32[128,1152]{1,0:T(8,128)S(1)} collective-permute-done((f32[128,1152]{1,0:T(8,128)S(1)}, f32[128,1152]{1,0:T(8,128)S(1)}, u32[]{:S(2)}, u32[]{:S(2)}) %collective-permute-start.7) | collective-permute-done | bytes 589856 | tf_op jit(solution)/shard_map/ppermute | solution.py:25
  39.2 0.1 shard_map.63.refs_0_.refs_4_
  39.2 2.8 %collective-permute-done.8.refs_0_ = f32[64,1152]{1,0:T(8,128)S(1)} collective-permute-done((f32[64,1152]{1,0:T(8,128)S(1)}, f32[64,1152]{1,0:T(8,128)S(1)}, u32[]{:S(2)}, u32[]{:S(2)}) %collective-permute-start.8) | collective-permute-done | bytes 294944 | tf_op jit(solution)/shard_map/ppermute | solution.py:25
  42.0 0.0 collective-permute-done.9.refs_1_
  42.0 1.6 %collective-permute-done.5.refs_0_.refs_2_ = f32[128,1152]{1,0:T(8,128)S(1)} collective-permute-done((f32[128,1152]{1,0:T(8,128)S(1)}, f32[128,1152]{1,0:T(8,128)S(1)}, u32[]{:S(2)}, u32[]{:S(2)}) %collective-permute-start.5) | collective-permute-done | bytes 589856 | tf_op jit(solution)/shard_map/ppermute | solution.py:25
  43.6 0.4 collective-permute-start.10
  44.0 1.2 %collective-permute-done.10.refs_2_ = f32[64,1152]{1,0:T(8,128)S(1)} collective-permute-done((f32[64,1152]{1,0:T(8,128)S(1)}, f32[64,1152]{1,0:T(8,128)S(1)}, u32[]{:S(2)}, u32[]{:S(2)}) %collective-permute-start.10) | collective-permute-done | bytes 294944 | tf_op jit(solution)/shard_map/ppermute | solution.py:25
  45.3 0.3 shard_map.67
  45.5 2.4 %shard_map.68 = (f32[256,512]{1,0:T(8,128)S(1)}, f32[128,1152]{1,0:T(8,128)S(1)}, f32[128,1152]{1,0:T(8,128)S(1)}) custom-call(f32[8,128]{1,0:T(8,128)S(1)} %shard_map.59.refs_0_.params, f32[128,1152]{1,0:T(8,128)S(1)} %collective-permute-done.5.refs_0_.refs_2_, f32[128,1152]{1,0:T(8,128)S(1)} %collective-permute-done.6.refs_1_.refs_3_, ...), custom_call_target="tpu_custom_call" | custom-call | tf_op jit(solution)/shard_map/pallas_call | solution.py:235
  47.9 2.8 %collective-permute-start.12 = (f32[128,1152]{1,0:T(8,128)S(1)}, f32[128,1152]{1,0:T(8,128)S(1)}, u32[]{:S(2)}, u32[]{:S(2)}) collective-permute-start(f32[128,1152]{1,0:T(8,128)S(1)} %get-tuple-element.118), channel_id=1, source_target_pairs={{0,6},{1,7},{2,0},{3,1},{4,2},{5,3},{6,4},{7,5},{8,14},{9,15},{10,... | collective-permute-start | bytes 1769480 | tf_op jit(solution)/shard_map/ppermute | solution.py:25
  50.7 0.0 collective-permute-start.13
  50.7 1.9 %shard_map.69 = (f32[128,512]{1,0:T(8,128)S(1)}, f32[128,1152]{1,0:T(8,128)S(1)}) custom-call(f32[8,128]{1,0:T(8,128)S(1)} %shard_map.59.refs_0_.params, f32[128,1152]{1,0:T(8,128)S(1)} %shard_map.63.refs_0_.refs_4_, bf16[512,1152]{1,0:T(8,128)(2,1)S(1)} %get-tuple-element.121.refs_2_.refs_1_.refs_3_, ...), custom_call_target="tpu_custom_call" | custom-call | tf_op jit(solution)/shard_map/pallas_call | solution.py:235
  52.6 1.9 %collective-permute-start.11 = (f32[128,1152]{1,0:T(8,128)S(1)}, f32[128,1152]{1,0:T(8,128)S(1)}, u32[]{:S(2)}, u32[]{:S(2)}) collective-permute-start(f32[128,1152]{1,0:T(8,128)S(1)} %get-tuple-element.142.two), channel_id=1, source_target_pairs={{0,120},{1,249},{2,122},{3,251},{4,124},{5,253},{6,126},{7,255},{8... | collective-permute-start | bytes 1769480 | tf_op jit(solution)/shard_map/ppermute | solution.py:25
  54.5 1.7 %shard_map.70 = (f32[128,128]{1,0:T(8,128)S(1)}, f32[128,1152]{1,0:T(8,128)S(1)}, f32[128,128]{1,0:T(8,128)S(1)}, f32[128,1152]{1,0:T(8,128)S(1)}) custom-call(f32[8,128]{1,0:T(8,128)S(1)} %shard_map.59.refs_0_.params, f32[128,1152]{1,0:T(8,128)S(1)} %get-tuple-element.92.own.refs_1_.refs_0_.y, f32[128,1152]{1,0:T(8,128)S(1)} %collective-permute-done.1.last.refs_2_.refs_1_, ...), custom_call_target="tpu_custom_call" | custom-call | tf_op jit(solution)/shard_map/pallas_call | solution.py:235
  56.2 1.4 %shard_map.71 = (f32[64,1152]{1,0:T(8,128)S(1)}, f32[64,1152]{1,0:T(8,128)S(1)}, f32[64,1152]{1,0:T(8,128)S(1)}, f32[64,1152]{1,0:T(8,128)S(1)}) custom-call(f32[128,1152]{1,0:T(8,128)S(1)} %get-tuple-element.92.own.refs_1_.refs_0_.y, f32[128,1152]{1,0:T(8,128)S(1)} %collective-permute-done.1.last.refs_2_.refs_1_, ...), custom_call_target="tpu_custom_call" | custom-call | tf_op jit(solution)/shard_map/pallas_call | solution.py:235
  57.6 0.8 collective-permute-start.17
  58.3 0.1 collective-permute-start.14
  58.4 1.1 %collective-permute-done.17.beside = f32[64,1152]{1,0:T(8,128)S(1)} collective-permute-done((f32[64,1152]{1,0:T(8,128)S(1)}, f32[64,1152]{1,0:T(8,128)S(1)}, u32[]{:S(2)}, u32[]{:S(2)}) %collective-permute-start.17) | collective-permute-done | bytes 294944 | tf_op jit(solution)/shard_map/ppermute | solution.py:25
  59.6 1.8 %collective-permute-start.18 = (f32[64,1152]{1,0:T(8,128)S(1)}, f32[64,1152]{1,0:T(8,128)S(1)}, u32[]{:S(2)}, u32[]{:S(2)}) collective-permute-start(f32[64,1152]{1,0:T(8,128)S(1)} %shard_map.76), channel_id=1, source_target_pairs={{0,128},{1,129},{2,130},{3,131},{4,132},{5,133},{6,134},{7,135},{8... | collective-permute-start | bytes 884744 | tf_op jit(solution)/shard_map/ppermute | solution.py:25
  61.3 1.4 %shard_map.72 = (f32[64,1152]{1,0:T(8,128)S(1)}, f32[64,1152]{1,0:T(8,128)S(1)}, f32[64,1152]{1,0:T(8,128)S(1)}, f32[64,1152]{1,0:T(8,128)S(1)}) custom-call(f32[128,1152]{1,0:T(8,128)S(1)} %get-tuple-element.92.own.refs_1_.refs_0_.y, f32[128,1152]{1,0:T(8,128)S(1)} %collective-permute-done.1.last.refs_2_.refs_1_, ...), custom_call_target="tpu_custom_call" | custom-call | tf_op jit(solution)/shard_map/pallas_call | solution.py:235
  62.7 0.0 collective-permute-done.14.beside
  62.8 0.3 collective-permute-done.12.back_1
  63.0 3.1 %collective-permute-done.13.back_3 = f32[128,1152]{1,0:T(8,128)S(1)} collective-permute-done((f32[128,1152]{1,0:T(8,128)S(1)}, f32[128,1152]{1,0:T(8,128)S(1)}, u32[]{:S(2)}, u32[]{:S(2)}) %collective-permute-start.13) | collective-permute-done | bytes 589856 | tf_op jit(solution)/shard_map/ppermute | solution.py:25
  66.1 0.1 shard_map.74
  66.3 1.9 %collective-permute-start.16 = (f32[128,1152]{1,0:T(8,128)S(1)}, f32[128,1152]{1,0:T(8,128)S(1)}, u32[]{:S(2)}, u32[]{:S(2)}) collective-permute-start(f32[128,1152]{1,0:T(8,128)S(1)} %shard_map.74), channel_id=1, source_target_pairs={{0,120},{1,249},{2,122},{3,251},{4,124},{5,253},{6,126},{7,255},{8... | collective-permute-start | bytes 1769480 | tf_op jit(solution)/shard_map/ppermute | solution.py:25
  68.2 0.0 collective-permute-done.11.two_last
  68.2 0.1 shard_map.75
  68.2 0.2 collective-permute-start.15
  68.4 2.2 %collective-permute-start.20 = (f32[64,1152]{1,0:T(8,128)S(1)}, f32[64,1152]{1,0:T(8,128)S(1)}, u32[]{:S(2)}, u32[]{:S(2)}) collective-permute-start(f32[64,1152]{1,0:T(8,128)S(1)} %get-tuple-element.151), channel_id=1, source_target_pairs={{0,1},{1,0},{2,3},{3,2},{4,5},{5,4},{6,7},{7,6},{8,9},{9,8},{10,11... | collective-permute-start | bytes 884744 | tf_op jit(solution)/shard_map/ppermute | solution.py:25
  70.6 1.4 %collective-permute-start.19 = (f32[64,1152]{1,0:T(8,128)S(1)}, f32[64,1152]{1,0:T(8,128)S(1)}, u32[]{:S(2)}, u32[]{:S(2)}) collective-permute-start(f32[64,1152]{1,0:T(8,128)S(1)} %shard_map.73), channel_id=1, source_target_pairs={{0,128},{1,129},{2,130},{3,131},{4,132},{5,133},{6,134},{7,135},{8... | collective-permute-start | bytes 884744 | tf_op jit(solution)/shard_map/ppermute | solution.py:25
  72.0 1.8 %collective-permute-done.18.three = f32[64,1152]{1,0:T(8,128)S(1)} collective-permute-done((f32[64,1152]{1,0:T(8,128)S(1)}, f32[64,1152]{1,0:T(8,128)S(1)}, u32[]{:S(2)}, u32[]{:S(2)}) %collective-permute-start.18) | collective-permute-done | bytes 294944 | tf_op jit(solution)/shard_map/ppermute | solution.py:25
  73.9 1.2 %collective-permute-start.21 = (f32[64,1152]{1,0:T(8,128)S(1)}, f32[64,1152]{1,0:T(8,128)S(1)}, u32[]{:S(2)}, u32[]{:S(2)}) collective-permute-start(f32[64,1152]{1,0:T(8,128)S(1)} %get-tuple-element.155), channel_id=1, source_target_pairs={{0,1},{1,0},{2,3},{3,2},{4,5},{5,4},{6,7},{7,6},{8,9},{9,8},{10,11... | collective-permute-start | bytes 884744 | tf_op jit(solution)/shard_map/ppermute | solution.py:25
  75.1 0.2 shard_map.77.here
  75.2 0.0 collective-permute-done.20.two
  75.3 0.1 shard_map.78.refs_5_
  75.3 10.4 %collective-permute-done.19.three = f32[64,1152]{1,0:T(8,128)S(1)} collective-permute-done((f32[64,1152]{1,0:T(8,128)S(1)}, f32[64,1152]{1,0:T(8,128)S(1)}, u32[]{:S(2)}, u32[]{:S(2)}) %collective-permute-start.19) | collective-permute-done | bytes 294944 | tf_op jit(solution)/shard_map/ppermute | solution.py:25
  85.7 0.0 collective-permute-done.21.two
  85.7 0.1 shard_map.79.refs_6_
  85.8 0.1 shard_map.80.refs_0_
  85.9 0.0 collective-permute-done.15.refs_1_
  85.9 1.4 %shard_map.81 = (f32[128,1152]{1,0:T(8,128)}, f32[128,1152]{1,0:T(8,128)}) custom-call(f32[8,128]{1,0:T(8,128)S(1)} %shard_map.59.refs_0_.params, f32[128,1152]{1,0:T(8,128)S(1)} %get-tuple-element.92.own.refs_1_.refs_0_.y, f32[128,1]{1,0:T(8,128)S(1)} %get-tuple-element.84._.y_inv, f32[128,1152]{1,0:T(8,128)S(1)} %shard_map.80.refs_0_, ...), custom_call_target="tpu_custom_call" | custom-call | tf_op jit(solution)/shard_map/pallas_call | solution.py:248
  (7 shorter events, 0.1 us)
Async XLA Ops:
  0.6 1.1 %copy-start.1 = (f32[128,1152]{1,0:T(8,128)S(1)}, f32[128,1152]{1,0:T(8,128)}, u32[]{:S(2)}) copy-start(f32[128,1152]{1,0:T(8,128)} %refs_0_.1) | copy-start | bytes 1769476
  1.8 15.7 %collective-permute-start.2 = (f32[128,1152]{1,0:T(8,128)S(1)}, f32[128,1152]{1,0:T(8,128)S(1)}, u32[]{:S(2)}, u32[]{:S(2)}) collective-permute-start(f32[128,1152]{1,0:T(8,128)S(1)} %get-tuple-element.92.own.refs_1_.refs_0_.y), channel_id=1, source_target_pairs={{0,4},{1,5},{2,6},{3,7},{4,0},{5,1},{6,2},{7,3},{8,12},{9,13},{10,... | collective-permute-start | bytes 1769480 | tf_op jit(solution)/shard_map/ppermute | solution.py:25
  5.5 21.4 %collective-permute-start.1 = (f32[128,1152]{1,0:T(8,128)S(1)}, f32[128,1152]{1,0:T(8,128)S(1)}, u32[]{:S(2)}, u32[]{:S(2)}) collective-permute-start(f32[128,1152]{1,0:T(8,128)S(1)} %get-tuple-element.92.own.refs_1_.refs_0_.y), channel_id=1, source_target_pairs={{0,8},{1,137},{2,10},{3,139},{4,12},{5,141},{6,14},{7,143},{8,16},... | collective-permute-start | bytes 1769480 | tf_op jit(solution)/shard_map/ppermute | solution.py:25
  8.2 1.1 %copy-start = (f32[128,1152]{1,0:T(8,128)S(1)}, f32[128,1152]{1,0:T(8,128)}, u32[]{:S(2)}) copy-start(f32[128,1152]{1,0:T(8,128)} %in_ref.1) | copy-start | bytes 1769476
  9.4 11.8 %collective-permute-start.3 = (f32[64,1152]{1,0:T(8,128)S(1)}, f32[64,1152]{1,0:T(8,128)S(1)}, u32[]{:S(2)}, u32[]{:S(2)}) collective-permute-start(f32[64,1152]{1,0:T(8,128)S(1)} %get-tuple-element.100.refs_0_.refs_2_), channel_id=1, source_target_pairs={{0,1},{1,0},{2,3},{3,2},{4,5},{5,4},{6,7},{7,6},{8,9},{9,8},{10,11... | collective-permute-start | bytes 884744 | tf_op jit(solution)/shard_map/ppermute | solution.py:25
  9.5 11.7 %collective-permute-start.4 = (f32[64,1152]{1,0:T(8,128)S(1)}, f32[64,1152]{1,0:T(8,128)S(1)}, u32[]{:S(2)}, u32[]{:S(2)}) collective-permute-start(f32[64,1152]{1,0:T(8,128)S(1)} %get-tuple-element.98.refs_1_.refs_3_), channel_id=1, source_target_pairs={{0,1},{1,0},{2,3},{3,2},{4,5},{5,4},{6,7},{7,6},{8,9},{9,8},{10,11... | collective-permute-start | bytes 884744 | tf_op jit(solution)/shard_map/ppermute | solution.py:25
  10.0 19.7 %collective-permute-start = (f32[64,1152]{1,0:T(8,128)S(1)}, f32[64,1152]{1,0:T(8,128)S(1)}, u32[]{:S(2)}, u32[]{:S(2)}) collective-permute-start(f32[64,1152]{1,0:T(8,128)S(1)} %get-tuple-element.100.refs_0_.refs_2_), channel_id=1, source_target_pairs={{0,128},{1,129},{2,130},{3,131},{4,132},{5,133},{6,134},{7,135},{8... | collective-permute-start | bytes 884744 | tf_op jit(solution)/shard_map/ppermute | solution.py:25
  17.5 21.7 %collective-permute-start.7 = (f32[128,1152]{1,0:T(8,128)S(1)}, f32[128,1152]{1,0:T(8,128)S(1)}, u32[]{:S(2)}, u32[]{:S(2)}) collective-permute-start(f32[128,1152]{1,0:T(8,128)S(1)} %collective-permute-done.2.two), channel_id=1, source_target_pairs={{0,8},{1,137},{2,10},{3,139},{4,12},{5,141},{6,14},{7,143},{8,16},... | collective-permute-start | bytes 1769480 | tf_op jit(solution)/shard_map/ppermute | solution.py:25
  27.0 16.6 %collective-permute-start.5 = (f32[128,1152]{1,0:T(8,128)S(1)}, f32[128,1152]{1,0:T(8,128)S(1)}, u32[]{:S(2)}, u32[]{:S(2)}) collective-permute-start(f32[128,1152]{1,0:T(8,128)S(1)} %get-tuple-element.91), channel_id=1, source_target_pairs={{0,2},{1,3},{2,4},{3,5},{4,6},{5,7},{6,0},{7,1},{8,10},{9,11},{10,... | collective-permute-start | bytes 1769480 | tf_op jit(solution)/shard_map/ppermute | solution.py:25
  27.4 16.2 %collective-permute-start.6 = (f32[128,1152]{1,0:T(8,128)S(1)}, f32[128,1152]{1,0:T(8,128)S(1)}, u32[]{:S(2)}, u32[]{:S(2)}) collective-permute-start(f32[128,1152]{1,0:T(8,128)S(1)} %get-tuple-element.93), channel_id=1, source_target_pairs={{0,6},{1,7},{2,0},{3,1},{4,2},{5,3},{6,4},{7,5},{8,14},{9,15},{10,... | collective-permute-start | bytes 1769480 | tf_op jit(solution)/shard_map/ppermute | solution.py:25
  29.8 12.2 %collective-permute-start.8 = (f32[64,1152]{1,0:T(8,128)S(1)}, f32[64,1152]{1,0:T(8,128)S(1)}, u32[]{:S(2)}, u32[]{:S(2)}) collective-permute-start(f32[64,1152]{1,0:T(8,128)S(1)} %get-tuple-element.98.refs_1_.refs_3_), channel_id=1, source_target_pairs={{0,128},{1,129},{2,130},{3,131},{4,132},{5,133},{6,134},{7,135},{8... | collective-permute-start | bytes 884744 | tf_op jit(solution)/shard_map/ppermute | solution.py:25
  30.3 11.8 %collective-permute-start.9 = (f32[64,1152]{1,0:T(8,128)S(1)}, f32[64,1152]{1,0:T(8,128)S(1)}, u32[]{:S(2)}, u32[]{:S(2)}) collective-permute-start(f32[64,1152]{1,0:T(8,128)S(1)} %collective-permute-done.refs_0_), channel_id=1, source_target_pairs={{0,1},{1,0},{2,3},{3,2},{4,5},{5,4},{6,7},{7,6},{8,9},{9,8},{10,11... | collective-permute-start | bytes 884744 | tf_op jit(solution)/shard_map/ppermute | solution.py:25
  43.6 1.7 %collective-permute-start.10 = (f32[64,1152]{1,0:T(8,128)S(1)}, f32[64,1152]{1,0:T(8,128)S(1)}, u32[]{:S(2)}, u32[]{:S(2)}) collective-permute-start(f32[64,1152]{1,0:T(8,128)S(1)} %collective-permute-done.8.refs_0_), channel_id=1, source_target_pairs={{0,1},{1,0},{2,3},{3,2},{4,5},{5,4},{6,7},{7,6},{8,9},{9,8},{10,11... | collective-permute-start | bytes 884744 | tf_op jit(solution)/shard_map/ppermute | solution.py:25
  47.9 15.1 %collective-permute-start.12 = (f32[128,1152]{1,0:T(8,128)S(1)}, f32[128,1152]{1,0:T(8,128)S(1)}, u32[]{:S(2)}, u32[]{:S(2)}) collective-permute-start(f32[128,1152]{1,0:T(8,128)S(1)} %get-tuple-element.118), channel_id=1, source_target_pairs={{0,6},{1,7},{2,0},{3,1},{4,2},{5,3},{6,4},{7,5},{8,14},{9,15},{10,... | collective-permute-start | bytes 1769480 | tf_op jit(solution)/shard_map/ppermute | solution.py:25
  50.7 15.4 %collective-permute-start.13 = (f32[128,1152]{1,0:T(8,128)S(1)}, f32[128,1152]{1,0:T(8,128)S(1)}, u32[]{:S(2)}, u32[]{:S(2)}) collective-permute-start(f32[128,1152]{1,0:T(8,128)S(1)} %get-tuple-element.119), channel_id=1, source_target_pairs={{0,2},{1,3},{2,4},{3,5},{4,6},{5,7},{6,0},{7,1},{8,10},{9,11},{10,... | collective-permute-start | bytes 1769480 | tf_op jit(solution)/shard_map/ppermute | solution.py:25
  52.6 15.5 %collective-permute-start.11 = (f32[128,1152]{1,0:T(8,128)S(1)}, f32[128,1152]{1,0:T(8,128)S(1)}, u32[]{:S(2)}, u32[]{:S(2)}) collective-permute-start(f32[128,1152]{1,0:T(8,128)S(1)} %get-tuple-element.142.two), channel_id=1, source_target_pairs={{0,120},{1,249},{2,122},{3,251},{4,124},{5,253},{6,126},{7,255},{8... | collective-permute-start | bytes 1769480 | tf_op jit(solution)/shard_map/ppermute | solution.py:25
  57.6 2.0 %collective-permute-start.17 = (f32[64,1152]{1,0:T(8,128)S(1)}, f32[64,1152]{1,0:T(8,128)S(1)}, u32[]{:S(2)}, u32[]{:S(2)}) collective-permute-start(f32[64,1152]{1,0:T(8,128)S(1)} %get-tuple-element.145), channel_id=1, source_target_pairs={{0,1},{1,0},{2,3},{3,2},{4,5},{5,4},{6,7},{7,6},{8,9},{9,8},{10,11... | collective-permute-start | bytes 884744 | tf_op jit(solution)/shard_map/ppermute | solution.py:25
  58.3 4.4 %collective-permute-start.14 = (f32[64,1152]{1,0:T(8,128)S(1)}, f32[64,1152]{1,0:T(8,128)S(1)}, u32[]{:S(2)}, u32[]{:S(2)}) collective-permute-start(f32[64,1152]{1,0:T(8,128)S(1)} %get-tuple-element.134), channel_id=1, source_target_pairs={{0,1},{1,0},{2,3},{3,2},{4,5},{5,4},{6,7},{7,6},{8,9},{9,8},{10,11... | collective-permute-start | bytes 884744 | tf_op jit(solution)/shard_map/ppermute | solution.py:25
  59.6 14.3 %collective-permute-start.18 = (f32[64,1152]{1,0:T(8,128)S(1)}, f32[64,1152]{1,0:T(8,128)S(1)}, u32[]{:S(2)}, u32[]{:S(2)}) collective-permute-start(f32[64,1152]{1,0:T(8,128)S(1)} %shard_map.76), channel_id=1, source_target_pairs={{0,128},{1,129},{2,130},{3,131},{4,132},{5,133},{6,134},{7,135},{8... | collective-permute-start | bytes 884744 | tf_op jit(solution)/shard_map/ppermute | solution.py:25
  66.3 19.5 %collective-permute-start.16 = (f32[128,1152]{1,0:T(8,128)S(1)}, f32[128,1152]{1,0:T(8,128)S(1)}, u32[]{:S(2)}, u32[]{:S(2)}) collective-permute-start(f32[128,1152]{1,0:T(8,128)S(1)} %shard_map.74), channel_id=1, source_target_pairs={{0,120},{1,249},{2,122},{3,251},{4,124},{5,253},{6,126},{7,255},{8... | collective-permute-start | bytes 1769480 | tf_op jit(solution)/shard_map/ppermute | solution.py:25
  68.2 17.7 %collective-permute-start.15 = (f32[128,1152]{1,0:T(8,128)S(1)}, f32[128,1152]{1,0:T(8,128)S(1)}, u32[]{:S(2)}, u32[]{:S(2)}) collective-permute-start(f32[128,1152]{1,0:T(8,128)S(1)} %shard_map.75), channel_id=1, source_target_pairs={{0,4},{1,5},{2,6},{3,7},{4,0},{5,1},{6,2},{7,3},{8,12},{9,13},{10,... | collective-permute-start | bytes 1769480 | tf_op jit(solution)/shard_map/ppermute | solution.py:25
  68.4 6.8 %collective-permute-start.20 = (f32[64,1152]{1,0:T(8,128)S(1)}, f32[64,1152]{1,0:T(8,128)S(1)}, u32[]{:S(2)}, u32[]{:S(2)}) collective-permute-start(f32[64,1152]{1,0:T(8,128)S(1)} %get-tuple-element.151), channel_id=1, source_target_pairs={{0,1},{1,0},{2,3},{3,2},{4,5},{5,4},{6,7},{7,6},{8,9},{9,8},{10,11... | collective-permute-start | bytes 884744 | tf_op jit(solution)/shard_map/ppermute | solution.py:25
  70.6 15.1 %collective-permute-start.19 = (f32[64,1152]{1,0:T(8,128)S(1)}, f32[64,1152]{1,0:T(8,128)S(1)}, u32[]{:S(2)}, u32[]{:S(2)}) collective-permute-start(f32[64,1152]{1,0:T(8,128)S(1)} %shard_map.73), channel_id=1, source_target_pairs={{0,128},{1,129},{2,130},{3,131},{4,132},{5,133},{6,134},{7,135},{8... | collective-permute-start | bytes 884744 | tf_op jit(solution)/shard_map/ppermute | solution.py:25
  73.9 11.9 %collective-permute-start.21 = (f32[64,1152]{1,0:T(8,128)S(1)}, f32[64,1152]{1,0:T(8,128)S(1)}, u32[]{:S(2)}, u32[]{:S(2)}) collective-permute-start(f32[64,1152]{1,0:T(8,128)S(1)} %get-tuple-element.155), channel_id=1, source_target_pairs={{0,1},{1,0},{2,3},{3,2},{4,5},{5,4},{6,7},{7,6},{8,9},{9,8},{10,11... | collective-permute-start | bytes 884744 | tf_op jit(solution)/shard_map/ppermute | solution.py:25

commit v6 on v5

--- a/solution.py
+++ b/solution.py
@@ -6,9 +6,11 @@
 from jax.sharding import PartitionSpec as P
 
 GROUPS, BLOCKS, ROW = 2, 128, 8
+FIRST = 64
 W_ONE = 0
-W_HOP = 300_000_000
-W_CUT = 600_000_000
+W_HOP = 0
+W_CUT = 300_000_000
+W_FAR = 3000_000_000
 W_LAST = 0
 W_BACK = 0
 W_HALF = 1_000_000_000
@@ -83,13 +85,19 @@
     out_ref[...] = jnp.where(row_ids == 0, scale, bias[0])
 
 
-def normalize_kernel(_, in_ref, inverse_ref, *outs):
+def image_norm_kernel(_, in_ref, inverse_ref, *outs):
+    normalize_kernel(in_ref, inverse_ref, *outs)
+
+
+def normalize_kernel(in_ref, inverse_ref, *outs):
     values = in_ref[...]
     inverse = lax.rsqrt(jnp.sum(values * values, axis=-1, keepdims=True) + 1e-06)
     inverse_ref[...] = inverse
     values = values * inverse
-    for at, out in enumerate(outs):
-        out[...] = values[at * out.shape[0] : (at + 1) * out.shape[0], :]
+    at = 0
+    for out in outs:
+        out[...] = values[at : at + out.shape[0], :]
+        at = (at + out.shape[0]) % values.shape[0]
 
 
 def split_kernel(*refs):
@@ -161,9 +169,10 @@
         grads = [g_13[:, columns], g_2[:, columns], mine[...]]
         grads = split(jnp.concatenate(grads, axis=0).T)
         to_image = dot3(grads, split(jnp.concatenate([*far, text], axis=0)), 0)
-        mine_outs = outs[side * len(outs) // 2 : (side + 1) * len(outs) // 2]
-        for at, out in enumerate(mine_outs):
-            out[...] = to_image[at * out.shape[0] : (at + 1) * out.shape[0], :]
+        at = 0
+        for out in outs[side * len(outs) // 2 : (side + 1) * len(outs) // 2]:
+            out[...] = to_image[at : at + out.shape[0], :]
+            at += out.shape[0]
 
 
 def select_kernel(own, last, one_ref, three_ref):
@@ -205,14 +214,14 @@
         refs[7:9],
         refs[9:],
     )
-    rows = x_halves[0].shape[0]
     copies = []
-    for at in range(4):
-        side, first = at // 2, at % 2 * rows
+    spans = [(0, at * y.shape[0] // 2, y.shape[0] // 2) for at in (0, 1)]
+    spans += [(1, 0, x_halves[0].shape[0]), (1, x_halves[0].shape[0], x_halves[1].shape[0])]
+    for at, (side, first, rows) in enumerate(spans):
         span = pl.ds(first, rows)
-        if side == 0:
-            normal, inverse = x_halves[at][...], x_inv[span, :]
-            total = x_totals[at][...]
+        if side == 1:
+            normal, inverse = x_halves[at - 2][...], x_inv[span, :]
+            total = x_totals[at - 2][...]
         else:
             normal, inverse = y[span, :], y_inv[span, :]
             total = y_parts[0][span, :] + y_parts[1][span, :]
@@ -221,7 +230,7 @@
         held[side, span, :] = inverse * (total - normal * along)
         copies.append(
             pltpu.make_async_copy(
-                held.at[side, span, :], outs[side].at[span, :], left.at[at]
+                held.at[side, span, :], outs[1 - side].at[span, :], left.at[at]
             )
         )
         copies[-1].start()
@@ -260,15 +269,15 @@
     rows, width = image_embed.shape
     f32, bf16 = jnp.float32, jnp.bfloat16
     block = ((rows, width), f32)
-    half = ((rows // 2, width), f32)
 
     square = ((rows, rows), f32)
     pair = ((2 * rows, width), bf16)
 
     outs = [((rows, 1), f32), block]
-    y_inv, y_own = call(lambda *refs: normalize_kernel(None, *refs), outs, text_embed)
-    outs = [((rows, 1), f32), half, half]
-    x_inv, x_0, x_1 = call(normalize_kernel, outs, y_inv, image_embed)
+    y_inv, y_own = call(normalize_kernel, outs, text_embed)
+    first, second = ((FIRST, width), f32), ((rows - FIRST, width), f32)
+    outs = [((rows, 1), f32), first, second]
+    x_inv, x_0, x_1 = call(image_norm_kernel, outs, y_inv, image_embed)
     params = call(params_kernel, [((8, 128), f32)], scalars=(log_scale, bias))
     y_last = moved(y_own, next_row)
     y_2 = moved(y_own, in_row(2))
@@ -276,15 +285,15 @@
     x_beside_0 = moved(x_0, other_core)
     x_beside_1 = moved(x_1, other_core)
     y_2_last = moved(y_2, next_row)
-    y_last, y_own, y_2, x_0, x_1, x_beside_0, x_beside_1 = together(
-        y_last, y_own, y_2, x_0, x_1, x_beside_0, x_beside_1
+    y_last, y_own, x_0, x_1, x_beside_0, x_beside_1 = together(
+        y_last, y_own, x_0, x_1, x_beside_0, x_beside_1
     )
     for_1, for_3 = call(select_kernel, [block] * 2, y_own, y_last, weight=W_ONE)
     y_1 = moved(for_1, in_row(1))
     y_3 = moved(for_3, in_row(-1))
     x_cut_0, x_1, y_own, _ = together(x_cut_0, x_1, y_own, for_1)
     xc_high, xc_low = call(
-        split_kernel, [((rows // 2, width), bf16)] * 2, x_cut_0, weight=W_CUT
+        split_kernel, [((FIRST, width), bf16)] * 2, x_cut_0, weight=W_CUT
     )
     x_1, xc_high, x_cut_0 = together(x_1, xc_high, x_cut_0)
     x_cut_1 = moved(x_1, other_group)
@@ -294,9 +303,8 @@
     kernel = lambda *refs: near_kernel(0, *refs)
     near = call(kernel, [square, block] * 2, *params, *arrays)
     ga_here, gya_here, ga_near, gya_near = near
-    y_2 = call(select_two_kernel, [block], y_2, y_2_last, weight=W_HOP)[0]
-    y_1, y_3, y_2, x_cut_1, x_cut_beside_0, ga_here = together(
-        y_1, y_3, y_2, x_cut_1, x_cut_beside_0, ga_here
+    y_1, y_3, x_cut_1, x_cut_beside_0, ga_here = together(
+        y_1, y_3, x_cut_1, x_cut_beside_0, ga_here
     )
 
     x_cut_beside_1 = moved(x_cut_1, other_core)
@@ -304,10 +312,12 @@
     outs = [((4 * rows, width), bf16)] * 2
     x_high, x_low = call(join_kernel, outs, xa_high, xa_low, xc_high, xc_low, *images)
     outs = [((2 * rows, 4 * rows), f32)] + [block] * 2
-    g_13, gy_1, gy_3 = call(far_kernel, outs, *params, y_1, y_3, x_high, x_low)
+    arrays = (*params, y_1, y_3, x_high, x_low)
+    g_13, gy_1, gy_3 = call(far_kernel, outs, *arrays, weight=W_FAR)
     back_1 = moved(gy_1, in_row(-1))
     back_3 = moved(gy_3, in_row(1))
-    g_13, y_2 = together(g_13, y_2)
+    g_13, y_2, y_2_last = together(g_13, y_2, y_2_last)
+    y_2 = call(select_two_kernel, [block], y_2, y_2_last, weight=W_HOP)[0]
     outs = [((rows, 4 * rows), f32), block]
     g_2, gy_2 = call(far_kernel, outs, *params, y_2, x_high, x_low)
     gy_2_last = moved(gy_2, last_row)
@@ -319,17 +329,17 @@
     gb_here, gyb_here, gb_near, gyb_near = near
     arrays = (y_own, y_last, y_1, y_3, y_2, gb_here, gb_near, g_13, g_2)
     kernel = lambda *refs: image_kernel(2 * rows, *refs)
-    gx_0, gx_1, gx_near_0, gx_near_1 = call(kernel, [half] * 4, *arrays)
+    gx_0, gx_1, gx_near_0, gx_near_1 = call(kernel, [first, second] * 2, *arrays)
     gx_beside_0 = moved(gx_near_0, other_core)
     gx_beside_1 = moved(gx_near_1, other_core)
-    gx_0 = call(add_kernel, [half], gx_0, gx_beside_0)[0]
+    gx_0 = call(add_kernel, [first], gx_0, gx_beside_0)[0]
     gx_cut_0 = moved(gx_0, other_group)
     gx_1, y_1, y_3 = together(gx_1, y_1, y_3)
     arrays = (y_own, y_last, y_1, y_3, y_2, ga_here, ga_near, g_13, g_2)
     kernel = lambda *refs: image_kernel(0, *refs)
-    outs = call(kernel, [half] * 4, *arrays)
+    outs = call(kernel, [first, second] * 2, *arrays)
     gx_own_0, gx_own_1, gx_near_own_0, gx_near_own_1 = outs
-    gx_1 = call(add_kernel, [half], gx_1, gx_beside_1)[0]
+    gx_1 = call(add_kernel, [second], gx_1, gx_beside_1)[0]
     back_1, back_3, gx_near_own_0, gx_near_own_1, gx_1 = together(
         back_1, back_3, gx_near_own_0, gx_near_own_1, gx_1
     )
@@ -348,10 +358,10 @@
     gy_own = call(own_kernel, [block], *arrays)[0]
     gx_cut_0, gy_own = together(gx_cut_0, gy_own)
     parts = (gx_own_0, gx_beside_own_0, gx_cut_0)
-    image_0 = call(add_three_kernel, [half], *parts, weight=W_HALF)[0]
+    image_0 = call(add_three_kernel, [first], *parts, weight=W_HALF)[0]
     gx_cut_1, image_0 = together(gx_cut_1, image_0)
     parts = (gx_own_1, gx_beside_own_1, gx_cut_1)
-    image_1 = call(add_three_kernel, [half], *parts, weight=W_END)[0]
+    image_1 = call(add_three_kernel, [second], *parts, weight=W_END)[0]
     home, gy_own, image_0, image_1 = together(home, gy_own, image_0, image_1)
     gy_own = call(add_kernel, [block], gy_own, home, weight=W_HOME)[0]
     back_2, gy_own, image_0, image_1 = together(back_2, gy_own, image_0, image_1)

time: 87.7 us -> 85 us (0.969)
  starting transfers between devices: 33.2 us -> 30.4 us
    ppermute x22, starting transfers between devices: 33.2 us -> 30.4 us  [moved(): return lax.ppermute(block, ('cuts', 'blk'), pairs)]
  transfers between devices with their start and end apart: 22 -> 22, of which waited for: 11 -> 8; matrix products, arithmetic and copies ran while one was open for 0% -> 0% of each run, Pallas kernels for 11% -> 14%
where the time goes in v6:
time: 85 us; the launch traced here: 84.8 us
  waiting for transfers between devices  36.5 us (43%)
  starting transfers between devices  30.4 us (36%)
  Pallas kernels  13.5 us (16%)
  between operations  2.27 us (3%)
  local copies, waits for them, and re-layouts  2.12 us (2%)
    ppermute x22, waiting for transfers between devices, moved(): return lax.ppermute(block, ('cuts', 'blk'), pairs)  36.5 us
    ppermute x22, starting transfers between devices, moved(): return lax.ppermute(block, ('cuts', 'blk'), pairs)  30.4 us
    pallas_call x22, Pallas kernels, call(): pl.pallas_call(kernel, out_shape=[jax.ShapeDtypeStruct(shape, dtype) for...  12.1 us
    unnamed x4, local copies, waits for them, and re-layouts  2.12 us
  transfers between devices with their start and end apart: 22, of which 8 were waited for; matrix products, arithmetic and copies ran while one was open for 0% of the time, Pallas kernels for 14%

profile of v6, /device:TPU:1, one launch (start us, length us, event | category | flops | bytes accessed | tf_op | source)
XLA Modules:
  0.0 84.8 jit_solution(5100731580368917986)
XLA Ops:
  0.6 1.1 %copy-done.1 = f32[128,1152]{1,0:T(8,128)S(1)} copy-done((f32[128,1152]{1,0:T(8,128)S(1)}, f32[128,1152]{1,0:T(8,128)}, u32[]{:S(2)}) %copy-start.1) | copy-done | bytes 589848
  1.7 0.1 shard_map.60
  1.8 3.6 %collective-permute-start.1 = (f32[128,1152]{1,0:T(8,128)S(1)}, f32[128,1152]{1,0:T(8,128)S(1)}, u32[]{:S(2)}, u32[]{:S(2)}) collective-permute-start(f32[128,1152]{1,0:T(8,128)S(1)} %get-tuple-element.91.own.refs_1_.refs_0_.y), channel_id=1, source_target_pairs={{0,8},{1,137},{2,10},{3,139},{4,12},{5,141},{6,14},{7,143},{8,16},... | collective-permute-start | bytes 1769480 | tf_op jit(solution)/shard_map/ppermute | solution.py:27
  5.5 1.1 %copy-done = f32[128,1152]{1,0:T(8,128)S(1)} copy-done((f32[128,1152]{1,0:T(8,128)S(1)}, f32[128,1152]{1,0:T(8,128)}, u32[]{:S(2)}) %copy-start) | copy-done | bytes 589848
  6.5 0.1 shard_map.61
  6.7 0.1 collective-permute-start.2
  6.8 0.5 collective-permute-start.3
  7.3 1.7 %collective-permute-start = (f32[64,1152]{1,0:T(8,128)S(1)}, f32[64,1152]{1,0:T(8,128)S(1)}, u32[]{:S(2)}, u32[]{:S(2)}) collective-permute-start(f32[64,1152]{1,0:T(8,128)S(1)} %get-tuple-element.98.refs_0_.refs_2_), channel_id=1, source_target_pairs={{0,128},{1,129},{2,130},{3,131},{4,132},{5,133},{6,134},{7,135},{8... | collective-permute-start | bytes 884744 | tf_op jit(solution)/shard_map/ppermute | solution.py:27
  9.0 2.7 %collective-permute-start.9 = (f32[128,1152]{1,0:T(8,128)S(1)}, f32[128,1152]{1,0:T(8,128)S(1)}, u32[]{:S(2)}, u32[]{:S(2)}) collective-permute-start(f32[128,1152]{1,0:T(8,128)S(1)} %get-tuple-element.91.own.refs_1_.refs_0_.y), channel_id=1, source_target_pairs={{0,4},{1,5},{2,6},{3,7},{4,0},{5,1},{6,2},{7,3},{8,12},{9,13},{10,... | collective-permute-start | bytes 1769480 | tf_op jit(solution)/shard_map/ppermute | solution.py:27
  11.7 0.0 collective-permute-done.2.refs_2_
  11.8 0.0 collective-permute-done.3.refs_3_
  11.8 12.4 %collective-permute-done.1.last.refs_2_.refs_1_ = f32[128,1152]{1,0:T(8,128)S(1)} collective-permute-done((f32[128,1152]{1,0:T(8,128)S(1)}, f32[128,1152]{1,0:T(8,128)S(1)}, u32[]{:S(2)}, u32[]{:S(2)}) %collective-permute-start.1) | collective-permute-done | bytes 589856 | tf_op jit(solution)/shard_map/ppermute | solution.py:27
  24.1 0.1 shard_map.62
  24.3 1.3 %collective-permute-start.4 = (f32[128,1152]{1,0:T(8,128)S(1)}, f32[128,1152]{1,0:T(8,128)S(1)}, u32[]{:S(2)}, u32[]{:S(2)}) collective-permute-start(f32[128,1152]{1,0:T(8,128)S(1)} %get-tuple-element.90), channel_id=1, source_target_pairs={{0,2},{1,3},{2,4},{3,5},{4,6},{5,7},{6,0},{7,1},{8,10},{9,11},{10,... | collective-permute-start | bytes 1769480 | tf_op jit(solution)/shard_map/ppermute | solution.py:27
  25.6 1.5 %collective-permute-start.5 = (f32[128,1152]{1,0:T(8,128)S(1)}, f32[128,1152]{1,0:T(8,128)S(1)}, u32[]{:S(2)}, u32[]{:S(2)}) collective-permute-start(f32[128,1152]{1,0:T(8,128)S(1)} %get-tuple-element.92), channel_id=1, source_target_pairs={{0,6},{1,7},{2,0},{3,1},{4,2},{5,3},{6,4},{7,5},{8,14},{9,15},{10,... | collective-permute-start | bytes 1769480 | tf_op jit(solution)/shard_map/ppermute | solution.py:27
  27.0 0.0 collective-permute-done.refs_0_
  27.0 0.1 shard_map.63
  27.1 0.7 collective-permute-start.6
  27.8 2.3 %collective-permute-start.7 = (f32[64,1152]{1,0:T(8,128)S(1)}, f32[64,1152]{1,0:T(8,128)S(1)}, u32[]{:S(2)}, u32[]{:S(2)}) collective-permute-start(f32[64,1152]{1,0:T(8,128)S(1)} %collective-permute-done.refs_0_), channel_id=1, source_target_pairs={{0,1},{1,0},{2,3},{3,2},{4,5},{5,4},{6,7},{7,6},{8,9},{9,8},{10,11... | collective-permute-start | bytes 884744 | tf_op jit(solution)/shard_map/ppermute | solution.py:27
  30.1 0.0 collective-permute-done.9.two
  30.1 0.0 collective-permute-start.10
  31.4 0.2 shard_map.64
  31.6 1.7 %shard_map.65 = (f32[128,128]{1,0:T(8,128)S(1)}, f32[128,1152]{1,0:T(8,128)S(1)}, f32[128,128]{1,0:T(8,128)S(1)}, f32[128,1152]{1,0:T(8,128)S(1)}) custom-call(f32[8,128]{1,0:T(8,128)S(1)} %shard_map.59.refs_0_.params, f32[128,1152]{1,0:T(8,128)S(1)} %get-tuple-element.91.own.refs_1_.refs_0_.y, f32[128,1152]{1,0:T(8,128)S(1)} %collective-permute-done.1.last.refs_2_.refs_1_, ...), custom_call_target="tpu_custom_call" | custom-call | tf_op jit(solution)/shard_map/pallas_call | solution.py:244
  33.3 4.0 %collective-permute-done.6.refs_0_ = f32[64,1152]{1,0:T(8,128)S(1)} collective-permute-done((f32[64,1152]{1,0:T(8,128)S(1)}, f32[64,1152]{1,0:T(8,128)S(1)}, u32[]{:S(2)}, u32[]{:S(2)}) %collective-permute-start.6) | collective-permute-done | bytes 294944 | tf_op jit(solution)/shard_map/ppermute | solution.py:27
  37.3 0.0 collective-permute-done.7.refs_1_
  37.3 3.5 %collective-permute-done.4.refs_0_.refs_2_ = f32[128,1152]{1,0:T(8,128)S(1)} collective-permute-done((f32[128,1152]{1,0:T(8,128)S(1)}, f32[128,1152]{1,0:T(8,128)S(1)}, u32[]{:S(2)}, u32[]{:S(2)}) %collective-permute-start.4) | collective-permute-done | bytes 589856 | tf_op jit(solution)/shard_map/ppermute | solution.py:27
  40.9 0.0 collective-permute-done.5.refs_1_.refs_3_
  40.9 0.4 collective-permute-start.8
  41.3 1.2 %collective-permute-done.8.refs_2_ = f32[64,1152]{1,0:T(8,128)S(1)} collective-permute-done((f32[64,1152]{1,0:T(8,128)S(1)}, f32[64,1152]{1,0:T(8,128)S(1)}, u32[]{:S(2)}, u32[]{:S(2)}) %collective-permute-start.8) | collective-permute-done | bytes 294944 | tf_op jit(solution)/shard_map/ppermute | solution.py:27
  42.5 0.3 shard_map.66
  42.8 2.4 %shard_map.67 = (f32[256,512]{1,0:T(8,128)S(1)}, f32[128,1152]{1,0:T(8,128)S(1)}, f32[128,1152]{1,0:T(8,128)S(1)}) custom-call(f32[8,128]{1,0:T(8,128)S(1)} %shard_map.59.refs_0_.params, f32[128,1152]{1,0:T(8,128)S(1)} %collective-permute-done.4.refs_0_.refs_2_, f32[128,1152]{1,0:T(8,128)S(1)} %collective-permute-done.5.refs_1_.refs_3_, ...), custom_call_target="tpu_custom_call" | custom-call | flops 3000000000 | tf_op jit(solution)/shard_map/pallas_call | solution.py:244
  45.2 2.8 %collective-permute-start.12 = (f32[128,1152]{1,0:T(8,128)S(1)}, f32[128,1152]{1,0:T(8,128)S(1)}, u32[]{:S(2)}, u32[]{:S(2)}) collective-permute-start(f32[128,1152]{1,0:T(8,128)S(1)} %get-tuple-element.116), channel_id=1, source_target_pairs={{0,6},{1,7},{2,0},{3,1},{4,2},{5,3},{6,4},{7,5},{8,14},{9,15},{10,... | collective-permute-start | bytes 1769480 | tf_op jit(solution)/shard_map/ppermute | solution.py:27
  48.0 0.0 collective-permute-start.13
  48.0 0.0 collective-permute-done.10.two_last
  48.0 0.1 shard_map.68.refs_0_.refs_4_
  48.0 1.9 %shard_map.69 = (f32[128,512]{1,0:T(8,128)S(1)}, f32[128,1152]{1,0:T(8,128)S(1)}) custom-call(f32[8,128]{1,0:T(8,128)S(1)} %shard_map.59.refs_0_.params, f32[128,1152]{1,0:T(8,128)S(1)} %shard_map.68.refs_0_.refs_4_, bf16[512,1152]{1,0:T(8,128)(2,1)S(1)} %get-tuple-element.119.refs_2_.refs_1_.refs_3_, ...), custom_call_target="tpu_custom_call" | custom-call | tf_op jit(solution)/shard_map/pallas_call | solution.py:244
  50.0 2.3 %collective-permute-start.11 = (f32[128,1152]{1,0:T(8,128)S(1)}, f32[128,1152]{1,0:T(8,128)S(1)}, u32[]{:S(2)}, u32[]{:S(2)}) collective-permute-start(f32[128,1152]{1,0:T(8,128)S(1)} %get-tuple-element.140.two), channel_id=1, source_target_pairs={{0,120},{1,249},{2,122},{3,251},{4,124},{5,253},{6,126},{7,255},{8... | collective-permute-start | bytes 1769480 | tf_op jit(solution)/shard_map/ppermute | solution.py:27
  52.2 1.7 %shard_map.70 = (f32[128,128]{1,0:T(8,128)S(1)}, f32[128,1152]{1,0:T(8,128)S(1)}, f32[128,128]{1,0:T(8,128)S(1)}, f32[128,1152]{1,0:T(8,128)S(1)}) custom-call(f32[8,128]{1,0:T(8,128)S(1)} %shard_map.59.refs_0_.params, f32[128,1152]{1,0:T(8,128)S(1)} %get-tuple-element.91.own.refs_1_.refs_0_.y, f32[128,1152]{1,0:T(8,128)S(1)} %collective-permute-done.1.last.refs_2_.refs_1_, ...), custom_call_target="tpu_custom_call" | custom-call | tf_op jit(solution)/shard_map/pallas_call | solution.py:244
  53.9 1.4 %shard_map.71 = (f32[64,1152]{1,0:T(8,128)S(1)}, f32[64,1152]{1,0:T(8,128)S(1)}, f32[64,1152]{1,0:T(8,128)S(1)}, f32[64,1152]{1,0:T(8,128)S(1)}) custom-call(f32[128,1152]{1,0:T(8,128)S(1)} %get-tuple-element.91.own.refs_1_.refs_0_.y, f32[128,1152]{1,0:T(8,128)S(1)} %collective-permute-done.1.last.refs_2_.refs_1_, ...), custom_call_target="tpu_custom_call" | custom-call | tf_op jit(solution)/shard_map/pallas_call | solution.py:244
  55.3 0.8 collective-permute-start.17
  56.1 0.1 collective-permute-start.14
  56.2 1.1 %collective-permute-done.17.beside = f32[64,1152]{1,0:T(8,128)S(1)} collective-permute-done((f32[64,1152]{1,0:T(8,128)S(1)}, f32[64,1152]{1,0:T(8,128)S(1)}, u32[]{:S(2)}, u32[]{:S(2)}) %collective-permute-start.17) | collective-permute-done | bytes 294944 | tf_op jit(solution)/shard_map/ppermute | solution.py:27
  57.3 1.5 %collective-permute-start.18 = (f32[64,1152]{1,0:T(8,128)S(1)}, f32[64,1152]{1,0:T(8,128)S(1)}, u32[]{:S(2)}, u32[]{:S(2)}) collective-permute-start(f32[64,1152]{1,0:T(8,128)S(1)} %shard_map.76), channel_id=1, source_target_pairs={{0,128},{1,129},{2,130},{3,131},{4,132},{5,133},{6,134},{7,135},{8... | collective-permute-start | bytes 884744 | tf_op jit(solution)/shard_map/ppermute | solution.py:27
  58.8 1.4 %shard_map.72 = (f32[64,1152]{1,0:T(8,128)S(1)}, f32[64,1152]{1,0:T(8,128)S(1)}, f32[64,1152]{1,0:T(8,128)S(1)}, f32[64,1152]{1,0:T(8,128)S(1)}) custom-call(f32[128,1152]{1,0:T(8,128)S(1)} %get-tuple-element.91.own.refs_1_.refs_0_.y, f32[128,1152]{1,0:T(8,128)S(1)} %collective-permute-done.1.last.refs_2_.refs_1_, ...), custom_call_target="tpu_custom_call" | custom-call | tf_op jit(solution)/shard_map/pallas_call | solution.py:244
  60.2 0.0 collective-permute-done.14.beside
  60.2 0.0 collective-permute-done.12.back_1
  60.3 3.1 %collective-permute-done.13.back_3 = f32[128,1152]{1,0:T(8,128)S(1)} collective-permute-done((f32[128,1152]{1,0:T(8,128)S(1)}, f32[128,1152]{1,0:T(8,128)S(1)}, u32[]{:S(2)}, u32[]{:S(2)}) %collective-permute-start.13) | collective-permute-done | bytes 589856 | tf_op jit(solution)/shard_map/ppermute | solution.py:27
  63.4 0.1 shard_map.74
  63.5 2.3 %collective-permute-start.16 = (f32[128,1152]{1,0:T(8,128)S(1)}, f32[128,1152]{1,0:T(8,128)S(1)}, u32[]{:S(2)}, u32[]{:S(2)}) collective-permute-start(f32[128,1152]{1,0:T(8,128)S(1)} %shard_map.74), channel_id=1, source_target_pairs={{0,120},{1,249},{2,122},{3,251},{4,124},{5,253},{6,126},{7,255},{8... | collective-permute-start | bytes 1769480 | tf_op jit(solution)/shard_map/ppermute | solution.py:27
  65.8 0.0 collective-permute-done.11.two_last
  65.8 0.1 shard_map.75
  65.9 0.4 collective-permute-start.15
  66.2 2.5 %collective-permute-start.20 = (f32[64,1152]{1,0:T(8,128)S(1)}, f32[64,1152]{1,0:T(8,128)S(1)}, u32[]{:S(2)}, u32[]{:S(2)}) collective-permute-start(f32[64,1152]{1,0:T(8,128)S(1)} %get-tuple-element.149), channel_id=1, source_target_pairs={{0,1},{1,0},{2,3},{3,2},{4,5},{5,4},{6,7},{7,6},{8,9},{9,8},{10,11... | collective-permute-start | bytes 884744 | tf_op jit(solution)/shard_map/ppermute | solution.py:27
  68.8 1.7 %collective-permute-start.19 = (f32[64,1152]{1,0:T(8,128)S(1)}, f32[64,1152]{1,0:T(8,128)S(1)}, u32[]{:S(2)}, u32[]{:S(2)}) collective-permute-start(f32[64,1152]{1,0:T(8,128)S(1)} %shard_map.73), channel_id=1, source_target_pairs={{0,128},{1,129},{2,130},{3,131},{4,132},{5,133},{6,134},{7,135},{8... | collective-permute-start | bytes 884744 | tf_op jit(solution)/shard_map/ppermute | solution.py:27
  70.5 1.0 %collective-permute-done.18.three = f32[64,1152]{1,0:T(8,128)S(1)} collective-permute-done((f32[64,1152]{1,0:T(8,128)S(1)}, f32[64,1152]{1,0:T(8,128)S(1)}, u32[]{:S(2)}, u32[]{:S(2)}) %collective-permute-start.18) | collective-permute-done | bytes 294944 | tf_op jit(solution)/shard_map/ppermute | solution.py:27
  71.6 1.2 %collective-permute-start.21 = (f32[64,1152]{1,0:T(8,128)S(1)}, f32[64,1152]{1,0:T(8,128)S(1)}, u32[]{:S(2)}, u32[]{:S(2)}) collective-permute-start(f32[64,1152]{1,0:T(8,128)S(1)} %get-tuple-element.153), channel_id=1, source_target_pairs={{0,1},{1,0},{2,3},{3,2},{4,5},{5,4},{6,7},{7,6},{8,9},{9,8},{10,11... | collective-permute-start | bytes 884744 | tf_op jit(solution)/shard_map/ppermute | solution.py:27
  72.7 0.2 shard_map.77.here
  72.9 0.0 collective-permute-done.20.two
  72.9 0.1 shard_map.78.refs_5_
  73.0 10.1 %collective-permute-done.19.three = f32[64,1152]{1,0:T(8,128)S(1)} collective-permute-done((f32[64,1152]{1,0:T(8,128)S(1)}, f32[64,1152]{1,0:T(8,128)S(1)}, u32[]{:S(2)}, u32[]{:S(2)}) %collective-permute-start.19) | collective-permute-done | bytes 294944 | tf_op jit(solution)/shard_map/ppermute | solution.py:27
  83.1 0.0 collective-permute-done.21.two
  83.1 0.1 shard_map.79.refs_6_
  83.1 0.1 shard_map.80.refs_0_
  83.2 1.4 %shard_map.81 = (f32[128,1152]{1,0:T(8,128)}, f32[128,1152]{1,0:T(8,128)}) custom-call(f32[8,128]{1,0:T(8,128)S(1)} %shard_map.59.refs_0_.params, f32[128,1152]{1,0:T(8,128)S(1)} %get-tuple-element.91.own.refs_1_.refs_0_.y, f32[128,1]{1,0:T(8,128)S(1)} %get-tuple-element.83._.y_inv, f32[128,1152]{1,0:T(8,128)S(1)} %shard_map.80.refs_0_, ...), custom_call_target="tpu_custom_call" | custom-call | tf_op jit(solution)/shard_map/pallas_call | solution.py:257
  (7 shorter events, 0.1 us)
Async XLA Ops:
  0.6 1.1 %copy-start.1 = (f32[128,1152]{1,0:T(8,128)S(1)}, f32[128,1152]{1,0:T(8,128)}, u32[]{:S(2)}) copy-start(f32[128,1152]{1,0:T(8,128)} %in_ref.2) | copy-start | bytes 1769476
  1.8 22.3 %collective-permute-start.1 = (f32[128,1152]{1,0:T(8,128)S(1)}, f32[128,1152]{1,0:T(8,128)S(1)}, u32[]{:S(2)}, u32[]{:S(2)}) collective-permute-start(f32[128,1152]{1,0:T(8,128)S(1)} %get-tuple-element.91.own.refs_1_.refs_0_.y), channel_id=1, source_target_pairs={{0,8},{1,137},{2,10},{3,139},{4,12},{5,141},{6,14},{7,143},{8,16},... | collective-permute-start | bytes 1769480 | tf_op jit(solution)/shard_map/ppermute | solution.py:27
  5.5 1.1 %copy-start = (f32[128,1152]{1,0:T(8,128)S(1)}, f32[128,1152]{1,0:T(8,128)}, u32[]{:S(2)}) copy-start(f32[128,1152]{1,0:T(8,128)} %in_ref.3) | copy-start | bytes 1769476
  6.7 5.1 %collective-permute-start.2 = (f32[64,1152]{1,0:T(8,128)S(1)}, f32[64,1152]{1,0:T(8,128)S(1)}, u32[]{:S(2)}, u32[]{:S(2)}) collective-permute-start(f32[64,1152]{1,0:T(8,128)S(1)} %get-tuple-element.98.refs_0_.refs_2_), channel_id=1, source_target_pairs={{0,1},{1,0},{2,3},{3,2},{4,5},{5,4},{6,7},{7,6},{8,9},{9,8},{10,11... | collective-permute-start | bytes 884744 | tf_op jit(solution)/shard_map/ppermute | solution.py:27
  6.8 5.0 %collective-permute-start.3 = (f32[64,1152]{1,0:T(8,128)S(1)}, f32[64,1152]{1,0:T(8,128)S(1)}, u32[]{:S(2)}, u32[]{:S(2)}) collective-permute-start(f32[64,1152]{1,0:T(8,128)S(1)} %get-tuple-element.96.refs_1_.refs_3_), channel_id=1, source_target_pairs={{0,1},{1,0},{2,3},{3,2},{4,5},{5,4},{6,7},{7,6},{8,9},{9,8},{10,11... | collective-permute-start | bytes 884744 | tf_op jit(solution)/shard_map/ppermute | solution.py:27
  7.3 19.8 %collective-permute-start = (f32[64,1152]{1,0:T(8,128)S(1)}, f32[64,1152]{1,0:T(8,128)S(1)}, u32[]{:S(2)}, u32[]{:S(2)}) collective-permute-start(f32[64,1152]{1,0:T(8,128)S(1)} %get-tuple-element.98.refs_0_.refs_2_), channel_id=1, source_target_pairs={{0,128},{1,129},{2,130},{3,131},{4,132},{5,133},{6,134},{7,135},{8... | collective-permute-start | bytes 884744 | tf_op jit(solution)/shard_map/ppermute | solution.py:27
  9.0 21.1 %collective-permute-start.9 = (f32[128,1152]{1,0:T(8,128)S(1)}, f32[128,1152]{1,0:T(8,128)S(1)}, u32[]{:S(2)}, u32[]{:S(2)}) collective-permute-start(f32[128,1152]{1,0:T(8,128)S(1)} %get-tuple-element.91.own.refs_1_.refs_0_.y), channel_id=1, source_target_pairs={{0,4},{1,5},{2,6},{3,7},{4,0},{5,1},{6,2},{7,3},{8,12},{9,13},{10,... | collective-permute-start | bytes 1769480 | tf_op jit(solution)/shard_map/ppermute | solution.py:27
  24.3 16.6 %collective-permute-start.4 = (f32[128,1152]{1,0:T(8,128)S(1)}, f32[128,1152]{1,0:T(8,128)S(1)}, u32[]{:S(2)}, u32[]{:S(2)}) collective-permute-start(f32[128,1152]{1,0:T(8,128)S(1)} %get-tuple-element.90), channel_id=1, source_target_pairs={{0,2},{1,3},{2,4},{3,5},{4,6},{5,7},{6,0},{7,1},{8,10},{9,11},{10,... | collective-permute-start | bytes 1769480 | tf_op jit(solution)/shard_map/ppermute | solution.py:27
  25.6 15.3 %collective-permute-start.5 = (f32[128,1152]{1,0:T(8,128)S(1)}, f32[128,1152]{1,0:T(8,128)S(1)}, u32[]{:S(2)}, u32[]{:S(2)}) collective-permute-start(f32[128,1152]{1,0:T(8,128)S(1)} %get-tuple-element.92), channel_id=1, source_target_pairs={{0,6},{1,7},{2,0},{3,1},{4,2},{5,3},{6,4},{7,5},{8,14},{9,15},{10,... | collective-permute-start | bytes 1769480 | tf_op jit(solution)/shard_map/ppermute | solution.py:27
  27.1 10.3 %collective-permute-start.6 = (f32[64,1152]{1,0:T(8,128)S(1)}, f32[64,1152]{1,0:T(8,128)S(1)}, u32[]{:S(2)}, u32[]{:S(2)}) collective-permute-start(f32[64,1152]{1,0:T(8,128)S(1)} %get-tuple-element.96.refs_1_.refs_3_), channel_id=1, source_target_pairs={{0,128},{1,129},{2,130},{3,131},{4,132},{5,133},{6,134},{7,135},{8... | collective-permute-start | bytes 884744 | tf_op jit(solution)/shard_map/ppermute | solution.py:27
  27.8 9.6 %collective-permute-start.7 = (f32[64,1152]{1,0:T(8,128)S(1)}, f32[64,1152]{1,0:T(8,128)S(1)}, u32[]{:S(2)}, u32[]{:S(2)}) collective-permute-start(f32[64,1152]{1,0:T(8,128)S(1)} %collective-permute-done.refs_0_), channel_id=1, source_target_pairs={{0,1},{1,0},{2,3},{3,2},{4,5},{5,4},{6,7},{7,6},{8,9},{9,8},{10,11... | collective-permute-start | bytes 884744 | tf_op jit(solution)/shard_map/ppermute | solution.py:27
  30.1 17.8 %collective-permute-start.10 = (f32[128,1152]{1,0:T(8,128)S(1)}, f32[128,1152]{1,0:T(8,128)S(1)}, u32[]{:S(2)}, u32[]{:S(2)}) collective-permute-start(f32[128,1152]{1,0:T(8,128)S(1)} %collective-permute-done.9.two), channel_id=1, source_target_pairs={{0,8},{1,137},{2,10},{3,139},{4,12},{5,141},{6,14},{7,143},{8,16},... | collective-permute-start | bytes 1769480 | tf_op jit(solution)/shard_map/ppermute | solution.py:27
  40.9 1.6 %collective-permute-start.8 = (f32[64,1152]{1,0:T(8,128)S(1)}, f32[64,1152]{1,0:T(8,128)S(1)}, u32[]{:S(2)}, u32[]{:S(2)}) collective-permute-start(f32[64,1152]{1,0:T(8,128)S(1)} %collective-permute-done.6.refs_0_), channel_id=1, source_target_pairs={{0,1},{1,0},{2,3},{3,2},{4,5},{5,4},{6,7},{7,6},{8,9},{9,8},{10,11... | collective-permute-start | bytes 884744 | tf_op jit(solution)/shard_map/ppermute | solution.py:27
  45.2 15.1 %collective-permute-start.12 = (f32[128,1152]{1,0:T(8,128)S(1)}, f32[128,1152]{1,0:T(8,128)S(1)}, u32[]{:S(2)}, u32[]{:S(2)}) collective-permute-start(f32[128,1152]{1,0:T(8,128)S(1)} %get-tuple-element.116), channel_id=1, source_target_pairs={{0,6},{1,7},{2,0},{3,1},{4,2},{5,3},{6,4},{7,5},{8,14},{9,15},{10,... | collective-permute-start | bytes 1769480 | tf_op jit(solution)/shard_map/ppermute | solution.py:27
  48.0 15.4 %collective-permute-start.13 = (f32[128,1152]{1,0:T(8,128)S(1)}, f32[128,1152]{1,0:T(8,128)S(1)}, u32[]{:S(2)}, u32[]{:S(2)}) collective-permute-start(f32[128,1152]{1,0:T(8,128)S(1)} %get-tuple-element.117), channel_id=1, source_target_pairs={{0,2},{1,3},{2,4},{3,5},{4,6},{5,7},{6,0},{7,1},{8,10},{9,11},{10,... | collective-permute-start | bytes 1769480 | tf_op jit(solution)/shard_map/ppermute | solution.py:27
  50.0 15.8 %collective-permute-start.11 = (f32[128,1152]{1,0:T(8,128)S(1)}, f32[128,1152]{1,0:T(8,128)S(1)}, u32[]{:S(2)}, u32[]{:S(2)}) collective-permute-start(f32[128,1152]{1,0:T(8,128)S(1)} %get-tuple-element.140.two), channel_id=1, source_target_pairs={{0,120},{1,249},{2,122},{3,251},{4,124},{5,253},{6,126},{7,255},{8... | collective-permute-start | bytes 1769480 | tf_op jit(solution)/shard_map/ppermute | solution.py:27
  55.3 2.0 %collective-permute-start.17 = (f32[64,1152]{1,0:T(8,128)S(1)}, f32[64,1152]{1,0:T(8,128)S(1)}, u32[]{:S(2)}, u32[]{:S(2)}) collective-permute-start(f32[64,1152]{1,0:T(8,128)S(1)} %get-tuple-element.143), channel_id=1, source_target_pairs={{0,1},{1,0},{2,3},{3,2},{4,5},{5,4},{6,7},{7,6},{8,9},{9,8},{10,11... | collective-permute-start | bytes 884744 | tf_op jit(solution)/shard_map/ppermute | solution.py:27
  56.1 4.1 %collective-permute-start.14 = (f32[64,1152]{1,0:T(8,128)S(1)}, f32[64,1152]{1,0:T(8,128)S(1)}, u32[]{:S(2)}, u32[]{:S(2)}) collective-permute-start(f32[64,1152]{1,0:T(8,128)S(1)} %get-tuple-element.132), channel_id=1, source_target_pairs={{0,1},{1,0},{2,3},{3,2},{4,5},{5,4},{6,7},{7,6},{8,9},{9,8},{10,11... | collective-permute-start | bytes 884744 | tf_op jit(solution)/shard_map/ppermute | solution.py:27
  57.3 14.3 %collective-permute-start.18 = (f32[64,1152]{1,0:T(8,128)S(1)}, f32[64,1152]{1,0:T(8,128)S(1)}, u32[]{:S(2)}, u32[]{:S(2)}) collective-permute-start(f32[64,1152]{1,0:T(8,128)S(1)} %shard_map.76), channel_id=1, source_target_pairs={{0,128},{1,129},{2,130},{3,131},{4,132},{5,133},{6,134},{7,135},{8... | collective-permute-start | bytes 884744 | tf_op jit(solution)/shard_map/ppermute | solution.py:27
  63.5 19.6 %collective-permute-start.16 = (f32[128,1152]{1,0:T(8,128)S(1)}, f32[128,1152]{1,0:T(8,128)S(1)}, u32[]{:S(2)}, u32[]{:S(2)}) collective-permute-start(f32[128,1152]{1,0:T(8,128)S(1)} %shard_map.74), channel_id=1, source_target_pairs={{0,120},{1,249},{2,122},{3,251},{4,124},{5,253},{6,126},{7,255},{8... | collective-permute-start | bytes 1769480 | tf_op jit(solution)/shard_map/ppermute | solution.py:27
  65.9 17.4 %collective-permute-start.15 = (f32[128,1152]{1,0:T(8,128)S(1)}, f32[128,1152]{1,0:T(8,128)S(1)}, u32[]{:S(2)}, u32[]{:S(2)}) collective-permute-start(f32[128,1152]{1,0:T(8,128)S(1)} %shard_map.75), channel_id=1, source_target_pairs={{0,4},{1,5},{2,6},{3,7},{4,0},{5,1},{6,2},{7,3},{8,12},{9,13},{10,... | collective-permute-start | bytes 1769480 | tf_op jit(solution)/shard_map/ppermute | solution.py:27
  66.2 6.7 %collective-permute-start.20 = (f32[64,1152]{1,0:T(8,128)S(1)}, f32[64,1152]{1,0:T(8,128)S(1)}, u32[]{:S(2)}, u32[]{:S(2)}) collective-permute-start(f32[64,1152]{1,0:T(8,128)S(1)} %get-tuple-element.149), channel_id=1, source_target_pairs={{0,1},{1,0},{2,3},{3,2},{4,5},{5,4},{6,7},{7,6},{8,9},{9,8},{10,11... | collective-permute-start | bytes 884744 | tf_op jit(solution)/shard_map/ppermute | solution.py:27
  68.8 14.3 %collective-permute-start.19 = (f32[64,1152]{1,0:T(8,128)S(1)}, f32[64,1152]{1,0:T(8,128)S(1)}, u32[]{:S(2)}, u32[]{:S(2)}) collective-permute-start(f32[64,1152]{1,0:T(8,128)S(1)} %shard_map.73), channel_id=1, source_target_pairs={{0,128},{1,129},{2,130},{3,131},{4,132},{5,133},{6,134},{7,135},{8... | collective-permute-start | bytes 884744 | tf_op jit(solution)/shard_map/ppermute | solution.py:27
  71.6 11.5 %collective-permute-start.21 = (f32[64,1152]{1,0:T(8,128)S(1)}, f32[64,1152]{1,0:T(8,128)S(1)}, u32[]{:S(2)}, u32[]{:S(2)}) collective-permute-start(f32[64,1152]{1,0:T(8,128)S(1)} %get-tuple-element.153), channel_id=1, source_target_pairs={{0,1},{1,0},{2,3},{3,2},{4,5},{5,4},{6,7},{7,6},{8,9},{9,8},{10,11... | collective-permute-start | bytes 884744 | tf_op jit(solution)/shard_map/ppermute | solution.py:27

commit v7 on v6

--- a/solution.py
+++ b/solution.py
@@ -10,6 +10,7 @@
 W_ONE = 0
 W_HOP = 0
 W_CUT = 300_000_000
+W_ARRIVE = 1000_000_000
 W_FAR = 3000_000_000
 W_LAST = 0
 W_BACK = 0
@@ -199,6 +200,11 @@
 
 def add_three_kernel(one, two, three, out_ref):
     out_ref[...] = one[...] + two[...] + three[...]
+
+
+def copy_kernel(one, two, one_out, two_out):
+    one_out[...] = one[...]
+    two_out[...] = two[...]
 
 
 def add_kernel(here, beside, out_ref):
@@ -303,13 +309,13 @@
     kernel = lambda *refs: near_kernel(0, *refs)
     near = call(kernel, [square, block] * 2, *params, *arrays)
     ga_here, gya_here, ga_near, gya_near = near
-    y_1, y_3, x_cut_1, x_cut_beside_0, ga_here = together(
-        y_1, y_3, x_cut_1, x_cut_beside_0, ga_here
-    )
+    x_cut_1, x_cut_beside_0, ga_here = together(x_cut_1, x_cut_beside_0, ga_here)
 
     x_cut_beside_1 = moved(x_cut_1, other_core)
     images = (x_cut_1, x_cut_beside_0, x_cut_beside_1)
     outs = [((4 * rows, width), bf16)] * 2
+    y_1, y_3 = call(copy_kernel, [block] * 2, y_1, y_3, weight=W_ARRIVE)
+    y_1, y_3, xa_high = together(y_1, y_3, xa_high)
     x_high, x_low = call(join_kernel, outs, xa_high, xa_low, xc_high, xc_low, *images)
     outs = [((2 * rows, 4 * rows), f32)] + [block] * 2
     arrays = (*params, y_1, y_3, x_high, x_low)

time: 85 us -> 84 us (0.988)
  waiting for transfers between devices: 36.5 us -> 34.2 us
  starting transfers between devices: 30.4 us -> 31.6 us
    ppermute x22, waiting for transfers between devices: 36.5 us -> 34.2 us  [moved(): return lax.ppermute(block, ('cuts', 'blk'), pairs)]
    ppermute x22, starting transfers between devices: 30.4 us -> 31.6 us  [moved(): return lax.ppermute(block, ('cuts', 'blk'), pairs)]
    pallas_call x22 -> x23, Pallas kernels: 12.1 us -> 12.2 us  [call(): pl.pallas_call(kernel, out_shape=[jax.ShapeDtypeStruct(shape, dtype) for...]
where the time goes in v7:
time: 84 us; the launch traced here: 83.8 us
  waiting for transfers between devices  34.2 us (41%)
  starting transfers between devices  31.6 us (38%)
  Pallas kernels  13.6 us (16%)
  between operations  2.3 us (3%)
  local copies, waits for them, and re-layouts  2.12 us (3%)
    ppermute x22, waiting for transfers between devices, moved(): return lax.ppermute(block, ('cuts', 'blk'), pairs)  34.2 us
    ppermute x22, starting transfers between devices, moved(): return lax.ppermute(block, ('cuts', 'blk'), pairs)  31.6 us
    pallas_call x23, Pallas kernels, call(): pl.pallas_call(kernel, out_shape=[jax.ShapeDtypeStruct(shape, dtype) for...  12.2 us
    unnamed x4, local copies, waits for them, and re-layouts  2.12 us
  transfers between devices with their start and end apart: 22, of which 8 were waited for; matrix products, arithmetic and copies ran while one was open for 0% of the time, Pallas kernels for 14%

profile of v7, /device:TPU:1, one launch (start us, length us, event | category | flops | bytes accessed | tf_op | source)
XLA Modules:
  0.0 83.8 jit_solution(11896260182203538714)
XLA Ops:
  0.6 1.1 %copy-done.1 = f32[128,1152]{1,0:T(8,128)S(1)} copy-done((f32[128,1152]{1,0:T(8,128)S(1)}, f32[128,1152]{1,0:T(8,128)}, u32[]{:S(2)}) %copy-start.1) | copy-done | bytes 589848
  1.7 0.1 shard_map.60
  1.8 3.6 %collective-permute-start.1 = (f32[128,1152]{1,0:T(8,128)S(1)}, f32[128,1152]{1,0:T(8,128)S(1)}, u32[]{:S(2)}, u32[]{:S(2)}) collective-permute-start(f32[128,1152]{1,0:T(8,128)S(1)} %get-tuple-element.94.own.refs_1_.refs_0_.y), channel_id=1, source_target_pairs={{0,8},{1,137},{2,10},{3,139},{4,12},{5,141},{6,14},{7,143},{8,16},... | collective-permute-start | bytes 1769480 | tf_op jit(solution)/shard_map/ppermute | solution.py:28
  5.5 1.1 %copy-done = f32[128,1152]{1,0:T(8,128)S(1)} copy-done((f32[128,1152]{1,0:T(8,128)S(1)}, f32[128,1152]{1,0:T(8,128)}, u32[]{:S(2)}) %copy-start) | copy-done | bytes 589848
  6.5 0.1 shard_map.61
  6.7 0.1 collective-permute-start.2
  6.8 0.5 collective-permute-start.3
  7.3 1.7 %collective-permute-start = (f32[64,1152]{1,0:T(8,128)S(1)}, f32[64,1152]{1,0:T(8,128)S(1)}, u32[]{:S(2)}, u32[]{:S(2)}) collective-permute-start(f32[64,1152]{1,0:T(8,128)S(1)} %get-tuple-element.98.refs_0_.refs_2_), channel_id=1, source_target_pairs={{0,128},{1,129},{2,130},{3,131},{4,132},{5,133},{6,134},{7,135},{8... | collective-permute-start | bytes 884744 | tf_op jit(solution)/shard_map/ppermute | solution.py:28
  9.0 2.7 %collective-permute-start.9 = (f32[128,1152]{1,0:T(8,128)S(1)}, f32[128,1152]{1,0:T(8,128)S(1)}, u32[]{:S(2)}, u32[]{:S(2)}) collective-permute-start(f32[128,1152]{1,0:T(8,128)S(1)} %get-tuple-element.94.own.refs_1_.refs_0_.y), channel_id=1, source_target_pairs={{0,4},{1,5},{2,6},{3,7},{4,0},{5,1},{6,2},{7,3},{8,12},{9,13},{10,... | collective-permute-start | bytes 1769480 | tf_op jit(solution)/shard_map/ppermute | solution.py:28
  11.7 0.0 collective-permute-done.2.refs_2_
  11.8 0.0 collective-permute-done.3.refs_3_
  11.8 12.4 %collective-permute-done.1.last.refs_2_.refs_1_ = f32[128,1152]{1,0:T(8,128)S(1)} collective-permute-done((f32[128,1152]{1,0:T(8,128)S(1)}, f32[128,1152]{1,0:T(8,128)S(1)}, u32[]{:S(2)}, u32[]{:S(2)}) %collective-permute-start.1) | collective-permute-done | bytes 589856 | tf_op jit(solution)/shard_map/ppermute | solution.py:28
  24.1 0.1 shard_map.62
  24.3 1.3 %collective-permute-start.4 = (f32[128,1152]{1,0:T(8,128)S(1)}, f32[128,1152]{1,0:T(8,128)S(1)}, u32[]{:S(2)}, u32[]{:S(2)}) collective-permute-start(f32[128,1152]{1,0:T(8,128)S(1)} %get-tuple-element.93), channel_id=1, source_target_pairs={{0,2},{1,3},{2,4},{3,5},{4,6},{5,7},{6,0},{7,1},{8,10},{9,11},{10,... | collective-permute-start | bytes 1769480 | tf_op jit(solution)/shard_map/ppermute | solution.py:28
  25.6 1.5 %collective-permute-start.5 = (f32[128,1152]{1,0:T(8,128)S(1)}, f32[128,1152]{1,0:T(8,128)S(1)}, u32[]{:S(2)}, u32[]{:S(2)}) collective-permute-start(f32[128,1152]{1,0:T(8,128)S(1)} %get-tuple-element.95), channel_id=1, source_target_pairs={{0,6},{1,7},{2,0},{3,1},{4,2},{5,3},{6,4},{7,5},{8,14},{9,15},{10,... | collective-permute-start | bytes 1769480 | tf_op jit(solution)/shard_map/ppermute | solution.py:28
  27.0 0.0 collective-permute-done.refs_0_
  27.0 0.1 shard_map.64
  27.1 0.7 collective-permute-start.6
  27.8 2.3 %collective-permute-start.7 = (f32[64,1152]{1,0:T(8,128)S(1)}, f32[64,1152]{1,0:T(8,128)S(1)}, u32[]{:S(2)}, u32[]{:S(2)}) collective-permute-start(f32[64,1152]{1,0:T(8,128)S(1)} %collective-permute-done.refs_0_), channel_id=1, source_target_pairs={{0,1},{1,0},{2,3},{3,2},{4,5},{5,4},{6,7},{7,6},{8,9},{9,8},{10,11... | collective-permute-start | bytes 884744 | tf_op jit(solution)/shard_map/ppermute | solution.py:28
  30.1 0.0 collective-permute-done.9.two
  30.1 0.0 collective-permute-start.10
  31.4 0.2 shard_map.65
  31.6 1.7 %shard_map.66 = (f32[128,128]{1,0:T(8,128)S(1)}, f32[128,1152]{1,0:T(8,128)S(1)}, f32[128,128]{1,0:T(8,128)S(1)}, f32[128,1152]{1,0:T(8,128)S(1)}) custom-call(f32[8,128]{1,0:T(8,128)S(1)} %shard_map.59.refs_0_.params, f32[128,1152]{1,0:T(8,128)S(1)} %get-tuple-element.94.own.refs_1_.refs_0_.y, f32[128,1152]{1,0:T(8,128)S(1)} %collective-permute-done.1.last.refs_2_.refs_1_, ...), custom_call_target="tpu_custom_call" | custom-call | tf_op jit(solution)/shard_map/pallas_call | solution.py:250
  33.3 4.0 %collective-permute-done.6.refs_0_ = f32[64,1152]{1,0:T(8,128)S(1)} collective-permute-done((f32[64,1152]{1,0:T(8,128)S(1)}, f32[64,1152]{1,0:T(8,128)S(1)}, u32[]{:S(2)}, u32[]{:S(2)}) %collective-permute-start.6) | collective-permute-done | bytes 294944 | tf_op jit(solution)/shard_map/ppermute | solution.py:28
  37.3 0.0 collective-permute-done.7.refs_1_
  37.3 1.6 %collective-permute-start.8 = (f32[64,1152]{1,0:T(8,128)S(1)}, f32[64,1152]{1,0:T(8,128)S(1)}, u32[]{:S(2)}, u32[]{:S(2)}) collective-permute-start(f32[64,1152]{1,0:T(8,128)S(1)} %collective-permute-done.6.refs_0_), channel_id=1, source_target_pairs={{0,1},{1,0},{2,3},{3,2},{4,5},{5,4},{6,7},{7,6},{8,9},{9,8},{10,11... | collective-permute-start | bytes 884744 | tf_op jit(solution)/shard_map/ppermute | solution.py:28
  39.0 1.9 %collective-permute-done.4.one = f32[128,1152]{1,0:T(8,128)S(1)} collective-permute-done((f32[128,1152]{1,0:T(8,128)S(1)}, f32[128,1152]{1,0:T(8,128)S(1)}, u32[]{:S(2)}, u32[]{:S(2)}) %collective-permute-start.4) | collective-permute-done | bytes 589856 | tf_op jit(solution)/shard_map/ppermute | solution.py:28
  40.9 0.0 collective-permute-done.5.two
  40.9 0.1 shard_map.63
  41.0 0.0 collective-permute-done.8.refs_2_
  41.0 0.3 shard_map.67
  41.2 2.4 %shard_map.68 = (f32[256,512]{1,0:T(8,128)S(1)}, f32[128,1152]{1,0:T(8,128)S(1)}, f32[128,1152]{1,0:T(8,128)S(1)}) custom-call(f32[8,128]{1,0:T(8,128)S(1)} %shard_map.59.refs_0_.params, f32[128,1152]{1,0:T(8,128)S(1)} %get-tuple-element.131.refs_0_.refs_2_, f32[128,1152]{1,0:T(8,128)S(1)} %get-tuple-element.132.refs_1_.refs_3_, ...), custom_call_target="tpu_custom_call" | custom-call | flops 3000000000 | tf_op jit(solution)/shard_map/pallas_call | solution.py:250
  43.7 2.5 %collective-permute-start.12 = (f32[128,1152]{1,0:T(8,128)S(1)}, f32[128,1152]{1,0:T(8,128)S(1)}, u32[]{:S(2)}, u32[]{:S(2)}) collective-permute-start(f32[128,1152]{1,0:T(8,128)S(1)} %get-tuple-element.122), channel_id=1, source_target_pairs={{0,6},{1,7},{2,0},{3,1},{4,2},{5,3},{6,4},{7,5},{8,14},{9,15},{10,... | collective-permute-start | bytes 1769480 | tf_op jit(solution)/shard_map/ppermute | solution.py:28
  46.1 0.0 collective-permute-start.13
  46.1 1.0 %collective-permute-done.10.two_last = f32[128,1152]{1,0:T(8,128)S(1)} collective-permute-done((f32[128,1152]{1,0:T(8,128)S(1)}, f32[128,1152]{1,0:T(8,128)S(1)}, u32[]{:S(2)}, u32[]{:S(2)}) %collective-permute-start.10) | collective-permute-done | bytes 589856 | tf_op jit(solution)/shard_map/ppermute | solution.py:28
  47.1 0.1 shard_map.69.refs_0_.refs_4_
  47.2 1.9 %shard_map.70 = (f32[128,512]{1,0:T(8,128)S(1)}, f32[128,1152]{1,0:T(8,128)S(1)}) custom-call(f32[8,128]{1,0:T(8,128)S(1)} %shard_map.59.refs_0_.params, f32[128,1152]{1,0:T(8,128)S(1)} %shard_map.69.refs_0_.refs_4_, bf16[512,1152]{1,0:T(8,128)(2,1)S(1)} %get-tuple-element.125.refs_2_.refs_1_.refs_3_, ...), custom_call_target="tpu_custom_call" | custom-call | tf_op jit(solution)/shard_map/pallas_call | solution.py:250
  49.1 1.6 %collective-permute-start.11 = (f32[128,1152]{1,0:T(8,128)S(1)}, f32[128,1152]{1,0:T(8,128)S(1)}, u32[]{:S(2)}, u32[]{:S(2)}) collective-permute-start(f32[128,1152]{1,0:T(8,128)S(1)} %get-tuple-element.146.two), channel_id=1, source_target_pairs={{0,120},{1,249},{2,122},{3,251},{4,124},{5,253},{6,126},{7,255},{8... | collective-permute-start | bytes 1769480 | tf_op jit(solution)/shard_map/ppermute | solution.py:28
  50.7 1.7 %shard_map.71 = (f32[128,128]{1,0:T(8,128)S(1)}, f32[128,1152]{1,0:T(8,128)S(1)}, f32[128,128]{1,0:T(8,128)S(1)}, f32[128,1152]{1,0:T(8,128)S(1)}) custom-call(f32[8,128]{1,0:T(8,128)S(1)} %shard_map.59.refs_0_.params, f32[128,1152]{1,0:T(8,128)S(1)} %get-tuple-element.94.own.refs_1_.refs_0_.y, f32[128,1152]{1,0:T(8,128)S(1)} %collective-permute-done.1.last.refs_2_.refs_1_, ...), custom_call_target="tpu_custom_call" | custom-call | tf_op jit(solution)/shard_map/pallas_call | solution.py:250
  52.4 1.4 %shard_map.72 = (f32[64,1152]{1,0:T(8,128)S(1)}, f32[64,1152]{1,0:T(8,128)S(1)}, f32[64,1152]{1,0:T(8,128)S(1)}, f32[64,1152]{1,0:T(8,128)S(1)}) custom-call(f32[128,1152]{1,0:T(8,128)S(1)} %get-tuple-element.94.own.refs_1_.refs_0_.y, f32[128,1152]{1,0:T(8,128)S(1)} %collective-permute-done.1.last.refs_2_.refs_1_, ...), custom_call_target="tpu_custom_call" | custom-call | tf_op jit(solution)/shard_map/pallas_call | solution.py:250
  53.7 2.3 %collective-permute-start.17 = (f32[64,1152]{1,0:T(8,128)S(1)}, f32[64,1152]{1,0:T(8,128)S(1)}, u32[]{:S(2)}, u32[]{:S(2)}) collective-permute-start(f32[64,1152]{1,0:T(8,128)S(1)} %get-tuple-element.149), channel_id=1, source_target_pairs={{0,1},{1,0},{2,3},{3,2},{4,5},{5,4},{6,7},{7,6},{8,9},{9,8},{10,11... | collective-permute-start | bytes 884744 | tf_op jit(solution)/shard_map/ppermute | solution.py:28
  56.1 0.1 collective-permute-start.14
  56.2 1.1 %collective-permute-done.17.beside = f32[64,1152]{1,0:T(8,128)S(1)} collective-permute-done((f32[64,1152]{1,0:T(8,128)S(1)}, f32[64,1152]{1,0:T(8,128)S(1)}, u32[]{:S(2)}, u32[]{:S(2)}) %collective-permute-start.17) | collective-permute-done | bytes 294944 | tf_op jit(solution)/shard_map/ppermute | solution.py:28
  57.3 0.1 collective-permute-start.18
  57.4 1.4 %shard_map.73 = (f32[64,1152]{1,0:T(8,128)S(1)}, f32[64,1152]{1,0:T(8,128)S(1)}, f32[64,1152]{1,0:T(8,128)S(1)}, f32[64,1152]{1,0:T(8,128)S(1)}) custom-call(f32[128,1152]{1,0:T(8,128)S(1)} %get-tuple-element.94.own.refs_1_.refs_0_.y, f32[128,1152]{1,0:T(8,128)S(1)} %collective-permute-done.1.last.refs_2_.refs_1_, ...), custom_call_target="tpu_custom_call" | custom-call | tf_op jit(solution)/shard_map/pallas_call | solution.py:250
  58.8 0.0 collective-permute-done.14.beside
  58.9 2.3 %collective-permute-done.13.back_3 = f32[128,1152]{1,0:T(8,128)S(1)} collective-permute-done((f32[128,1152]{1,0:T(8,128)S(1)}, f32[128,1152]{1,0:T(8,128)S(1)}, u32[]{:S(2)}, u32[]{:S(2)}) %collective-permute-start.13) | collective-permute-done | bytes 589856 | tf_op jit(solution)/shard_map/ppermute | solution.py:28
  61.2 0.1 shard_map.75
  61.3 2.9 %collective-permute-start.16 = (f32[128,1152]{1,0:T(8,128)S(1)}, f32[128,1152]{1,0:T(8,128)S(1)}, u32[]{:S(2)}, u32[]{:S(2)}) collective-permute-start(f32[128,1152]{1,0:T(8,128)S(1)} %shard_map.75), channel_id=1, source_target_pairs={{0,120},{1,249},{2,122},{3,251},{4,124},{5,253},{6,126},{7,255},{8... | collective-permute-start | bytes 1769480 | tf_op jit(solution)/shard_map/ppermute | solution.py:28
  64.2 0.1 shard_map.76
  64.3 0.1 collective-permute-start.15
  64.4 2.8 %collective-permute-start.20 = (f32[64,1152]{1,0:T(8,128)S(1)}, f32[64,1152]{1,0:T(8,128)S(1)}, u32[]{:S(2)}, u32[]{:S(2)}) collective-permute-start(f32[64,1152]{1,0:T(8,128)S(1)} %get-tuple-element.155), channel_id=1, source_target_pairs={{0,1},{1,0},{2,3},{3,2},{4,5},{5,4},{6,7},{7,6},{8,9},{9,8},{10,11... | collective-permute-start | bytes 884744 | tf_op jit(solution)/shard_map/ppermute | solution.py:28
  67.2 1.2 %collective-permute-start.19 = (f32[64,1152]{1,0:T(8,128)S(1)}, f32[64,1152]{1,0:T(8,128)S(1)}, u32[]{:S(2)}, u32[]{:S(2)}) collective-permute-start(f32[64,1152]{1,0:T(8,128)S(1)} %shard_map.74), channel_id=1, source_target_pairs={{0,128},{1,129},{2,130},{3,131},{4,132},{5,133},{6,134},{7,135},{8... | collective-permute-start | bytes 884744 | tf_op jit(solution)/shard_map/ppermute | solution.py:28
  68.4 3.5 %collective-permute-done.18.three = f32[64,1152]{1,0:T(8,128)S(1)} collective-permute-done((f32[64,1152]{1,0:T(8,128)S(1)}, f32[64,1152]{1,0:T(8,128)S(1)}, u32[]{:S(2)}, u32[]{:S(2)}) %collective-permute-start.18) | collective-permute-done | bytes 294944 | tf_op jit(solution)/shard_map/ppermute | solution.py:28
  71.9 1.9 %collective-permute-start.21 = (f32[64,1152]{1,0:T(8,128)S(1)}, f32[64,1152]{1,0:T(8,128)S(1)}, u32[]{:S(2)}, u32[]{:S(2)}) collective-permute-start(f32[64,1152]{1,0:T(8,128)S(1)} %get-tuple-element.159), channel_id=1, source_target_pairs={{0,1},{1,0},{2,3},{3,2},{4,5},{5,4},{6,7},{7,6},{8,9},{9,8},{10,11... | collective-permute-start | bytes 884744 | tf_op jit(solution)/shard_map/ppermute | solution.py:28
  73.9 0.2 shard_map.78.here
  74.1 0.0 collective-permute-done.20.two
  74.1 0.1 shard_map.79.refs_5_
  74.1 7.9 %collective-permute-done.19.three = f32[64,1152]{1,0:T(8,128)S(1)} collective-permute-done((f32[64,1152]{1,0:T(8,128)S(1)}, f32[64,1152]{1,0:T(8,128)S(1)}, u32[]{:S(2)}, u32[]{:S(2)}) %collective-permute-start.19) | collective-permute-done | bytes 294944 | tf_op jit(solution)/shard_map/ppermute | solution.py:28
  82.1 0.1 shard_map.80.refs_6_
  82.1 0.0 collective-permute-done.16.beside
  82.1 0.1 shard_map.81.refs_0_
  82.2 0.0 collective-permute-done.15.refs_1_
  82.2 1.4 %shard_map.82 = (f32[128,1152]{1,0:T(8,128)}, f32[128,1152]{1,0:T(8,128)}) custom-call(f32[8,128]{1,0:T(8,128)S(1)} %shard_map.59.refs_0_.params, f32[128,1152]{1,0:T(8,128)S(1)} %get-tuple-element.94.own.refs_1_.refs_0_.y, f32[128,1]{1,0:T(8,128)S(1)} %get-tuple-element.86._.y_inv, f32[128,1152]{1,0:T(8,128)S(1)} %shard_map.81.refs_0_, ...), custom_call_target="tpu_custom_call" | custom-call | tf_op jit(solution)/shard_map/pallas_call | solution.py:263
  (8 shorter events, 0.1 us)
Async XLA Ops:
  0.6 1.1 %copy-start.1 = (f32[128,1152]{1,0:T(8,128)S(1)}, f32[128,1152]{1,0:T(8,128)}, u32[]{:S(2)}) copy-start(f32[128,1152]{1,0:T(8,128)} %in_ref.2) | copy-start | bytes 1769476
  1.8 22.3 %collective-permute-start.1 = (f32[128,1152]{1,0:T(8,128)S(1)}, f32[128,1152]{1,0:T(8,128)S(1)}, u32[]{:S(2)}, u32[]{:S(2)}) collective-permute-start(f32[128,1152]{1,0:T(8,128)S(1)} %get-tuple-element.94.own.refs_1_.refs_0_.y), channel_id=1, source_target_pairs={{0,8},{1,137},{2,10},{3,139},{4,12},{5,141},{6,14},{7,143},{8,16},... | collective-permute-start | bytes 1769480 | tf_op jit(solution)/shard_map/ppermute | solution.py:28
  5.5 1.1 %copy-start = (f32[128,1152]{1,0:T(8,128)S(1)}, f32[128,1152]{1,0:T(8,128)}, u32[]{:S(2)}) copy-start(f32[128,1152]{1,0:T(8,128)} %in_ref.3) | copy-start | bytes 1769476
  6.7 5.1 %collective-permute-start.2 = (f32[64,1152]{1,0:T(8,128)S(1)}, f32[64,1152]{1,0:T(8,128)S(1)}, u32[]{:S(2)}, u32[]{:S(2)}) collective-permute-start(f32[64,1152]{1,0:T(8,128)S(1)} %get-tuple-element.98.refs_0_.refs_2_), channel_id=1, source_target_pairs={{0,1},{1,0},{2,3},{3,2},{4,5},{5,4},{6,7},{7,6},{8,9},{9,8},{10,11... | collective-permute-start | bytes 884744 | tf_op jit(solution)/shard_map/ppermute | solution.py:28
  6.8 5.0 %collective-permute-start.3 = (f32[64,1152]{1,0:T(8,128)S(1)}, f32[64,1152]{1,0:T(8,128)S(1)}, u32[]{:S(2)}, u32[]{:S(2)}) collective-permute-start(f32[64,1152]{1,0:T(8,128)S(1)} %get-tuple-element.102.refs_1_.refs_3_), channel_id=1, source_target_pairs={{0,1},{1,0},{2,3},{3,2},{4,5},{5,4},{6,7},{7,6},{8,9},{9,8},{10,11... | collective-permute-start | bytes 884744 | tf_op jit(solution)/shard_map/ppermute | solution.py:28
  7.3 19.8 %collective-permute-start = (f32[64,1152]{1,0:T(8,128)S(1)}, f32[64,1152]{1,0:T(8,128)S(1)}, u32[]{:S(2)}, u32[]{:S(2)}) collective-permute-start(f32[64,1152]{1,0:T(8,128)S(1)} %get-tuple-element.98.refs_0_.refs_2_), channel_id=1, source_target_pairs={{0,128},{1,129},{2,130},{3,131},{4,132},{5,133},{6,134},{7,135},{8... | collective-permute-start | bytes 884744 | tf_op jit(solution)/shard_map/ppermute | solution.py:28
  9.0 21.1 %collective-permute-start.9 = (f32[128,1152]{1,0:T(8,128)S(1)}, f32[128,1152]{1,0:T(8,128)S(1)}, u32[]{:S(2)}, u32[]{:S(2)}) collective-permute-start(f32[128,1152]{1,0:T(8,128)S(1)} %get-tuple-element.94.own.refs_1_.refs_0_.y), channel_id=1, source_target_pairs={{0,4},{1,5},{2,6},{3,7},{4,0},{5,1},{6,2},{7,3},{8,12},{9,13},{10,... | collective-permute-start | bytes 1769480 | tf_op jit(solution)/shard_map/ppermute | solution.py:28
  24.3 16.6 %collective-permute-start.4 = (f32[128,1152]{1,0:T(8,128)S(1)}, f32[128,1152]{1,0:T(8,128)S(1)}, u32[]{:S(2)}, u32[]{:S(2)}) collective-permute-start(f32[128,1152]{1,0:T(8,128)S(1)} %get-tuple-element.93), channel_id=1, source_target_pairs={{0,2},{1,3},{2,4},{3,5},{4,6},{5,7},{6,0},{7,1},{8,10},{9,11},{10,... | collective-permute-start | bytes 1769480 | tf_op jit(solution)/shard_map/ppermute | solution.py:28
  25.6 15.3 %collective-permute-start.5 = (f32[128,1152]{1,0:T(8,128)S(1)}, f32[128,1152]{1,0:T(8,128)S(1)}, u32[]{:S(2)}, u32[]{:S(2)}) collective-permute-start(f32[128,1152]{1,0:T(8,128)S(1)} %get-tuple-element.95), channel_id=1, source_target_pairs={{0,6},{1,7},{2,0},{3,1},{4,2},{5,3},{6,4},{7,5},{8,14},{9,15},{10,... | collective-permute-start | bytes 1769480 | tf_op jit(solution)/shard_map/ppermute | solution.py:28
  27.1 10.3 %collective-permute-start.6 = (f32[64,1152]{1,0:T(8,128)S(1)}, f32[64,1152]{1,0:T(8,128)S(1)}, u32[]{:S(2)}, u32[]{:S(2)}) collective-permute-start(f32[64,1152]{1,0:T(8,128)S(1)} %get-tuple-element.102.refs_1_.refs_3_), channel_id=1, source_target_pairs={{0,128},{1,129},{2,130},{3,131},{4,132},{5,133},{6,134},{7,135},{8... | collective-permute-start | bytes 884744 | tf_op jit(solution)/shard_map/ppermute | solution.py:28
  27.8 9.6 %collective-permute-start.7 = (f32[64,1152]{1,0:T(8,128)S(1)}, f32[64,1152]{1,0:T(8,128)S(1)}, u32[]{:S(2)}, u32[]{:S(2)}) collective-permute-start(f32[64,1152]{1,0:T(8,128)S(1)} %collective-permute-done.refs_0_), channel_id=1, source_target_pairs={{0,1},{1,0},{2,3},{3,2},{4,5},{5,4},{6,7},{7,6},{8,9},{9,8},{10,11... | collective-permute-start | bytes 884744 | tf_op jit(solution)/shard_map/ppermute | solution.py:28
  30.1 17.0 %collective-permute-start.10 = (f32[128,1152]{1,0:T(8,128)S(1)}, f32[128,1152]{1,0:T(8,128)S(1)}, u32[]{:S(2)}, u32[]{:S(2)}) collective-permute-start(f32[128,1152]{1,0:T(8,128)S(1)} %collective-permute-done.9.two), channel_id=1, source_target_pairs={{0,8},{1,137},{2,10},{3,139},{4,12},{5,141},{6,14},{7,143},{8,16},... | collective-permute-start | bytes 1769480 | tf_op jit(solution)/shard_map/ppermute | solution.py:28
  37.3 3.6 %collective-permute-start.8 = (f32[64,1152]{1,0:T(8,128)S(1)}, f32[64,1152]{1,0:T(8,128)S(1)}, u32[]{:S(2)}, u32[]{:S(2)}) collective-permute-start(f32[64,1152]{1,0:T(8,128)S(1)} %collective-permute-done.6.refs_0_), channel_id=1, source_target_pairs={{0,1},{1,0},{2,3},{3,2},{4,5},{5,4},{6,7},{7,6},{8,9},{9,8},{10,11... | collective-permute-start | bytes 884744 | tf_op jit(solution)/shard_map/ppermute | solution.py:28
  43.7 15.2 %collective-permute-start.12 = (f32[128,1152]{1,0:T(8,128)S(1)}, f32[128,1152]{1,0:T(8,128)S(1)}, u32[]{:S(2)}, u32[]{:S(2)}) collective-permute-start(f32[128,1152]{1,0:T(8,128)S(1)} %get-tuple-element.122), channel_id=1, source_target_pairs={{0,6},{1,7},{2,0},{3,1},{4,2},{5,3},{6,4},{7,5},{8,14},{9,15},{10,... | collective-permute-start | bytes 1769480 | tf_op jit(solution)/shard_map/ppermute | solution.py:28
  46.1 15.1 %collective-permute-start.13 = (f32[128,1152]{1,0:T(8,128)S(1)}, f32[128,1152]{1,0:T(8,128)S(1)}, u32[]{:S(2)}, u32[]{:S(2)}) collective-permute-start(f32[128,1152]{1,0:T(8,128)S(1)} %get-tuple-element.123), channel_id=1, source_target_pairs={{0,2},{1,3},{2,4},{3,5},{4,6},{5,7},{6,0},{7,1},{8,10},{9,11},{10,... | collective-permute-start | bytes 1769480 | tf_op jit(solution)/shard_map/ppermute | solution.py:28
  49.1 15.1 %collective-permute-start.11 = (f32[128,1152]{1,0:T(8,128)S(1)}, f32[128,1152]{1,0:T(8,128)S(1)}, u32[]{:S(2)}, u32[]{:S(2)}) collective-permute-start(f32[128,1152]{1,0:T(8,128)S(1)} %get-tuple-element.146.two), channel_id=1, source_target_pairs={{0,120},{1,249},{2,122},{3,251},{4,124},{5,253},{6,126},{7,255},{8... | collective-permute-start | bytes 1769480 | tf_op jit(solution)/shard_map/ppermute | solution.py:28
  53.7 3.5 %collective-permute-start.17 = (f32[64,1152]{1,0:T(8,128)S(1)}, f32[64,1152]{1,0:T(8,128)S(1)}, u32[]{:S(2)}, u32[]{:S(2)}) collective-permute-start(f32[64,1152]{1,0:T(8,128)S(1)} %get-tuple-element.149), channel_id=1, source_target_pairs={{0,1},{1,0},{2,3},{3,2},{4,5},{5,4},{6,7},{7,6},{8,9},{9,8},{10,11... | collective-permute-start | bytes 884744 | tf_op jit(solution)/shard_map/ppermute | solution.py:28
  56.1 2.7 %collective-permute-start.14 = (f32[64,1152]{1,0:T(8,128)S(1)}, f32[64,1152]{1,0:T(8,128)S(1)}, u32[]{:S(2)}, u32[]{:S(2)}) collective-permute-start(f32[64,1152]{1,0:T(8,128)S(1)} %get-tuple-element.138), channel_id=1, source_target_pairs={{0,1},{1,0},{2,3},{3,2},{4,5},{5,4},{6,7},{7,6},{8,9},{9,8},{10,11... | collective-permute-start | bytes 884744 | tf_op jit(solution)/shard_map/ppermute | solution.py:28
  57.3 14.6 %collective-permute-start.18 = (f32[64,1152]{1,0:T(8,128)S(1)}, f32[64,1152]{1,0:T(8,128)S(1)}, u32[]{:S(2)}, u32[]{:S(2)}) collective-permute-start(f32[64,1152]{1,0:T(8,128)S(1)} %shard_map.77), channel_id=1, source_target_pairs={{0,128},{1,129},{2,130},{3,131},{4,132},{5,133},{6,134},{7,135},{8... | collective-permute-start | bytes 884744 | tf_op jit(solution)/shard_map/ppermute | solution.py:28
  61.3 20.8 %collective-permute-start.16 = (f32[128,1152]{1,0:T(8,128)S(1)}, f32[128,1152]{1,0:T(8,128)S(1)}, u32[]{:S(2)}, u32[]{:S(2)}) collective-permute-start(f32[128,1152]{1,0:T(8,128)S(1)} %shard_map.75), channel_id=1, source_target_pairs={{0,120},{1,249},{2,122},{3,251},{4,124},{5,253},{6,126},{7,255},{8... | collective-permute-start | bytes 1769480 | tf_op jit(solution)/shard_map/ppermute | solution.py:28
  64.3 18.0 %collective-permute-start.15 = (f32[128,1152]{1,0:T(8,128)S(1)}, f32[128,1152]{1,0:T(8,128)S(1)}, u32[]{:S(2)}, u32[]{:S(2)}) collective-permute-start(f32[128,1152]{1,0:T(8,128)S(1)} %shard_map.76), channel_id=1, source_target_pairs={{0,4},{1,5},{2,6},{3,7},{4,0},{5,1},{6,2},{7,3},{8,12},{9,13},{10,... | collective-permute-start | bytes 1769480 | tf_op jit(solution)/shard_map/ppermute | solution.py:28
  64.4 9.7 %collective-permute-start.20 = (f32[64,1152]{1,0:T(8,128)S(1)}, f32[64,1152]{1,0:T(8,128)S(1)}, u32[]{:S(2)}, u32[]{:S(2)}) collective-permute-start(f32[64,1152]{1,0:T(8,128)S(1)} %get-tuple-element.155), channel_id=1, source_target_pairs={{0,1},{1,0},{2,3},{3,2},{4,5},{5,4},{6,7},{7,6},{8,9},{9,8},{10,11... | collective-permute-start | bytes 884744 | tf_op jit(solution)/shard_map/ppermute | solution.py:28
  67.2 14.9 %collective-permute-start.19 = (f32[64,1152]{1,0:T(8,128)S(1)}, f32[64,1152]{1,0:T(8,128)S(1)}, u32[]{:S(2)}, u32[]{:S(2)}) collective-permute-start(f32[64,1152]{1,0:T(8,128)S(1)} %shard_map.74), channel_id=1, source_target_pairs={{0,128},{1,129},{2,130},{3,131},{4,132},{5,133},{6,134},{7,135},{8... | collective-permute-start | bytes 884744 | tf_op jit(solution)/shard_map/ppermute | solution.py:28
  71.9 10.1 %collective-permute-start.21 = (f32[64,1152]{1,0:T(8,128)S(1)}, f32[64,1152]{1,0:T(8,128)S(1)}, u32[]{:S(2)}, u32[]{:S(2)}) collective-permute-start(f32[64,1152]{1,0:T(8,128)S(1)} %get-tuple-element.159), channel_id=1, source_target_pairs={{0,1},{1,0},{2,3},{3,2},{4,5},{5,4},{6,7},{7,6},{8,9},{9,8},{10,11... | collective-permute-start | bytes 884744 | tf_op jit(solution)/shard_map/ppermute | solution.py:28

commit v8 on v7

--- a/solution.py
+++ b/solution.py
@@ -67,7 +67,9 @@
     def one(u, v):
         return lax.dot_general(u, v, dims, preferred_element_type=jnp.float32)
 
-    return one(a_high, b_high) + (one(a_low, b_high) + one(a_high, b_low))
+    rows = a_high.shape[0]
+    both = one(jnp.concatenate([a_high, a_low], axis=0), b_high)
+    return both[:rows] + (both[rows:] + one(a_high, b_low))
 
 
 def places():

time: 84 us -> 83.5 us (level)
  Pallas kernels: 13.6 us -> 12.6 us
    pallas_call x23, Pallas kernels: 12.2 us -> 11.2 us  [call(): pl.pallas_call(kernel, out_shape=[jax.ShapeDtypeStruct(shape, dtype) for...]
    ppermute x22, waiting for transfers between devices: 34.2 us -> 35 us  [moved(): return lax.ppermute(block, ('cuts', 'blk'), pairs)]
  transfers between devices with their start and end apart: 22 -> 22, of which waited for: 8 -> 8; matrix products, arithmetic and copies ran while one was open for 0% -> 0% of each run, Pallas kernels for 14% -> 13%
where the time goes in v8:
time: 83.5 us; the launch traced here: 83.3 us
  waiting for transfers between devices  35 us (42%)
  starting transfers between devices  31.3 us (37%)
  Pallas kernels  12.6 us (15%)
  between operations  2.3 us (3%)
  local copies, waits for them, and re-layouts  2.12 us (3%)
    ppermute x22, waiting for transfers between devices, moved(): return lax.ppermute(block, ('cuts', 'blk'), pairs)  35 us
    ppermute x22, starting transfers between devices, moved(): return lax.ppermute(block, ('cuts', 'blk'), pairs)  31.3 us
    pallas_call x23, Pallas kernels, call(): pl.pallas_call(kernel, out_shape=[jax.ShapeDtypeStruct(shape, dtype) for...  11.2 us
    unnamed x4, local copies, waits for them, and re-layouts  2.12 us
  transfers between devices with their start and end apart: 22, of which 8 were waited for; matrix products, arithmetic and copies ran while one was open for 0% of the time, Pallas kernels for 13%

profile of v8, /device:TPU:1, one launch (start us, length us, event | category | flops | bytes accessed | tf_op | source)
XLA Modules:
  0.0 83.3 jit_solution(4789636535004603257)
XLA Ops:
  0.6 1.1 %copy-done.1 = f32[128,1152]{1,0:T(8,128)S(1)} copy-done((f32[128,1152]{1,0:T(8,128)S(1)}, f32[128,1152]{1,0:T(8,128)}, u32[]{:S(2)}) %copy-start.1) | copy-done | bytes 589848
  1.7 0.1 shard_map.60
  1.8 3.6 %collective-permute-start.1 = (f32[128,1152]{1,0:T(8,128)S(1)}, f32[128,1152]{1,0:T(8,128)S(1)}, u32[]{:S(2)}, u32[]{:S(2)}) collective-permute-start(f32[128,1152]{1,0:T(8,128)S(1)} %get-tuple-element.94.own.refs_1_.refs_0_.y), channel_id=1, source_target_pairs={{0,8},{1,137},{2,10},{3,139},{4,12},{5,141},{6,14},{7,143},{8,16},... | collective-permute-start | bytes 1769480 | tf_op jit(solution)/shard_map/ppermute | solution.py:28
  5.5 1.1 %copy-done = f32[128,1152]{1,0:T(8,128)S(1)} copy-done((f32[128,1152]{1,0:T(8,128)S(1)}, f32[128,1152]{1,0:T(8,128)}, u32[]{:S(2)}) %copy-start) | copy-done | bytes 589848
  6.5 0.1 shard_map.61
  6.7 0.1 collective-permute-start.2
  6.8 0.5 collective-permute-start.3
  7.3 1.7 %collective-permute-start = (f32[64,1152]{1,0:T(8,128)S(1)}, f32[64,1152]{1,0:T(8,128)S(1)}, u32[]{:S(2)}, u32[]{:S(2)}) collective-permute-start(f32[64,1152]{1,0:T(8,128)S(1)} %get-tuple-element.98.refs_0_.refs_2_), channel_id=1, source_target_pairs={{0,128},{1,129},{2,130},{3,131},{4,132},{5,133},{6,134},{7,135},{8... | collective-permute-start | bytes 884744 | tf_op jit(solution)/shard_map/ppermute | solution.py:28
  9.0 2.7 %collective-permute-start.9 = (f32[128,1152]{1,0:T(8,128)S(1)}, f32[128,1152]{1,0:T(8,128)S(1)}, u32[]{:S(2)}, u32[]{:S(2)}) collective-permute-start(f32[128,1152]{1,0:T(8,128)S(1)} %get-tuple-element.94.own.refs_1_.refs_0_.y), channel_id=1, source_target_pairs={{0,4},{1,5},{2,6},{3,7},{4,0},{5,1},{6,2},{7,3},{8,12},{9,13},{10,... | collective-permute-start | bytes 1769480 | tf_op jit(solution)/shard_map/ppermute | solution.py:28
  11.7 0.0 collective-permute-done.2.refs_2_
  11.8 0.0 collective-permute-done.3.refs_3_
  11.8 12.4 %collective-permute-done.1.last.refs_2_.refs_1_ = f32[128,1152]{1,0:T(8,128)S(1)} collective-permute-done((f32[128,1152]{1,0:T(8,128)S(1)}, f32[128,1152]{1,0:T(8,128)S(1)}, u32[]{:S(2)}, u32[]{:S(2)}) %collective-permute-start.1) | collective-permute-done | bytes 589856 | tf_op jit(solution)/shard_map/ppermute | solution.py:28
  24.1 0.1 shard_map.62
  24.3 1.3 %collective-permute-start.4 = (f32[128,1152]{1,0:T(8,128)S(1)}, f32[128,1152]{1,0:T(8,128)S(1)}, u32[]{:S(2)}, u32[]{:S(2)}) collective-permute-start(f32[128,1152]{1,0:T(8,128)S(1)} %get-tuple-element.93), channel_id=1, source_target_pairs={{0,2},{1,3},{2,4},{3,5},{4,6},{5,7},{6,0},{7,1},{8,10},{9,11},{10,... | collective-permute-start | bytes 1769480 | tf_op jit(solution)/shard_map/ppermute | solution.py:28
  25.6 1.5 %collective-permute-start.5 = (f32[128,1152]{1,0:T(8,128)S(1)}, f32[128,1152]{1,0:T(8,128)S(1)}, u32[]{:S(2)}, u32[]{:S(2)}) collective-permute-start(f32[128,1152]{1,0:T(8,128)S(1)} %get-tuple-element.95), channel_id=1, source_target_pairs={{0,6},{1,7},{2,0},{3,1},{4,2},{5,3},{6,4},{7,5},{8,14},{9,15},{10,... | collective-permute-start | bytes 1769480 | tf_op jit(solution)/shard_map/ppermute | solution.py:28
  27.0 0.0 collective-permute-done.refs_0_
  27.0 0.1 shard_map.64
  27.1 0.7 collective-permute-start.6
  27.8 2.3 %collective-permute-start.7 = (f32[64,1152]{1,0:T(8,128)S(1)}, f32[64,1152]{1,0:T(8,128)S(1)}, u32[]{:S(2)}, u32[]{:S(2)}) collective-permute-start(f32[64,1152]{1,0:T(8,128)S(1)} %collective-permute-done.refs_0_), channel_id=1, source_target_pairs={{0,1},{1,0},{2,3},{3,2},{4,5},{5,4},{6,7},{7,6},{8,9},{9,8},{10,11... | collective-permute-start | bytes 884744 | tf_op jit(solution)/shard_map/ppermute | solution.py:28
  30.1 0.0 collective-permute-done.9.two
  30.1 0.0 collective-permute-start.10
  31.4 0.2 shard_map.65
  31.6 1.4 %shard_map.66 = (f32[128,128]{1,0:T(8,128)S(1)}, f32[128,1152]{1,0:T(8,128)S(1)}, f32[128,128]{1,0:T(8,128)S(1)}, f32[128,1152]{1,0:T(8,128)S(1)}) custom-call(f32[8,128]{1,0:T(8,128)S(1)} %shard_map.59.refs_0_.params, f32[128,1152]{1,0:T(8,128)S(1)} %get-tuple-element.94.own.refs_1_.refs_0_.y, f32[128,1152]{1,0:T(8,128)S(1)} %collective-permute-done.1.last.refs_2_.refs_1_, ...), custom_call_target="tpu_custom_call" | custom-call | tf_op jit(solution)/shard_map/pallas_call | solution.py:252
  33.1 4.3 %collective-permute-done.6.refs_0_ = f32[64,1152]{1,0:T(8,128)S(1)} collective-permute-done((f32[64,1152]{1,0:T(8,128)S(1)}, f32[64,1152]{1,0:T(8,128)S(1)}, u32[]{:S(2)}, u32[]{:S(2)}) %collective-permute-start.6) | collective-permute-done | bytes 294944 | tf_op jit(solution)/shard_map/ppermute | solution.py:28
  37.3 0.0 collective-permute-done.7.refs_1_
  37.3 1.6 %collective-permute-start.8 = (f32[64,1152]{1,0:T(8,128)S(1)}, f32[64,1152]{1,0:T(8,128)S(1)}, u32[]{:S(2)}, u32[]{:S(2)}) collective-permute-start(f32[64,1152]{1,0:T(8,128)S(1)} %collective-permute-done.6.refs_0_), channel_id=1, source_target_pairs={{0,1},{1,0},{2,3},{3,2},{4,5},{5,4},{6,7},{7,6},{8,9},{9,8},{10,11... | collective-permute-start | bytes 884744 | tf_op jit(solution)/shard_map/ppermute | solution.py:28
  39.0 1.9 %collective-permute-done.4.one = f32[128,1152]{1,0:T(8,128)S(1)} collective-permute-done((f32[128,1152]{1,0:T(8,128)S(1)}, f32[128,1152]{1,0:T(8,128)S(1)}, u32[]{:S(2)}, u32[]{:S(2)}) %collective-permute-start.4) | collective-permute-done | bytes 589856 | tf_op jit(solution)/shard_map/ppermute | solution.py:28
  40.9 0.0 collective-permute-done.5.two
  40.9 0.1 shard_map.63
  41.0 0.3 shard_map.67
  41.2 2.3 %shard_map.68 = (f32[256,512]{1,0:T(8,128)S(1)}, f32[128,1152]{1,0:T(8,128)S(1)}, f32[128,1152]{1,0:T(8,128)S(1)}) custom-call(f32[8,128]{1,0:T(8,128)S(1)} %shard_map.59.refs_0_.params, f32[128,1152]{1,0:T(8,128)S(1)} %get-tuple-element.131.refs_0_.refs_2_, f32[128,1152]{1,0:T(8,128)S(1)} %get-tuple-element.132.refs_1_.refs_3_, ...), custom_call_target="tpu_custom_call" | custom-call | flops 3000000000 | tf_op jit(solution)/shard_map/pallas_call | solution.py:252
  43.6 2.5 %collective-permute-start.12 = (f32[128,1152]{1,0:T(8,128)S(1)}, f32[128,1152]{1,0:T(8,128)S(1)}, u32[]{:S(2)}, u32[]{:S(2)}) collective-permute-start(f32[128,1152]{1,0:T(8,128)S(1)} %get-tuple-element.122), channel_id=1, source_target_pairs={{0,6},{1,7},{2,0},{3,1},{4,2},{5,3},{6,4},{7,5},{8,14},{9,15},{10,... | collective-permute-start | bytes 1769480 | tf_op jit(solution)/shard_map/ppermute | solution.py:28
  46.0 0.0 collective-permute-start.13
  46.0 1.1 %collective-permute-done.10.two_last = f32[128,1152]{1,0:T(8,128)S(1)} collective-permute-done((f32[128,1152]{1,0:T(8,128)S(1)}, f32[128,1152]{1,0:T(8,128)S(1)}, u32[]{:S(2)}, u32[]{:S(2)}) %collective-permute-start.10) | collective-permute-done | bytes 589856 | tf_op jit(solution)/shard_map/ppermute | solution.py:28
  47.1 0.1 shard_map.69.refs_0_.refs_4_
  47.2 1.5 %shard_map.70 = (f32[128,512]{1,0:T(8,128)S(1)}, f32[128,1152]{1,0:T(8,128)S(1)}) custom-call(f32[8,128]{1,0:T(8,128)S(1)} %shard_map.59.refs_0_.params, f32[128,1152]{1,0:T(8,128)S(1)} %shard_map.69.refs_0_.refs_4_, bf16[512,1152]{1,0:T(8,128)(2,1)S(1)} %get-tuple-element.125.refs_2_.refs_1_.refs_3_, ...), custom_call_target="tpu_custom_call" | custom-call | tf_op jit(solution)/shard_map/pallas_call | solution.py:252
  48.7 1.5 %collective-permute-start.11 = (f32[128,1152]{1,0:T(8,128)S(1)}, f32[128,1152]{1,0:T(8,128)S(1)}, u32[]{:S(2)}, u32[]{:S(2)}) collective-permute-start(f32[128,1152]{1,0:T(8,128)S(1)} %get-tuple-element.146.two), channel_id=1, source_target_pairs={{0,120},{1,249},{2,122},{3,251},{4,124},{5,253},{6,126},{7,255},{8... | collective-permute-start | bytes 1769480 | tf_op jit(solution)/shard_map/ppermute | solution.py:28
  50.2 1.4 %shard_map.71 = (f32[128,128]{1,0:T(8,128)S(1)}, f32[128,1152]{1,0:T(8,128)S(1)}, f32[128,128]{1,0:T(8,128)S(1)}, f32[128,1152]{1,0:T(8,128)S(1)}) custom-call(f32[8,128]{1,0:T(8,128)S(1)} %shard_map.59.refs_0_.params, f32[128,1152]{1,0:T(8,128)S(1)} %get-tuple-element.94.own.refs_1_.refs_0_.y, f32[128,1152]{1,0:T(8,128)S(1)} %collective-permute-done.1.last.refs_2_.refs_1_, ...), custom_call_target="tpu_custom_call" | custom-call | tf_op jit(solution)/shard_map/pallas_call | solution.py:252
  51.6 1.4 %shard_map.72 = (f32[64,1152]{1,0:T(8,128)S(1)}, f32[64,1152]{1,0:T(8,128)S(1)}, f32[64,1152]{1,0:T(8,128)S(1)}, f32[64,1152]{1,0:T(8,128)S(1)}) custom-call(f32[128,1152]{1,0:T(8,128)S(1)} %get-tuple-element.94.own.refs_1_.refs_0_.y, f32[128,1152]{1,0:T(8,128)S(1)} %collective-permute-done.1.last.refs_2_.refs_1_, ...), custom_call_target="tpu_custom_call" | custom-call | tf_op jit(solution)/shard_map/pallas_call | solution.py:252
  53.0 2.4 %collective-permute-start.17 = (f32[64,1152]{1,0:T(8,128)S(1)}, f32[64,1152]{1,0:T(8,128)S(1)}, u32[]{:S(2)}, u32[]{:S(2)}) collective-permute-start(f32[64,1152]{1,0:T(8,128)S(1)} %get-tuple-element.149), channel_id=1, source_target_pairs={{0,1},{1,0},{2,3},{3,2},{4,5},{5,4},{6,7},{7,6},{8,9},{9,8},{10,11... | collective-permute-start | bytes 884744 | tf_op jit(solution)/shard_map/ppermute | solution.py:28
  55.4 0.1 collective-permute-start.14
  55.5 1.1 %collective-permute-done.17.beside = f32[64,1152]{1,0:T(8,128)S(1)} collective-permute-done((f32[64,1152]{1,0:T(8,128)S(1)}, f32[64,1152]{1,0:T(8,128)S(1)}, u32[]{:S(2)}, u32[]{:S(2)}) %collective-permute-start.17) | collective-permute-done | bytes 294944 | tf_op jit(solution)/shard_map/ppermute | solution.py:28
  56.7 0.1 collective-permute-start.18
  56.8 1.4 %shard_map.73 = (f32[64,1152]{1,0:T(8,128)S(1)}, f32[64,1152]{1,0:T(8,128)S(1)}, f32[64,1152]{1,0:T(8,128)S(1)}, f32[64,1152]{1,0:T(8,128)S(1)}) custom-call(f32[128,1152]{1,0:T(8,128)S(1)} %get-tuple-element.94.own.refs_1_.refs_0_.y, f32[128,1152]{1,0:T(8,128)S(1)} %collective-permute-done.1.last.refs_2_.refs_1_, ...), custom_call_target="tpu_custom_call" | custom-call | tf_op jit(solution)/shard_map/pallas_call | solution.py:252
  58.2 0.0 collective-permute-done.14.beside
  58.2 0.0 collective-permute-done.12.back_1
  58.2 2.9 %collective-permute-done.13.back_3 = f32[128,1152]{1,0:T(8,128)S(1)} collective-permute-done((f32[128,1152]{1,0:T(8,128)S(1)}, f32[128,1152]{1,0:T(8,128)S(1)}, u32[]{:S(2)}, u32[]{:S(2)}) %collective-permute-start.13) | collective-permute-done | bytes 589856 | tf_op jit(solution)/shard_map/ppermute | solution.py:28
  61.1 0.1 shard_map.75
  61.2 2.9 %collective-permute-start.16 = (f32[128,1152]{1,0:T(8,128)S(1)}, f32[128,1152]{1,0:T(8,128)S(1)}, u32[]{:S(2)}, u32[]{:S(2)}) collective-permute-start(f32[128,1152]{1,0:T(8,128)S(1)} %shard_map.75), channel_id=1, source_target_pairs={{0,120},{1,249},{2,122},{3,251},{4,124},{5,253},{6,126},{7,255},{8... | collective-permute-start | bytes 1769480 | tf_op jit(solution)/shard_map/ppermute | solution.py:28
  64.1 0.1 shard_map.76
  64.2 0.1 collective-permute-start.15
  64.3 2.6 %collective-permute-start.20 = (f32[64,1152]{1,0:T(8,128)S(1)}, f32[64,1152]{1,0:T(8,128)S(1)}, u32[]{:S(2)}, u32[]{:S(2)}) collective-permute-start(f32[64,1152]{1,0:T(8,128)S(1)} %get-tuple-element.155), channel_id=1, source_target_pairs={{0,1},{1,0},{2,3},{3,2},{4,5},{5,4},{6,7},{7,6},{8,9},{9,8},{10,11... | collective-permute-start | bytes 884744 | tf_op jit(solution)/shard_map/ppermute | solution.py:28
  66.9 1.2 %collective-permute-start.19 = (f32[64,1152]{1,0:T(8,128)S(1)}, f32[64,1152]{1,0:T(8,128)S(1)}, u32[]{:S(2)}, u32[]{:S(2)}) collective-permute-start(f32[64,1152]{1,0:T(8,128)S(1)} %shard_map.74), channel_id=1, source_target_pairs={{0,128},{1,129},{2,130},{3,131},{4,132},{5,133},{6,134},{7,135},{8... | collective-permute-start | bytes 884744 | tf_op jit(solution)/shard_map/ppermute | solution.py:28
  68.1 2.9 %collective-permute-done.18.three = f32[64,1152]{1,0:T(8,128)S(1)} collective-permute-done((f32[64,1152]{1,0:T(8,128)S(1)}, f32[64,1152]{1,0:T(8,128)S(1)}, u32[]{:S(2)}, u32[]{:S(2)}) %collective-permute-start.18) | collective-permute-done | bytes 294944 | tf_op jit(solution)/shard_map/ppermute | solution.py:28
  71.0 1.8 %collective-permute-start.21 = (f32[64,1152]{1,0:T(8,128)S(1)}, f32[64,1152]{1,0:T(8,128)S(1)}, u32[]{:S(2)}, u32[]{:S(2)}) collective-permute-start(f32[64,1152]{1,0:T(8,128)S(1)} %get-tuple-element.159), channel_id=1, source_target_pairs={{0,1},{1,0},{2,3},{3,2},{4,5},{5,4},{6,7},{7,6},{8,9},{9,8},{10,11... | collective-permute-start | bytes 884744 | tf_op jit(solution)/shard_map/ppermute | solution.py:28
  72.8 0.2 shard_map.78.here
  73.0 0.0 collective-permute-done.20.two
  73.0 0.1 shard_map.79.refs_5_
  73.1 8.5 %collective-permute-done.19.three = f32[64,1152]{1,0:T(8,128)S(1)} collective-permute-done((f32[64,1152]{1,0:T(8,128)S(1)}, f32[64,1152]{1,0:T(8,128)S(1)}, u32[]{:S(2)}, u32[]{:S(2)}) %collective-permute-start.19) | collective-permute-done | bytes 294944 | tf_op jit(solution)/shard_map/ppermute | solution.py:28
  81.6 0.0 collective-permute-done.21.two
  81.6 0.1 shard_map.80.refs_6_
  81.6 0.1 shard_map.81.refs_0_
  81.7 0.0 collective-permute-done.15.refs_1_
  81.7 1.4 %shard_map.82 = (f32[128,1152]{1,0:T(8,128)}, f32[128,1152]{1,0:T(8,128)}) custom-call(f32[8,128]{1,0:T(8,128)S(1)} %shard_map.59.refs_0_.params, f32[128,1152]{1,0:T(8,128)S(1)} %get-tuple-element.94.own.refs_1_.refs_0_.y, f32[128,1]{1,0:T(8,128)S(1)} %get-tuple-element.86._.y_inv, f32[128,1152]{1,0:T(8,128)S(1)} %shard_map.81.refs_0_, ...), custom_call_target="tpu_custom_call" | custom-call | tf_op jit(solution)/shard_map/pallas_call | solution.py:265
  (8 shorter events, 0.1 us)
Async XLA Ops:
  0.6 1.1 %copy-start.1 = (f32[128,1152]{1,0:T(8,128)S(1)}, f32[128,1152]{1,0:T(8,128)}, u32[]{:S(2)}) copy-start(f32[128,1152]{1,0:T(8,128)} %in_ref.2) | copy-start | bytes 1769476
  1.8 22.3 %collective-permute-start.1 = (f32[128,1152]{1,0:T(8,128)S(1)}, f32[128,1152]{1,0:T(8,128)S(1)}, u32[]{:S(2)}, u32[]{:S(2)}) collective-permute-start(f32[128,1152]{1,0:T(8,128)S(1)} %get-tuple-element.94.own.refs_1_.refs_0_.y), channel_id=1, source_target_pairs={{0,8},{1,137},{2,10},{3,139},{4,12},{5,141},{6,14},{7,143},{8,16},... | collective-permute-start | bytes 1769480 | tf_op jit(solution)/shard_map/ppermute | solution.py:28
  5.5 1.1 %copy-start = (f32[128,1152]{1,0:T(8,128)S(1)}, f32[128,1152]{1,0:T(8,128)}, u32[]{:S(2)}) copy-start(f32[128,1152]{1,0:T(8,128)} %in_ref.3) | copy-start | bytes 1769476
  6.7 5.1 %collective-permute-start.2 = (f32[64,1152]{1,0:T(8,128)S(1)}, f32[64,1152]{1,0:T(8,128)S(1)}, u32[]{:S(2)}, u32[]{:S(2)}) collective-permute-start(f32[64,1152]{1,0:T(8,128)S(1)} %get-tuple-element.98.refs_0_.refs_2_), channel_id=1, source_target_pairs={{0,1},{1,0},{2,3},{3,2},{4,5},{5,4},{6,7},{7,6},{8,9},{9,8},{10,11... | collective-permute-start | bytes 884744 | tf_op jit(solution)/shard_map/ppermute | solution.py:28
  6.8 5.0 %collective-permute-start.3 = (f32[64,1152]{1,0:T(8,128)S(1)}, f32[64,1152]{1,0:T(8,128)S(1)}, u32[]{:S(2)}, u32[]{:S(2)}) collective-permute-start(f32[64,1152]{1,0:T(8,128)S(1)} %get-tuple-element.102.refs_1_.refs_3_), channel_id=1, source_target_pairs={{0,1},{1,0},{2,3},{3,2},{4,5},{5,4},{6,7},{7,6},{8,9},{9,8},{10,11... | collective-permute-start | bytes 884744 | tf_op jit(solution)/shard_map/ppermute | solution.py:28
  7.3 19.8 %collective-permute-start = (f32[64,1152]{1,0:T(8,128)S(1)}, f32[64,1152]{1,0:T(8,128)S(1)}, u32[]{:S(2)}, u32[]{:S(2)}) collective-permute-start(f32[64,1152]{1,0:T(8,128)S(1)} %get-tuple-element.98.refs_0_.refs_2_), channel_id=1, source_target_pairs={{0,128},{1,129},{2,130},{3,131},{4,132},{5,133},{6,134},{7,135},{8... | collective-permute-start | bytes 884744 | tf_op jit(solution)/shard_map/ppermute | solution.py:28
  9.0 21.1 %collective-permute-start.9 = (f32[128,1152]{1,0:T(8,128)S(1)}, f32[128,1152]{1,0:T(8,128)S(1)}, u32[]{:S(2)}, u32[]{:S(2)}) collective-permute-start(f32[128,1152]{1,0:T(8,128)S(1)} %get-tuple-element.94.own.refs_1_.refs_0_.y), channel_id=1, source_target_pairs={{0,4},{1,5},{2,6},{3,7},{4,0},{5,1},{6,2},{7,3},{8,12},{9,13},{10,... | collective-permute-start | bytes 1769480 | tf_op jit(solution)/shard_map/ppermute | solution.py:28
  24.3 16.6 %collective-permute-start.4 = (f32[128,1152]{1,0:T(8,128)S(1)}, f32[128,1152]{1,0:T(8,128)S(1)}, u32[]{:S(2)}, u32[]{:S(2)}) collective-permute-start(f32[128,1152]{1,0:T(8,128)S(1)} %get-tuple-element.93), channel_id=1, source_target_pairs={{0,2},{1,3},{2,4},{3,5},{4,6},{5,7},{6,0},{7,1},{8,10},{9,11},{10,... | collective-permute-start | bytes 1769480 | tf_op jit(solution)/shard_map/ppermute | solution.py:28
  25.6 15.3 %collective-permute-start.5 = (f32[128,1152]{1,0:T(8,128)S(1)}, f32[128,1152]{1,0:T(8,128)S(1)}, u32[]{:S(2)}, u32[]{:S(2)}) collective-permute-start(f32[128,1152]{1,0:T(8,128)S(1)} %get-tuple-element.95), channel_id=1, source_target_pairs={{0,6},{1,7},{2,0},{3,1},{4,2},{5,3},{6,4},{7,5},{8,14},{9,15},{10,... | collective-permute-start | bytes 1769480 | tf_op jit(solution)/shard_map/ppermute | solution.py:28
  27.1 10.3 %collective-permute-start.6 = (f32[64,1152]{1,0:T(8,128)S(1)}, f32[64,1152]{1,0:T(8,128)S(1)}, u32[]{:S(2)}, u32[]{:S(2)}) collective-permute-start(f32[64,1152]{1,0:T(8,128)S(1)} %get-tuple-element.102.refs_1_.refs_3_), channel_id=1, source_target_pairs={{0,128},{1,129},{2,130},{3,131},{4,132},{5,133},{6,134},{7,135},{8... | collective-permute-start | bytes 884744 | tf_op jit(solution)/shard_map/ppermute | solution.py:28
  27.8 9.6 %collective-permute-start.7 = (f32[64,1152]{1,0:T(8,128)S(1)}, f32[64,1152]{1,0:T(8,128)S(1)}, u32[]{:S(2)}, u32[]{:S(2)}) collective-permute-start(f32[64,1152]{1,0:T(8,128)S(1)} %collective-permute-done.refs_0_), channel_id=1, source_target_pairs={{0,1},{1,0},{2,3},{3,2},{4,5},{5,4},{6,7},{7,6},{8,9},{9,8},{10,11... | collective-permute-start | bytes 884744 | tf_op jit(solution)/shard_map/ppermute | solution.py:28
  30.1 17.0 %collective-permute-start.10 = (f32[128,1152]{1,0:T(8,128)S(1)}, f32[128,1152]{1,0:T(8,128)S(1)}, u32[]{:S(2)}, u32[]{:S(2)}) collective-permute-start(f32[128,1152]{1,0:T(8,128)S(1)} %collective-permute-done.9.two), channel_id=1, source_target_pairs={{0,8},{1,137},{2,10},{3,139},{4,12},{5,141},{6,14},{7,143},{8,16},... | collective-permute-start | bytes 1769480 | tf_op jit(solution)/shard_map/ppermute | solution.py:28
  37.3 3.6 %collective-permute-start.8 = (f32[64,1152]{1,0:T(8,128)S(1)}, f32[64,1152]{1,0:T(8,128)S(1)}, u32[]{:S(2)}, u32[]{:S(2)}) collective-permute-start(f32[64,1152]{1,0:T(8,128)S(1)} %collective-permute-done.6.refs_0_), channel_id=1, source_target_pairs={{0,1},{1,0},{2,3},{3,2},{4,5},{5,4},{6,7},{7,6},{8,9},{9,8},{10,11... | collective-permute-start | bytes 884744 | tf_op jit(solution)/shard_map/ppermute | solution.py:28
  43.6 14.7 %collective-permute-start.12 = (f32[128,1152]{1,0:T(8,128)S(1)}, f32[128,1152]{1,0:T(8,128)S(1)}, u32[]{:S(2)}, u32[]{:S(2)}) collective-permute-start(f32[128,1152]{1,0:T(8,128)S(1)} %get-tuple-element.122), channel_id=1, source_target_pairs={{0,6},{1,7},{2,0},{3,1},{4,2},{5,3},{6,4},{7,5},{8,14},{9,15},{10,... | collective-permute-start | bytes 1769480 | tf_op jit(solution)/shard_map/ppermute | solution.py:28
  46.0 15.1 %collective-permute-start.13 = (f32[128,1152]{1,0:T(8,128)S(1)}, f32[128,1152]{1,0:T(8,128)S(1)}, u32[]{:S(2)}, u32[]{:S(2)}) collective-permute-start(f32[128,1152]{1,0:T(8,128)S(1)} %get-tuple-element.123), channel_id=1, source_target_pairs={{0,2},{1,3},{2,4},{3,5},{4,6},{5,7},{6,0},{7,1},{8,10},{9,11},{10,... | collective-permute-start | bytes 1769480 | tf_op jit(solution)/shard_map/ppermute | solution.py:28
  48.7 15.4 %collective-permute-start.11 = (f32[128,1152]{1,0:T(8,128)S(1)}, f32[128,1152]{1,0:T(8,128)S(1)}, u32[]{:S(2)}, u32[]{:S(2)}) collective-permute-start(f32[128,1152]{1,0:T(8,128)S(1)} %get-tuple-element.146.two), channel_id=1, source_target_pairs={{0,120},{1,249},{2,122},{3,251},{4,124},{5,253},{6,126},{7,255},{8... | collective-permute-start | bytes 1769480 | tf_op jit(solution)/shard_map/ppermute | solution.py:28
  53.0 3.6 %collective-permute-start.17 = (f32[64,1152]{1,0:T(8,128)S(1)}, f32[64,1152]{1,0:T(8,128)S(1)}, u32[]{:S(2)}, u32[]{:S(2)}) collective-permute-start(f32[64,1152]{1,0:T(8,128)S(1)} %get-tuple-element.149), channel_id=1, source_target_pairs={{0,1},{1,0},{2,3},{3,2},{4,5},{5,4},{6,7},{7,6},{8,9},{9,8},{10,11... | collective-permute-start | bytes 884744 | tf_op jit(solution)/shard_map/ppermute | solution.py:28
  55.4 2.7 %collective-permute-start.14 = (f32[64,1152]{1,0:T(8,128)S(1)}, f32[64,1152]{1,0:T(8,128)S(1)}, u32[]{:S(2)}, u32[]{:S(2)}) collective-permute-start(f32[64,1152]{1,0:T(8,128)S(1)} %get-tuple-element.138), channel_id=1, source_target_pairs={{0,1},{1,0},{2,3},{3,2},{4,5},{5,4},{6,7},{7,6},{8,9},{9,8},{10,11... | collective-permute-start | bytes 884744 | tf_op jit(solution)/shard_map/ppermute | solution.py:28
  56.7 14.4 %collective-permute-start.18 = (f32[64,1152]{1,0:T(8,128)S(1)}, f32[64,1152]{1,0:T(8,128)S(1)}, u32[]{:S(2)}, u32[]{:S(2)}) collective-permute-start(f32[64,1152]{1,0:T(8,128)S(1)} %shard_map.77), channel_id=1, source_target_pairs={{0,128},{1,129},{2,130},{3,131},{4,132},{5,133},{6,134},{7,135},{8... | collective-permute-start | bytes 884744 | tf_op jit(solution)/shard_map/ppermute | solution.py:28
  61.2 20.4 %collective-permute-start.16 = (f32[128,1152]{1,0:T(8,128)S(1)}, f32[128,1152]{1,0:T(8,128)S(1)}, u32[]{:S(2)}, u32[]{:S(2)}) collective-permute-start(f32[128,1152]{1,0:T(8,128)S(1)} %shard_map.75), channel_id=1, source_target_pairs={{0,120},{1,249},{2,122},{3,251},{4,124},{5,253},{6,126},{7,255},{8... | collective-permute-start | bytes 1769480 | tf_op jit(solution)/shard_map/ppermute | solution.py:28
  64.2 17.6 %collective-permute-start.15 = (f32[128,1152]{1,0:T(8,128)S(1)}, f32[128,1152]{1,0:T(8,128)S(1)}, u32[]{:S(2)}, u32[]{:S(2)}) collective-permute-start(f32[128,1152]{1,0:T(8,128)S(1)} %shard_map.76), channel_id=1, source_target_pairs={{0,4},{1,5},{2,6},{3,7},{4,0},{5,1},{6,2},{7,3},{8,12},{9,13},{10,... | collective-permute-start | bytes 1769480 | tf_op jit(solution)/shard_map/ppermute | solution.py:28
  64.3 8.7 %collective-permute-start.20 = (f32[64,1152]{1,0:T(8,128)S(1)}, f32[64,1152]{1,0:T(8,128)S(1)}, u32[]{:S(2)}, u32[]{:S(2)}) collective-permute-start(f32[64,1152]{1,0:T(8,128)S(1)} %get-tuple-element.155), channel_id=1, source_target_pairs={{0,1},{1,0},{2,3},{3,2},{4,5},{5,4},{6,7},{7,6},{8,9},{9,8},{10,11... | collective-permute-start | bytes 884744 | tf_op jit(solution)/shard_map/ppermute | solution.py:28
  66.9 14.7 %collective-permute-start.19 = (f32[64,1152]{1,0:T(8,128)S(1)}, f32[64,1152]{1,0:T(8,128)S(1)}, u32[]{:S(2)}, u32[]{:S(2)}) collective-permute-start(f32[64,1152]{1,0:T(8,128)S(1)} %shard_map.74), channel_id=1, source_target_pairs={{0,128},{1,129},{2,130},{3,131},{4,132},{5,133},{6,134},{7,135},{8... | collective-permute-start | bytes 884744 | tf_op jit(solution)/shard_map/ppermute | solution.py:28
  71.0 10.5 %collective-permute-start.21 = (f32[64,1152]{1,0:T(8,128)S(1)}, f32[64,1152]{1,0:T(8,128)S(1)}, u32[]{:S(2)}, u32[]{:S(2)}) collective-permute-start(f32[64,1152]{1,0:T(8,128)S(1)} %get-tuple-element.159), channel_id=1, source_target_pairs={{0,1},{1,0},{2,3},{3,2},{4,5},{5,4},{6,7},{7,6},{8,9},{9,8},{10,11... | collective-permute-start | bytes 884744 | tf_op jit(solution)/shard_map/ppermute | solution.py:28

commit v9 on v8

--- a/solution.py
+++ b/solution.py
@@ -7,6 +7,7 @@
 
 GROUPS, BLOCKS, ROW = 2, 128, 8
 FIRST = 64
+MORE = 48
 W_ONE = 0
 W_HOP = 0
 W_CUT = 300_000_000
@@ -284,8 +285,9 @@
     outs = [((rows, 1), f32), block]
     y_inv, y_own = call(normalize_kernel, outs, text_embed)
     first, second = ((FIRST, width), f32), ((rows - FIRST, width), f32)
-    outs = [((rows, 1), f32), first, second]
-    x_inv, x_0, x_1 = call(image_norm_kernel, outs, y_inv, image_embed)
+    more, less = ((MORE, width), f32), ((rows - MORE, width), f32)
+    outs = [((rows, 1), f32), first, second, more, less]
+    x_inv, x_0, x_1, x_more, x_less = call(image_norm_kernel, outs, y_inv, image_embed)
     params = call(params_kernel, [((8, 128), f32)], scalars=(log_scale, bias))
     y_last = moved(y_own, next_row)
     y_2 = moved(y_own, in_row(2))
@@ -337,17 +339,17 @@
     gb_here, gyb_here, gb_near, gyb_near = near
     arrays = (y_own, y_last, y_1, y_3, y_2, gb_here, gb_near, g_13, g_2)
     kernel = lambda *refs: image_kernel(2 * rows, *refs)
-    gx_0, gx_1, gx_near_0, gx_near_1 = call(kernel, [first, second] * 2, *arrays)
+    gx_0, gx_1, gx_near_0, gx_near_1 = call(kernel, [more, less] * 2, *arrays)
     gx_beside_0 = moved(gx_near_0, other_core)
     gx_beside_1 = moved(gx_near_1, other_core)
-    gx_0 = call(add_kernel, [first], gx_0, gx_beside_0)[0]
+    gx_0 = call(add_kernel, [more], gx_0, gx_beside_0)[0]
     gx_cut_0 = moved(gx_0, other_group)
     gx_1, y_1, y_3 = together(gx_1, y_1, y_3)
     arrays = (y_own, y_last, y_1, y_3, y_2, ga_here, ga_near, g_13, g_2)
     kernel = lambda *refs: image_kernel(0, *refs)
-    outs = call(kernel, [first, second] * 2, *arrays)
+    outs = call(kernel, [more, less] * 2, *arrays)
     gx_own_0, gx_own_1, gx_near_own_0, gx_near_own_1 = outs
-    gx_1 = call(add_kernel, [second], gx_1, gx_beside_1)[0]
+    gx_1 = call(add_kernel, [less], gx_1, gx_beside_1)[0]
     back_1, back_3, gx_near_own_0, gx_near_own_1, gx_1 = together(
         back_1, back_3, gx_near_own_0, gx_near_own_1, gx_1
     )
@@ -366,15 +368,15 @@
     gy_own = call(own_kernel, [block], *arrays)[0]
     gx_cut_0, gy_own = together(gx_cut_0, gy_own)
     parts = (gx_own_0, gx_beside_own_0, gx_cut_0)
-    image_0 = call(add_three_kernel, [first], *parts, weight=W_HALF)[0]
+    image_0 = call(add_three_kernel, [more], *parts, weight=W_HALF)[0]
     gx_cut_1, image_0 = together(gx_cut_1, image_0)
     parts = (gx_own_1, gx_beside_own_1, gx_cut_1)
-    image_1 = call(add_three_kernel, [second], *parts, weight=W_END)[0]
+    image_1 = call(add_three_kernel, [less], *parts, weight=W_END)[0]
     home, gy_own, image_0, image_1 = together(home, gy_own, image_0, image_1)
     gy_own = call(add_kernel, [block], gy_own, home, weight=W_HOME)[0]
     back_2, gy_own, image_0, image_1 = together(back_2, gy_own, image_0, image_1)
     return tuple(
-        finish(*params, y_own, y_inv, gy_own, back_2, x_0, x_1, x_inv, image_0, image_1)
+        finish(*params, y_own, y_inv, gy_own, back_2, x_more, x_less, x_inv, image_0, image_1)
     )
 
 

time: 83.5 us -> 82.8 us (level)
  transfers between devices with their start and end apart: 22 -> 22, of which waited for: 8 -> 9; matrix products, arithmetic and copies ran while one was open for 0% -> 0% of each run, Pallas kernels for 13% -> 13%
where the time goes in v9:
time: 82.8 us; the launch traced here: 82.7 us
  waiting for transfers between devices  34.8 us (42%)
  starting transfers between devices  30.9 us (37%)
  Pallas kernels  12.6 us (15%)
  between operations  2.28 us (3%)
  local copies, waits for them, and re-layouts  2.12 us (3%)
    ppermute x22, waiting for transfers between devices, moved(): return lax.ppermute(block, ('cuts', 'blk'), pairs)  34.8 us
    ppermute x22, starting transfers between devices, moved(): return lax.ppermute(block, ('cuts', 'blk'), pairs)  30.9 us
    pallas_call x23, Pallas kernels, call(): pl.pallas_call(kernel, out_shape=[jax.ShapeDtypeStruct(shape, dtype) for...  11.2 us
    unnamed x4, local copies, waits for them, and re-layouts  2.12 us
  transfers between devices with their start and end apart: 22, of which 9 were waited for; matrix products, arithmetic and copies ran while one was open for 0% of the time, Pallas kernels for 13%

profile of v9, /device:TPU:1, one launch (start us, length us, event | category | flops | bytes accessed | tf_op | source)
XLA Modules:
  0.0 82.7 jit_solution(4838189560875196497)
XLA Ops:
  0.6 1.1 %copy-done.1 = f32[128,1152]{1,0:T(8,128)S(1)} copy-done((f32[128,1152]{1,0:T(8,128)S(1)}, f32[128,1152]{1,0:T(8,128)}, u32[]{:S(2)}) %copy-start.1) | copy-done | bytes 589848
  1.7 0.1 shard_map.60
  1.8 3.6 %collective-permute-start.1 = (f32[128,1152]{1,0:T(8,128)S(1)}, f32[128,1152]{1,0:T(8,128)S(1)}, u32[]{:S(2)}, u32[]{:S(2)}) collective-permute-start(f32[128,1152]{1,0:T(8,128)S(1)} %get-tuple-element.96.own.refs_1_.refs_0_.y), channel_id=1, source_target_pairs={{0,8},{1,137},{2,10},{3,139},{4,12},{5,141},{6,14},{7,143},{8,16},... | collective-permute-start | bytes 1769480 | tf_op jit(solution)/shard_map/ppermute | solution.py:29
  5.5 1.1 %copy-done = f32[128,1152]{1,0:T(8,128)S(1)} copy-done((f32[128,1152]{1,0:T(8,128)S(1)}, f32[128,1152]{1,0:T(8,128)}, u32[]{:S(2)}) %copy-start) | copy-done | bytes 589848
  6.5 0.2 shard_map.61
  6.7 0.1 collective-permute-start.2
  6.8 0.5 collective-permute-start.3
  7.3 1.7 %collective-permute-start = (f32[64,1152]{1,0:T(8,128)S(1)}, f32[64,1152]{1,0:T(8,128)S(1)}, u32[]{:S(2)}, u32[]{:S(2)}) collective-permute-start(f32[64,1152]{1,0:T(8,128)S(1)} %get-tuple-element.100.refs_0_), channel_id=1, source_target_pairs={{0,128},{1,129},{2,130},{3,131},{4,132},{5,133},{6,134},{7,135},{8... | collective-permute-start | bytes 884744 | tf_op jit(solution)/shard_map/ppermute | solution.py:29
  9.0 2.7 %collective-permute-start.9 = (f32[128,1152]{1,0:T(8,128)S(1)}, f32[128,1152]{1,0:T(8,128)S(1)}, u32[]{:S(2)}, u32[]{:S(2)}) collective-permute-start(f32[128,1152]{1,0:T(8,128)S(1)} %get-tuple-element.96.own.refs_1_.refs_0_.y), channel_id=1, source_target_pairs={{0,4},{1,5},{2,6},{3,7},{4,0},{5,1},{6,2},{7,3},{8,12},{9,13},{10,... | collective-permute-start | bytes 1769480 | tf_op jit(solution)/shard_map/ppermute | solution.py:29
  11.8 0.0 collective-permute-done.2.refs_2_
  11.8 0.0 collective-permute-done.3.refs_3_
  11.8 12.4 %collective-permute-done.1.last.refs_2_.refs_1_ = f32[128,1152]{1,0:T(8,128)S(1)} collective-permute-done((f32[128,1152]{1,0:T(8,128)S(1)}, f32[128,1152]{1,0:T(8,128)S(1)}, u32[]{:S(2)}, u32[]{:S(2)}) %collective-permute-start.1) | collective-permute-done | bytes 589856 | tf_op jit(solution)/shard_map/ppermute | solution.py:29
  24.2 0.1 shard_map.62
  24.3 1.3 %collective-permute-start.4 = (f32[128,1152]{1,0:T(8,128)S(1)}, f32[128,1152]{1,0:T(8,128)S(1)}, u32[]{:S(2)}, u32[]{:S(2)}) collective-permute-start(f32[128,1152]{1,0:T(8,128)S(1)} %get-tuple-element.95), channel_id=1, source_target_pairs={{0,2},{1,3},{2,4},{3,5},{4,6},{5,7},{6,0},{7,1},{8,10},{9,11},{10,... | collective-permute-start | bytes 1769480 | tf_op jit(solution)/shard_map/ppermute | solution.py:29
  25.6 1.5 %collective-permute-start.5 = (f32[128,1152]{1,0:T(8,128)S(1)}, f32[128,1152]{1,0:T(8,128)S(1)}, u32[]{:S(2)}, u32[]{:S(2)}) collective-permute-start(f32[128,1152]{1,0:T(8,128)S(1)} %get-tuple-element.97), channel_id=1, source_target_pairs={{0,6},{1,7},{2,0},{3,1},{4,2},{5,3},{6,4},{7,5},{8,14},{9,15},{10,... | collective-permute-start | bytes 1769480 | tf_op jit(solution)/shard_map/ppermute | solution.py:29
  27.0 0.0 collective-permute-done.refs_0_
  27.1 0.1 shard_map.64
  27.1 0.7 collective-permute-start.6
  27.8 2.3 %collective-permute-start.7 = (f32[64,1152]{1,0:T(8,128)S(1)}, f32[64,1152]{1,0:T(8,128)S(1)}, u32[]{:S(2)}, u32[]{:S(2)}) collective-permute-start(f32[64,1152]{1,0:T(8,128)S(1)} %collective-permute-done.refs_0_), channel_id=1, source_target_pairs={{0,1},{1,0},{2,3},{3,2},{4,5},{5,4},{6,7},{7,6},{8,9},{9,8},{10,11... | collective-permute-start | bytes 884744 | tf_op jit(solution)/shard_map/ppermute | solution.py:29
  30.1 0.0 collective-permute-done.9.two
  30.1 0.0 collective-permute-start.10
  31.4 0.2 shard_map.65
  31.6 1.4 %shard_map.66 = (f32[128,128]{1,0:T(8,128)S(1)}, f32[128,1152]{1,0:T(8,128)S(1)}, f32[128,128]{1,0:T(8,128)S(1)}, f32[128,1152]{1,0:T(8,128)S(1)}) custom-call(f32[8,128]{1,0:T(8,128)S(1)} %shard_map.59.refs_0_.params, f32[128,1152]{1,0:T(8,128)S(1)} %get-tuple-element.96.own.refs_1_.refs_0_.y, f32[128,1152]{1,0:T(8,128)S(1)} %collective-permute-done.1.last.refs_2_.refs_1_, ...), custom_call_target="tpu_custom_call" | custom-call | tf_op jit(solution)/shard_map/pallas_call | solution.py:253
  33.1 4.3 %collective-permute-done.6.refs_0_ = f32[64,1152]{1,0:T(8,128)S(1)} collective-permute-done((f32[64,1152]{1,0:T(8,128)S(1)}, f32[64,1152]{1,0:T(8,128)S(1)}, u32[]{:S(2)}, u32[]{:S(2)}) %collective-permute-start.6) | collective-permute-done | bytes 294944 | tf_op jit(solution)/shard_map/ppermute | solution.py:29
  37.4 0.0 collective-permute-done.7.refs_1_
  37.4 1.6 %collective-permute-start.8 = (f32[64,1152]{1,0:T(8,128)S(1)}, f32[64,1152]{1,0:T(8,128)S(1)}, u32[]{:S(2)}, u32[]{:S(2)}) collective-permute-start(f32[64,1152]{1,0:T(8,128)S(1)} %collective-permute-done.6.refs_0_), channel_id=1, source_target_pairs={{0,1},{1,0},{2,3},{3,2},{4,5},{5,4},{6,7},{7,6},{8,9},{9,8},{10,11... | collective-permute-start | bytes 884744 | tf_op jit(solution)/shard_map/ppermute | solution.py:29
  39.0 1.9 %collective-permute-done.4.one = f32[128,1152]{1,0:T(8,128)S(1)} collective-permute-done((f32[128,1152]{1,0:T(8,128)S(1)}, f32[128,1152]{1,0:T(8,128)S(1)}, u32[]{:S(2)}, u32[]{:S(2)}) %collective-permute-start.4) | collective-permute-done | bytes 589856 | tf_op jit(solution)/shard_map/ppermute | solution.py:29
  40.9 0.0 collective-permute-done.5.two
  40.9 0.1 shard_map.63
  41.0 0.3 shard_map.67
  41.3 2.3 %shard_map.68 = (f32[256,512]{1,0:T(8,128)S(1)}, f32[128,1152]{1,0:T(8,128)S(1)}, f32[128,1152]{1,0:T(8,128)S(1)}) custom-call(f32[8,128]{1,0:T(8,128)S(1)} %shard_map.59.refs_0_.params, f32[128,1152]{1,0:T(8,128)S(1)} %get-tuple-element.133.refs_0_.refs_2_, f32[128,1152]{1,0:T(8,128)S(1)} %get-tuple-element.134.refs_1_.refs_3_, ...), custom_call_target="tpu_custom_call" | custom-call | flops 3000000000 | tf_op jit(solution)/shard_map/pallas_call | solution.py:253
  43.6 2.5 %collective-permute-start.12 = (f32[128,1152]{1,0:T(8,128)S(1)}, f32[128,1152]{1,0:T(8,128)S(1)}, u32[]{:S(2)}, u32[]{:S(2)}) collective-permute-start(f32[128,1152]{1,0:T(8,128)S(1)} %get-tuple-element.124), channel_id=1, source_target_pairs={{0,6},{1,7},{2,0},{3,1},{4,2},{5,3},{6,4},{7,5},{8,14},{9,15},{10,... | collective-permute-start | bytes 1769480 | tf_op jit(solution)/shard_map/ppermute | solution.py:29
  46.1 0.0 collective-permute-start.13
  46.1 1.0 %collective-permute-done.10.two_last = f32[128,1152]{1,0:T(8,128)S(1)} collective-permute-done((f32[128,1152]{1,0:T(8,128)S(1)}, f32[128,1152]{1,0:T(8,128)S(1)}, u32[]{:S(2)}, u32[]{:S(2)}) %collective-permute-start.10) | collective-permute-done | bytes 589856 | tf_op jit(solution)/shard_map/ppermute | solution.py:29
  47.1 0.1 shard_map.69.refs_0_.refs_4_
  47.2 1.5 %shard_map.70 = (f32[128,512]{1,0:T(8,128)S(1)}, f32[128,1152]{1,0:T(8,128)S(1)}) custom-call(f32[8,128]{1,0:T(8,128)S(1)} %shard_map.59.refs_0_.params, f32[128,1152]{1,0:T(8,128)S(1)} %shard_map.69.refs_0_.refs_4_, bf16[512,1152]{1,0:T(8,128)(2,1)S(1)} %get-tuple-element.127.refs_2_.refs_1_.refs_3_, ...), custom_call_target="tpu_custom_call" | custom-call | tf_op jit(solution)/shard_map/pallas_call | solution.py:253
  48.7 1.5 %collective-permute-start.11 = (f32[128,1152]{1,0:T(8,128)S(1)}, f32[128,1152]{1,0:T(8,128)S(1)}, u32[]{:S(2)}, u32[]{:S(2)}) collective-permute-start(f32[128,1152]{1,0:T(8,128)S(1)} %get-tuple-element.148.two), channel_id=1, source_target_pairs={{0,120},{1,249},{2,122},{3,251},{4,124},{5,253},{6,126},{7,255},{8... | collective-permute-start | bytes 1769480 | tf_op jit(solution)/shard_map/ppermute | solution.py:29
  50.2 1.4 %shard_map.71 = (f32[128,128]{1,0:T(8,128)S(1)}, f32[128,1152]{1,0:T(8,128)S(1)}, f32[128,128]{1,0:T(8,128)S(1)}, f32[128,1152]{1,0:T(8,128)S(1)}) custom-call(f32[8,128]{1,0:T(8,128)S(1)} %shard_map.59.refs_0_.params, f32[128,1152]{1,0:T(8,128)S(1)} %get-tuple-element.96.own.refs_1_.refs_0_.y, f32[128,1152]{1,0:T(8,128)S(1)} %collective-permute-done.1.last.refs_2_.refs_1_, ...), custom_call_target="tpu_custom_call" | custom-call | tf_op jit(solution)/shard_map/pallas_call | solution.py:253
  51.7 1.4 %shard_map.72 = (f32[48,1152]{1,0:T(8,128)S(1)}, f32[80,1152]{1,0:T(8,128)S(1)}, f32[48,1152]{1,0:T(8,128)S(1)}, f32[80,1152]{1,0:T(8,128)S(1)}) custom-call(f32[128,1152]{1,0:T(8,128)S(1)} %get-tuple-element.96.own.refs_1_.refs_0_.y, f32[128,1152]{1,0:T(8,128)S(1)} %collective-permute-done.1.last.refs_2_.refs_1_, ...), custom_call_target="tpu_custom_call" | custom-call | tf_op jit(solution)/shard_map/pallas_call | solution.py:253
  53.0 2.4 %collective-permute-start.14 = (f32[80,1152]{1,0:T(8,128)S(1)}, f32[80,1152]{1,0:T(8,128)S(1)}, u32[]{:S(2)}, u32[]{:S(2)}) collective-permute-start(f32[80,1152]{1,0:T(8,128)S(1)} %get-tuple-element.140), channel_id=1, source_target_pairs={{0,1},{1,0},{2,3},{3,2},{4,5},{5,4},{6,7},{7,6},{8,9},{9,8},{10,11... | collective-permute-start | bytes 1105928 | tf_op jit(solution)/shard_map/ppermute | solution.py:29
  55.4 0.1 collective-permute-start.17
  55.5 1.5 %collective-permute-done.17.beside = f32[48,1152]{1,0:T(8,128)S(1)} collective-permute-done((f32[48,1152]{1,0:T(8,128)S(1)}, f32[48,1152]{1,0:T(8,128)S(1)}, u32[]{:S(2)}, u32[]{:S(2)}) %collective-permute-start.17) | collective-permute-done | bytes 221216 | tf_op jit(solution)/shard_map/ppermute | solution.py:29
  57.1 0.1 collective-permute-start.18
  57.2 1.4 %shard_map.73 = (f32[48,1152]{1,0:T(8,128)S(1)}, f32[80,1152]{1,0:T(8,128)S(1)}, f32[48,1152]{1,0:T(8,128)S(1)}, f32[80,1152]{1,0:T(8,128)S(1)}) custom-call(f32[128,1152]{1,0:T(8,128)S(1)} %get-tuple-element.96.own.refs_1_.refs_0_.y, f32[128,1152]{1,0:T(8,128)S(1)} %collective-permute-done.1.last.refs_2_.refs_1_, ...), custom_call_target="tpu_custom_call" | custom-call | tf_op jit(solution)/shard_map/pallas_call | solution.py:253
  58.6 0.1 shard_map.74
  58.6 2.5 %collective-permute-done.13.back_3 = f32[128,1152]{1,0:T(8,128)S(1)} collective-permute-done((f32[128,1152]{1,0:T(8,128)S(1)}, f32[128,1152]{1,0:T(8,128)S(1)}, u32[]{:S(2)}, u32[]{:S(2)}) %collective-permute-start.13) | collective-permute-done | bytes 589856 | tf_op jit(solution)/shard_map/ppermute | solution.py:29
  61.1 0.1 shard_map.75
  61.3 2.9 %collective-permute-start.16 = (f32[128,1152]{1,0:T(8,128)S(1)}, f32[128,1152]{1,0:T(8,128)S(1)}, u32[]{:S(2)}, u32[]{:S(2)}) collective-permute-start(f32[128,1152]{1,0:T(8,128)S(1)} %shard_map.75), channel_id=1, source_target_pairs={{0,120},{1,249},{2,122},{3,251},{4,124},{5,253},{6,126},{7,255},{8... | collective-permute-start | bytes 1769480 | tf_op jit(solution)/shard_map/ppermute | solution.py:29
  64.1 0.0 collective-permute-done.11.two_last
  64.1 0.1 shard_map.76
  64.2 0.1 collective-permute-start.15
  64.3 1.3 %collective-permute-start.19 = (f32[80,1152]{1,0:T(8,128)S(1)}, f32[80,1152]{1,0:T(8,128)S(1)}, u32[]{:S(2)}, u32[]{:S(2)}) collective-permute-start(f32[80,1152]{1,0:T(8,128)S(1)} %shard_map.74), channel_id=1, source_target_pairs={{0,128},{1,129},{2,130},{3,131},{4,132},{5,133},{6,134},{7,135},{8... | collective-permute-start | bytes 1105928 | tf_op jit(solution)/shard_map/ppermute | solution.py:29
  65.7 2.4 %collective-permute-start.21 = (f32[80,1152]{1,0:T(8,128)S(1)}, f32[80,1152]{1,0:T(8,128)S(1)}, u32[]{:S(2)}, u32[]{:S(2)}) collective-permute-start(f32[80,1152]{1,0:T(8,128)S(1)} %get-tuple-element.161), channel_id=1, source_target_pairs={{0,1},{1,0},{2,3},{3,2},{4,5},{5,4},{6,7},{7,6},{8,9},{9,8},{10,11... | collective-permute-start | bytes 1105928 | tf_op jit(solution)/shard_map/ppermute | solution.py:29
  68.1 0.2 collective-permute-done.18.three
  68.3 1.5 %collective-permute-start.20 = (f32[48,1152]{1,0:T(8,128)S(1)}, f32[48,1152]{1,0:T(8,128)S(1)}, u32[]{:S(2)}, u32[]{:S(2)}) collective-permute-start(f32[48,1152]{1,0:T(8,128)S(1)} %get-tuple-element.157), channel_id=1, source_target_pairs={{0,1},{1,0},{2,3},{3,2},{4,5},{5,4},{6,7},{7,6},{8,9},{9,8},{10,11... | collective-permute-start | bytes 663560 | tf_op jit(solution)/shard_map/ppermute | solution.py:29
  69.8 0.2 shard_map.78.here
  70.0 0.9 %collective-permute-done.20.two = f32[48,1152]{1,0:T(8,128)S(1)} collective-permute-done((f32[48,1152]{1,0:T(8,128)S(1)}, f32[48,1152]{1,0:T(8,128)S(1)}, u32[]{:S(2)}, u32[]{:S(2)}) %collective-permute-start.20) | collective-permute-done | bytes 221216 | tf_op jit(solution)/shard_map/ppermute | solution.py:29
  70.9 10.0 %collective-permute-done.19.three = f32[80,1152]{1,0:T(8,128)S(1)} collective-permute-done((f32[80,1152]{1,0:T(8,128)S(1)}, f32[80,1152]{1,0:T(8,128)S(1)}, u32[]{:S(2)}, u32[]{:S(2)}) %collective-permute-start.19) | collective-permute-done | bytes 368672 | tf_op jit(solution)/shard_map/ppermute | solution.py:29
  80.9 0.0 collective-permute-done.21.two
  80.9 0.1 shard_map.80.refs_6_
  81.0 0.0 collective-permute-done.16.beside
  81.0 0.1 shard_map.81.refs_0_
  81.1 0.0 collective-permute-done.15.refs_1_
  81.1 1.4 %shard_map.82 = (f32[128,1152]{1,0:T(8,128)}, f32[128,1152]{1,0:T(8,128)}) custom-call(f32[8,128]{1,0:T(8,128)S(1)} %shard_map.59.refs_0_.params, f32[128,1152]{1,0:T(8,128)S(1)} %get-tuple-element.96.own.refs_1_.refs_0_.y, f32[128,1]{1,0:T(8,128)S(1)} %get-tuple-element.88._.y_inv, f32[128,1152]{1,0:T(8,128)S(1)} %shard_map.81.refs_0_, ...), custom_call_target="tpu_custom_call" | custom-call | tf_op jit(solution)/shard_map/pallas_call | solution.py:266
  (8 shorter events, 0.1 us)
Async XLA Ops:
  0.6 1.1 %copy-start.1 = (f32[128,1152]{1,0:T(8,128)S(1)}, f32[128,1152]{1,0:T(8,128)}, u32[]{:S(2)}) copy-start(f32[128,1152]{1,0:T(8,128)} %in_ref.2) | copy-start | bytes 1769476
  1.8 22.3 %collective-permute-start.1 = (f32[128,1152]{1,0:T(8,128)S(1)}, f32[128,1152]{1,0:T(8,128)S(1)}, u32[]{:S(2)}, u32[]{:S(2)}) collective-permute-start(f32[128,1152]{1,0:T(8,128)S(1)} %get-tuple-element.96.own.refs_1_.refs_0_.y), channel_id=1, source_target_pairs={{0,8},{1,137},{2,10},{3,139},{4,12},{5,141},{6,14},{7,143},{8,16},... | collective-permute-start | bytes 1769480 | tf_op jit(solution)/shard_map/ppermute | solution.py:29
  5.5 1.1 %copy-start = (f32[128,1152]{1,0:T(8,128)S(1)}, f32[128,1152]{1,0:T(8,128)}, u32[]{:S(2)}) copy-start(f32[128,1152]{1,0:T(8,128)} %in_ref.3) | copy-start | bytes 1769476
  6.7 5.1 %collective-permute-start.2 = (f32[64,1152]{1,0:T(8,128)S(1)}, f32[64,1152]{1,0:T(8,128)S(1)}, u32[]{:S(2)}, u32[]{:S(2)}) collective-permute-start(f32[64,1152]{1,0:T(8,128)S(1)} %get-tuple-element.100.refs_0_), channel_id=1, source_target_pairs={{0,1},{1,0},{2,3},{3,2},{4,5},{5,4},{6,7},{7,6},{8,9},{9,8},{10,11... | collective-permute-start | bytes 884744 | tf_op jit(solution)/shard_map/ppermute | solution.py:29
  6.8 5.0 %collective-permute-start.3 = (f32[64,1152]{1,0:T(8,128)S(1)}, f32[64,1152]{1,0:T(8,128)S(1)}, u32[]{:S(2)}, u32[]{:S(2)}) collective-permute-start(f32[64,1152]{1,0:T(8,128)S(1)} %get-tuple-element.104.refs_1_), channel_id=1, source_target_pairs={{0,1},{1,0},{2,3},{3,2},{4,5},{5,4},{6,7},{7,6},{8,9},{9,8},{10,11... | collective-permute-start | bytes 884744 | tf_op jit(solution)/shard_map/ppermute | solution.py:29
  7.3 19.7 %collective-permute-start = (f32[64,1152]{1,0:T(8,128)S(1)}, f32[64,1152]{1,0:T(8,128)S(1)}, u32[]{:S(2)}, u32[]{:S(2)}) collective-permute-start(f32[64,1152]{1,0:T(8,128)S(1)} %get-tuple-element.100.refs_0_), channel_id=1, source_target_pairs={{0,128},{1,129},{2,130},{3,131},{4,132},{5,133},{6,134},{7,135},{8... | collective-permute-start | bytes 884744 | tf_op jit(solution)/shard_map/ppermute | solution.py:29
  9.0 21.1 %collective-permute-start.9 = (f32[128,1152]{1,0:T(8,128)S(1)}, f32[128,1152]{1,0:T(8,128)S(1)}, u32[]{:S(2)}, u32[]{:S(2)}) collective-permute-start(f32[128,1152]{1,0:T(8,128)S(1)} %get-tuple-element.96.own.refs_1_.refs_0_.y), channel_id=1, source_target_pairs={{0,4},{1,5},{2,6},{3,7},{4,0},{5,1},{6,2},{7,3},{8,12},{9,13},{10,... | collective-permute-start | bytes 1769480 | tf_op jit(solution)/shard_map/ppermute | solution.py:29
  24.3 16.6 %collective-permute-start.4 = (f32[128,1152]{1,0:T(8,128)S(1)}, f32[128,1152]{1,0:T(8,128)S(1)}, u32[]{:S(2)}, u32[]{:S(2)}) collective-permute-start(f32[128,1152]{1,0:T(8,128)S(1)} %get-tuple-element.95), channel_id=1, source_target_pairs={{0,2},{1,3},{2,4},{3,5},{4,6},{5,7},{6,0},{7,1},{8,10},{9,11},{10,... | collective-permute-start | bytes 1769480 | tf_op jit(solution)/shard_map/ppermute | solution.py:29
  25.6 15.3 %collective-permute-start.5 = (f32[128,1152]{1,0:T(8,128)S(1)}, f32[128,1152]{1,0:T(8,128)S(1)}, u32[]{:S(2)}, u32[]{:S(2)}) collective-permute-start(f32[128,1152]{1,0:T(8,128)S(1)} %get-tuple-element.97), channel_id=1, source_target_pairs={{0,6},{1,7},{2,0},{3,1},{4,2},{5,3},{6,4},{7,5},{8,14},{9,15},{10,... | collective-permute-start | bytes 1769480 | tf_op jit(solution)/shard_map/ppermute | solution.py:29
  27.1 10.3 %collective-permute-start.6 = (f32[64,1152]{1,0:T(8,128)S(1)}, f32[64,1152]{1,0:T(8,128)S(1)}, u32[]{:S(2)}, u32[]{:S(2)}) collective-permute-start(f32[64,1152]{1,0:T(8,128)S(1)} %get-tuple-element.104.refs_1_), channel_id=1, source_target_pairs={{0,128},{1,129},{2,130},{3,131},{4,132},{5,133},{6,134},{7,135},{8... | collective-permute-start | bytes 884744 | tf_op jit(solution)/shard_map/ppermute | solution.py:29
  27.8 9.6 %collective-permute-start.7 = (f32[64,1152]{1,0:T(8,128)S(1)}, f32[64,1152]{1,0:T(8,128)S(1)}, u32[]{:S(2)}, u32[]{:S(2)}) collective-permute-start(f32[64,1152]{1,0:T(8,128)S(1)} %collective-permute-done.refs_0_), channel_id=1, source_target_pairs={{0,1},{1,0},{2,3},{3,2},{4,5},{5,4},{6,7},{7,6},{8,9},{9,8},{10,11... | collective-permute-start | bytes 884744 | tf_op jit(solution)/shard_map/ppermute | solution.py:29
  30.1 17.0 %collective-permute-start.10 = (f32[128,1152]{1,0:T(8,128)S(1)}, f32[128,1152]{1,0:T(8,128)S(1)}, u32[]{:S(2)}, u32[]{:S(2)}) collective-permute-start(f32[128,1152]{1,0:T(8,128)S(1)} %collective-permute-done.9.two), channel_id=1, source_target_pairs={{0,8},{1,137},{2,10},{3,139},{4,12},{5,141},{6,14},{7,143},{8,16},... | collective-permute-start | bytes 1769480 | tf_op jit(solution)/shard_map/ppermute | solution.py:29
  37.4 3.6 %collective-permute-start.8 = (f32[64,1152]{1,0:T(8,128)S(1)}, f32[64,1152]{1,0:T(8,128)S(1)}, u32[]{:S(2)}, u32[]{:S(2)}) collective-permute-start(f32[64,1152]{1,0:T(8,128)S(1)} %collective-permute-done.6.refs_0_), channel_id=1, source_target_pairs={{0,1},{1,0},{2,3},{3,2},{4,5},{5,4},{6,7},{7,6},{8,9},{9,8},{10,11... | collective-permute-start | bytes 884744 | tf_op jit(solution)/shard_map/ppermute | solution.py:29
  43.6 15.0 %collective-permute-start.12 = (f32[128,1152]{1,0:T(8,128)S(1)}, f32[128,1152]{1,0:T(8,128)S(1)}, u32[]{:S(2)}, u32[]{:S(2)}) collective-permute-start(f32[128,1152]{1,0:T(8,128)S(1)} %get-tuple-element.124), channel_id=1, source_target_pairs={{0,6},{1,7},{2,0},{3,1},{4,2},{5,3},{6,4},{7,5},{8,14},{9,15},{10,... | collective-permute-start | bytes 1769480 | tf_op jit(solution)/shard_map/ppermute | solution.py:29
  46.1 15.1 %collective-permute-start.13 = (f32[128,1152]{1,0:T(8,128)S(1)}, f32[128,1152]{1,0:T(8,128)S(1)}, u32[]{:S(2)}, u32[]{:S(2)}) collective-permute-start(f32[128,1152]{1,0:T(8,128)S(1)} %get-tuple-element.125), channel_id=1, source_target_pairs={{0,2},{1,3},{2,4},{3,5},{4,6},{5,7},{6,0},{7,1},{8,10},{9,11},{10,... | collective-permute-start | bytes 1769480 | tf_op jit(solution)/shard_map/ppermute | solution.py:29
  48.7 15.4 %collective-permute-start.11 = (f32[128,1152]{1,0:T(8,128)S(1)}, f32[128,1152]{1,0:T(8,128)S(1)}, u32[]{:S(2)}, u32[]{:S(2)}) collective-permute-start(f32[128,1152]{1,0:T(8,128)S(1)} %get-tuple-element.148.two), channel_id=1, source_target_pairs={{0,120},{1,249},{2,122},{3,251},{4,124},{5,253},{6,126},{7,255},{8... | collective-permute-start | bytes 1769480 | tf_op jit(solution)/shard_map/ppermute | solution.py:29
  53.0 5.5 %collective-permute-start.14 = (f32[80,1152]{1,0:T(8,128)S(1)}, f32[80,1152]{1,0:T(8,128)S(1)}, u32[]{:S(2)}, u32[]{:S(2)}) collective-permute-start(f32[80,1152]{1,0:T(8,128)S(1)} %get-tuple-element.140), channel_id=1, source_target_pairs={{0,1},{1,0},{2,3},{3,2},{4,5},{5,4},{6,7},{7,6},{8,9},{9,8},{10,11... | collective-permute-start | bytes 1105928 | tf_op jit(solution)/shard_map/ppermute | solution.py:29
  55.4 1.6 %collective-permute-start.17 = (f32[48,1152]{1,0:T(8,128)S(1)}, f32[48,1152]{1,0:T(8,128)S(1)}, u32[]{:S(2)}, u32[]{:S(2)}) collective-permute-start(f32[48,1152]{1,0:T(8,128)S(1)} %get-tuple-element.151), channel_id=1, source_target_pairs={{0,1},{1,0},{2,3},{3,2},{4,5},{5,4},{6,7},{7,6},{8,9},{9,8},{10,11... | collective-permute-start | bytes 663560 | tf_op jit(solution)/shard_map/ppermute | solution.py:29
  57.1 11.2 %collective-permute-start.18 = (f32[48,1152]{1,0:T(8,128)S(1)}, f32[48,1152]{1,0:T(8,128)S(1)}, u32[]{:S(2)}, u32[]{:S(2)}) collective-permute-start(f32[48,1152]{1,0:T(8,128)S(1)} %shard_map.77), channel_id=1, source_target_pairs={{0,128},{1,129},{2,130},{3,131},{4,132},{5,133},{6,134},{7,135},{8... | collective-permute-start | bytes 663560 | tf_op jit(solution)/shard_map/ppermute | solution.py:29
  61.3 19.7 %collective-permute-start.16 = (f32[128,1152]{1,0:T(8,128)S(1)}, f32[128,1152]{1,0:T(8,128)S(1)}, u32[]{:S(2)}, u32[]{:S(2)}) collective-permute-start(f32[128,1152]{1,0:T(8,128)S(1)} %shard_map.75), channel_id=1, source_target_pairs={{0,120},{1,249},{2,122},{3,251},{4,124},{5,253},{6,126},{7,255},{8... | collective-permute-start | bytes 1769480 | tf_op jit(solution)/shard_map/ppermute | solution.py:29
  64.2 16.9 %collective-permute-start.15 = (f32[128,1152]{1,0:T(8,128)S(1)}, f32[128,1152]{1,0:T(8,128)S(1)}, u32[]{:S(2)}, u32[]{:S(2)}) collective-permute-start(f32[128,1152]{1,0:T(8,128)S(1)} %shard_map.76), channel_id=1, source_target_pairs={{0,4},{1,5},{2,6},{3,7},{4,0},{5,1},{6,2},{7,3},{8,12},{9,13},{10,... | collective-permute-start | bytes 1769480 | tf_op jit(solution)/shard_map/ppermute | solution.py:29
  64.3 16.6 %collective-permute-start.19 = (f32[80,1152]{1,0:T(8,128)S(1)}, f32[80,1152]{1,0:T(8,128)S(1)}, u32[]{:S(2)}, u32[]{:S(2)}) collective-permute-start(f32[80,1152]{1,0:T(8,128)S(1)} %shard_map.74), channel_id=1, source_target_pairs={{0,128},{1,129},{2,130},{3,131},{4,132},{5,133},{6,134},{7,135},{8... | collective-permute-start | bytes 1105928 | tf_op jit(solution)/shard_map/ppermute | solution.py:29
  65.7 15.3 %collective-permute-start.21 = (f32[80,1152]{1,0:T(8,128)S(1)}, f32[80,1152]{1,0:T(8,128)S(1)}, u32[]{:S(2)}, u32[]{:S(2)}) collective-permute-start(f32[80,1152]{1,0:T(8,128)S(1)} %get-tuple-element.161), channel_id=1, source_target_pairs={{0,1},{1,0},{2,3},{3,2},{4,5},{5,4},{6,7},{7,6},{8,9},{9,8},{10,11... | collective-permute-start | bytes 1105928 | tf_op jit(solution)/shard_map/ppermute | solution.py:29
  68.3 2.6 %collective-permute-start.20 = (f32[48,1152]{1,0:T(8,128)S(1)}, f32[48,1152]{1,0:T(8,128)S(1)}, u32[]{:S(2)}, u32[]{:S(2)}) collective-permute-start(f32[48,1152]{1,0:T(8,128)S(1)} %get-tuple-element.157), channel_id=1, source_target_pairs={{0,1},{1,0},{2,3},{3,2},{4,5},{5,4},{6,7},{7,6},{8,9},{9,8},{10,11... | collective-permute-start | bytes 663560 | tf_op jit(solution)/shard_map/ppermute | solution.py:29
